TPU v7x, 128 devices: a whole 4x4x4 slice. The times are simulated.
128 devices in a mesh: tx: 8 (over y, core), brick: 16 (over x, z).
Axes of the slice: x: 4, y: 4, z: 4, core: 2. Of those that a mesh axis runs over, the one named last changes fastest.
Arguments:
- fields: float32 [8, 2, 2, 3, 128, 64, 128], P('tx', None, None, None, 'brick'), may hold values from -6 to 6
- sources: float32 [8, 2, 2, 3, 128, 64, 128], P('tx', None, None, None, 'brick'), may hold values from -6 to 6
- conductivity: float32 [8, 128, 64, 128], P('tx', 'brick'), may hold values from 0.1 to 1.5
- omegas: float32 [2], replicated, may hold values from 0.4 to 2
- tx_bricks: int32 [8], replicated, may hold values from 6 to 16, as said below
- owner_map: int32 [128], replicated, may hold values from 0 to 127, each once
- row_brick: int32 [8, 8192, 1], P('tx', 'brick'), may hold values from 0 to 127; in each aligned block of 512 rows (0 to 511, 512 to 1023, ..., all dimensions but the last counted through in order) at most 8 rows name the same one
- row_offset: int32 [8, 8192], P('tx', 'brick'), may hold values from 0 to 31
Outputs:
- grid_gradient: float32 [4096, 128], P(('tx', 'brick'))
Inputs may be any that keep to these rules, and one draw needn't show every extreme that they name: `tx_bricks`: every transmitter occupies between a third and all of its group; some transmitter occupies all 16 and some the fewest. `row_brick`: within the rows of one device no brick is named more than 8 times, a bound that some block reaches.
All inputs are finite; a program needn't handle non-finite values.
Results may differ from a plain program's by a relative error of at most 0.0001.
Values sent between devices are 32-bit elements; how exact they have to be, the bound alone decides.
No kernel may reach another device: no remote copies, remote signals or barrier semaphores. Data moves between devices by JAX's collectives and lax.ppermute only.
A program may use at most 64 MiB of HBM per device.

v0:
```python
import jax
import jax.numpy as jnp
from jax import lax
from jax.sharding import PartitionSpec as P

G_DEV = 32


def with_halo(block, sides, width):
    for axis, dim in sides:
        count = lax.axis_size(axis)
        forward = [(i, i + 1) for i in range(count - 1)]
        backward = [(target, source) for source, target in forward]
        low = lax.ppermute(
            lax.slice_in_dim(block, block.shape[dim] - width, None, axis=dim), axis, forward
        )
        high = lax.ppermute(lax.slice_in_dim(block, 0, width, axis=dim), axis, backward)
        block = jnp.concatenate([low, block, high], axis=dim)
    return block


def shift_next(values, axis):
    count = values.shape[axis]
    return jnp.concatenate(
        [
            lax.slice_in_dim(values, 1, count, axis=axis),
            jnp.zeros_like(lax.slice_in_dim(values, 0, 1, axis=axis)),
        ],
        axis=axis,
    )


def shift_prev(values, axis):
    count = values.shape[axis]
    return jnp.concatenate(
        [
            jnp.zeros_like(lax.slice_in_dim(values, 0, 1, axis=axis)),
            lax.slice_in_dim(values, 0, count - 1, axis=axis),
        ],
        axis=axis,
    )


def diff_forward(values, axis):
    return shift_next(values, axis) - values


def diff_backward(values, axis):
    return values - shift_prev(values, axis)


def curl_with(field, differ):
    comp_x = field[..., 0, :, :, :]
    comp_y = field[..., 1, :, :, :]
    comp_z = field[..., 2, :, :, :]
    rank = comp_x.ndim
    ax_x, ax_y, ax_z = (rank - 3, rank - 2, rank - 1)
    out_x = differ(comp_z, ax_y) - differ(comp_y, ax_z)
    out_y = differ(comp_x, ax_z) - differ(comp_z, ax_x)
    out_z = differ(comp_y, ax_x) - differ(comp_x, ax_y)
    return jnp.stack([out_x, out_y, out_z], axis=rank - 3)


def apply_crop(extended, conduct, omegas, lowest_plane):
    first_curl = curl_with(extended, diff_forward)
    plane_count = extended.shape[3]
    kept_planes = (jnp.arange(plane_count) + lowest_plane >= 0).astype(jnp.float32)[:, None, None]
    curled = curl_with(first_curl * kept_planes, diff_backward)[:, :, :, 1:-1]
    inner = extended[:, :, :, 1:-1]
    rotated = jnp.stack([-inner[:, 1], inner[:, 0]], axis=1)
    return curled + omegas[:, None, None, None, None, None] * conduct * rotated


def per_device(fields, sources, conductivity, omegas, tx_bricks, owner_map, row_brick, row_offset):
    freqs, planes, width_y, width_z = (
        fields.shape[1],
        fields.shape[4],
        fields.shape[5],
        fields.shape[6],
    )
    brick_index = lax.axis_index("brick")
    base_plane = brick_index * planes
    span = jnp.sum(jnp.where(jnp.arange(tx_bricks.shape[0]) == lax.axis_index("tx"), tx_bricks, 0))
    active = (brick_index < span).astype(jnp.float32)
    efield = fields[0] * active
    flat_field = efield.reshape(freqs * 6, planes, width_y, width_z)
    extended = with_halo(flat_field, (("brick", 1),), 1)
    applied = apply_crop(
        extended.reshape(freqs, 2, 3, planes + 2, width_y, width_z),
        conductivity[0],
        omegas,
        base_plane - 1,
    )
    residual = (applied - sources[0]) * active
    extended_res = with_halo(
        residual.reshape(freqs * 6, planes, width_y, width_z), (("brick", 1),), 1
    )
    adjoint = (
        apply_crop(
            extended_res.reshape(freqs, 2, 3, planes + 2, width_y, width_z),
            conductivity[0],
            omegas,
            base_plane - 1,
        )
        * active
    )
    terms = efield[:, 0] * adjoint[:, 1] - efield[:, 1] * adjoint[:, 0]
    local = 0.003 * jnp.sum(omegas[:, None, None, None, None] * terms, axis=(0, 1))
    local_rows = local.reshape(planes * width_y, width_z)
    dev_count = lax.axis_size("tx") * lax.axis_size("brick")
    hit_brick = row_brick[0, :, 0][:, None] == jnp.arange(dev_count)[None, :]
    dest_dev = jnp.sum(jnp.where(hit_brick, owner_map[None, :], 0), axis=1)
    offsets = row_offset[0]
    buffer = (
        jnp.zeros((dev_count * G_DEV, width_z), jnp.float32)
        .at[dest_dev * G_DEV + offsets]
        .add(local_rows)
    )
    return lax.psum_scatter(buffer, ("tx", "brick"), scatter_dimension=0, tiled=True)


def solution(mesh):
    return jax.shard_map(
        per_device,
        mesh=mesh,
        in_specs=(
            P("tx", None, None, None, "brick", None, None),
            P("tx", None, None, None, "brick", None, None),
            P("tx", "brick", None, None),
            P(),
            P(),
            P(),
            P("tx", "brick", None),
            P("tx", "brick"),
        ),
        out_specs=P(("tx", "brick"), None),
        check_vma=False,
    )
```

profile of v0, /device:TPU:0, one launch (start us, length us, event | category | flops | bytes accessed | tf_op | source)
XLA Modules:
  0.0 718.0 jit_solution(14431355999872983797)
XLA Ops:
  6.5 1.3 fusion.10
  8.5 2.3 broadcast_multiply_fusion
  10.8 1.0 fusion.12
  11.8 4.7 collective-permute-start
  16.5 1.3 collective-permute-start.1
  17.8 1.9 fusion.13
  19.7 4.0 fusion.11
  23.7 0.2 select_reduce_fusion
  24.0 1.1 broadcast_multiply_fusion.1
  25.0 1.6 copy_negate_fusion
  26.6 1.0 copy_dynamic-update-slice_fusion.4
  27.6 0.3 constant_dynamic-update-slice_fusion
  28.0 1.2 collective-permute-done.1
  29.2 0.4 slice_bitcast_fusion.11
  29.5 0.4 slice.212
  29.9 0.1 slice.215
  30.1 0.1 slice.208
  30.3 0.4 slice.210
  30.8 1.7 subtract_bitcast_fusion.11
  32.5 0.8 maximum_multiply_fusion
  33.4 0.5 slice_bitcast_fusion.8
  33.9 0.1 slice.222
  34.0 0.1 slice.223
  34.2 1.8 subtract_bitcast_fusion.8
  36.0 0.5 copy-done.3
  36.5 1.1 copy_multiply_fusion
  37.7 3.4 collective-permute-start.2
  41.2 1.5 collective-permute-start.3
  42.6 0.3 slice_negate_fusion
  42.9 6.0 collective-permute-done.2
  48.9 1.4 copy_dynamic-update-slice_fusion
  50.3 2.8 collective-permute-done.3
  53.1 0.5 slice_bitcast_fusion.5
  53.6 0.4 slice.233
  54.1 0.2 slice.236
  54.2 0.2 slice.229
  54.5 0.4 slice.231
  55.0 1.7 subtract_bitcast_fusion.5
  56.7 0.8 maximum_multiply_fusion.1
  57.6 0.5 slice_bitcast_fusion.2
  58.1 0.1 slice.243
  58.2 0.1 slice.244
  58.4 1.8 subtract_bitcast_fusion.2
  60.2 1.1 fusion.1
  61.3 0.7 copy-done.2
  62.1 0.8 fusion.7
  62.9 3.7 scatter_custom_fusion
  66.6 644.5 %reduce-scatter.2.cloned.1.call-done = f32[32,128]{1,0:T(8,128)} async-done(((f32[4096,128]{1,0:T(8,128)}), f32[32,128]{1,0:T(8,128)}) %reduce-scatter.2.cloned.1.call-update) | async-done | bytes 16400 | tf_op jit(solution)/shard_map/reduce_scatter | solution.py:119
  (29 shorter events, 0.7 us)
Async XLA Ops:
  6.5 704.6 %reduce-scatter.2.cloned.1.call-start = ((), (), s32[]{:S(2)}) async-start(), calls=%async_computation.1 | async-start | bytes 2113536 | tf_op jit(solution)/shard_map/reduce_scatter | solution.py:119
  8.5 9.3 %copy-start = (f32[1,2,2,3,8,64,128]{6,5,4,3,2,1,0:T(8,128)S(1)}, f32[1,2,2,3,8,64,128]{6,5,4,3,2,1,0:T(8,128)}, u32[]{:S(2)}) copy-start(f32[1,2,2,3,8,64,128]{6,5,4,3,2,1,0:T(8,128)} %param.8) | copy-start | bytes 9437188
  11.8 14.8 %collective-permute-start = (f32[12,1,64,128]{3,2,1,0:T(8,128)}, f32[12,1,64,128]{3,2,1,0:T(8,128)}, u32[]{:S(2)}, u32[]{:S(2)}) collective-permute-start(f32[12,1,64,128]{3,2,1,0:T(8,128)} %get-tuple-element.36), channel_id=1, source_target_pairs={{0,1},{1,2},{2,3},{3,4},{4,5},{5,6},{6,7},{7,8},{8,9},{9,10},{10,1... | collective-permute-start | bytes 1179656 | tf_op jit(solution)/shard_map/ppermute | solution.py:14
  16.5 12.7 %collective-permute-start.1 = (f32[12,1,64,128]{3,2,1,0:T(8,128)}, f32[12,1,64,128]{3,2,1,0:T(8,128)S(1)}, u32[]{:S(2)}, u32[]{:S(2)}) collective-permute-start(f32[12,1,64,128]{3,2,1,0:T(8,128)} %get-tuple-element.35), channel_id=1, source_target_pairs={{1,0},{2,1},{3,2},{4,3},{5,4},{6,5},{7,6},{8,7},{9,8},{10,9},{11,1... | collective-permute-start | bytes 1179656 | tf_op jit(solution)/shard_map/ppermute | solution.py:17
  19.7 4.0 copy-start.5
  19.7 4.0 copy-start.7
  19.7 4.3 copy-start.6
  34.2 1.9 copy-start.1
  34.2 2.4 copy-start.3
  37.6 3.5 copy-start.4
  37.7 11.2 %collective-permute-start.2 = (f32[12,1,64,128]{3,2,0,1:T(8,128)S(1)}, f32[12,1,64,128]{3,2,0,1:T(8,128)S(1)}, u32[]{:S(2)}, u32[]{:S(2)}) collective-permute-start(f32[12,1,64,128]{3,2,0,1:T(8,128)S(1)} %get-tuple-element.32), channel_id=1, source_target_pairs={{0,1},{1,2},{2,3},{3,4},{4,5},{5,6},{6,7},{7,8},{8,9},{9,10},{10,1... | collective-permute-start | bytes 1179656 | tf_op jit(solution)/shard_map/ppermute | solution.py:14
  41.2 11.9 %collective-permute-start.3 = (f32[12,1,64,128]{3,2,0,1:T(8,128)S(1)}, f32[12,1,64,128]{3,2,0,1:T(8,128)S(1)}, u32[]{:S(2)}, u32[]{:S(2)}) collective-permute-start(f32[12,1,64,128]{3,2,0,1:T(8,128)S(1)} %get-tuple-element.31), channel_id=1, source_target_pairs={{1,0},{2,1},{3,2},{4,3},{5,4},{6,5},{7,6},{8,7},{9,8},{10,9},{11,1... | collective-permute-start | bytes 1179656 | tf_op jit(solution)/shard_map/ppermute | solution.py:17
  60.2 1.9 copy-start.2
Sparse Core Ops, SparseCore 0:
  66.7 644.3 reduce-scatter.1
where the time goes:
time: 718 us
  waiting for transfers between devices  654 us (91%)
  other arithmetic  25.8 us (4%)
  between operations  14.5 us (2%)
  local copies, waits for them, and re-layouts  12.5 us (2%)
  starting transfers between devices  10.8 us (2%)
    reduce_scatter x1, waiting for transfers between devices, per_device(): lax.psum_scatter(buffer, ('tx', 'brick'), scatter_dimension=0, tiled=True)  644 us
  transfers between devices with their start and end apart: 5, of which 4 were waited for; matrix products, arithmetic and copies ran while one was open for 2% of the time, Pallas kernels for 0%

commit v1 on v0

v1 whole, which is shorter than its diff:
```python
import jax
import jax.numpy as jnp
from jax import lax
from jax.experimental import pallas as pl
from jax.experimental.pallas import tpu as pltpu
from jax.sharding import PartitionSpec as P

PL, NY, NZ, NF = 8, 64, 128, 2
ROWS = PL * NY
G_DEV = 32
CAP = 8
DEV = 128
SLOTS = CAP + 1
TX, BRICK = 8, 16
F32, BF16, I32 = jnp.float32, jnp.bfloat16, jnp.int32
SCALE = 0.003


def next_y(v):
    rows = lax.broadcasted_iota(I32, v.shape, 0)
    return jnp.where(rows == NY - 1, 0.0, pltpu.roll(v, NY - 1, 0))


def prev_y(v):
    rows = lax.broadcasted_iota(I32, v.shape, 0)
    return jnp.where(rows == 0, 0.0, pltpu.roll(v, 1, 0))


def next_z(v):
    lanes = lax.broadcasted_iota(I32, v.shape, 1)
    return jnp.where(lanes == NZ - 1, 0.0, pltpu.roll(v, NZ - 1, 1))


def prev_z(v):
    lanes = lax.broadcasted_iota(I32, v.shape, 1)
    return jnp.where(lanes == 0, 0.0, pltpu.roll(v, 1, 1))


def fy(v):
    return next_y(v) - v


def by(v):
    return v - prev_y(v)


def fz(v):
    return next_z(v) - v


def bz(v):
    return v - prev_z(v)


def q_of(vx, vy, vz):
    return fz(vx) + vz, vy + fy(vx)


def rotate_add(part, weight, other):
    return -(weight * other) if part == 0 else weight * other


def payload_kernel(om_ref, elo_ref, ehi_ref, slo_ref, shi_ref, clo_ref, chi_ref, up_ref, dn_ref):
    for f in range(NF):
        om = om_ref[f]
        for part in range(2):
            ch = 2 * f + part
            vx, vy, vz = (elo_ref[0, f, part, c, 0] for c in range(3))
            hx = fy(vz) - fz(vy)
            hy = fz(vx) - (elo_ref[0, f, part, 2, 1] - vz)
            hz = (elo_ref[0, f, part, 1, 1] - vy) - fy(vx)
            w = om * clo_ref[0, 0]
            ry = bz(hx) - hz + rotate_add(part, w, elo_ref[0, f, 1 - part, 1, 0]) - slo_ref[0, f, part, 1, 0]
            rz = hy - by(hx) + rotate_add(part, w, elo_ref[0, f, 1 - part, 2, 0]) - slo_ref[0, f, part, 2, 0]
            dn_ref[2 * ch] = vy
            dn_ref[2 * ch + 1] = vz
            dn_ref[8 + 2 * ch] = ry
            dn_ref[8 + 2 * ch + 1] = rz
            ux, uy, uz = (ehi_ref[0, f, part, c, 0] for c in range(3))
            vx, vy, vz = (ehi_ref[0, f, part, c, 1] for c in range(3))
            qy, qz = q_of(vx, vy, vz)
            hx = fy(vz) - fz(vy)
            hy = qy
            hz = -qz
            gy = fz(ux) - (vz - uz)
            gz = (vy - uy) - fy(ux)
            w = om * chi_ref[0, 0]
            o = [ehi_ref[0, f, 1 - part, c, 1] for c in range(3)]
            rx = by(hz) - bz(hy) + rotate_add(part, w, o[0]) - shi_ref[0, f, part, 0, 0]
            ry = bz(hx) - (hz - gz) + rotate_add(part, w, o[1]) - shi_ref[0, f, part, 1, 0]
            rz = (hy - gy) - by(hx) + rotate_add(part, w, o[2]) - shi_ref[0, f, part, 2, 0]
            sy, sz = q_of(rx, ry, rz)
            up_ref[2 * ch] = qy
            up_ref[2 * ch + 1] = qz
            up_ref[8 + 2 * ch] = sy
            up_ref[8 + 2 * ch + 1] = sz


def one_hot(cond):
    return jnp.where(cond, 1.0, 0.0).astype(BF16)


def split3(v):
    hi = v.astype(BF16)
    rest = v - hi.astype(F32)
    mid = rest.astype(BF16)
    low = (rest - mid.astype(F32)).astype(BF16)
    return hi, mid, low


def dot(a, b):
    return jnp.dot(a, b, preferred_element_type=F32)


def exact_dot(hot, v):
    hi, mid, low = split3(v)
    return dot(hot, hi) + (dot(hot, mid) + dot(hot, low))


def active_of(tb_ref):
    brick = lax.axis_index("brick")
    span = tb_ref[lax.axis_index("tx")]
    return brick, span


def main_kernel(om_ref, tb_ref, e_ref, s_ref, c_ref, rb_ref, ro_ref, own_ref, out_ref, slot_ref, r_ref, h_ref, loc_ref):
    brick, span = active_of(tb_ref)
    live = jnp.where(brick < span, 1.0, 0.0).astype(F32)
    zero = jnp.zeros((NY, NZ), F32)
    for i in range(12):
        r_ref[i, PL] = zero
    for i in range(8):
        h_ref[i] = zero

    def first(p, carry):
        q = jnp.minimum(p + 1, PL - 1)
        inside = jnp.where(p < PL - 1, 1.0, 0.0).astype(F32)
        sig = c_ref[0, p]
        for f in range(NF):
            w = om_ref[f] * sig
            for part in range(2):
                ch = 2 * f + part
                vx, vy, vz = (e_ref[0, f, part, c, p] for c in range(3))
                ny = e_ref[0, f, part, 1, q] * inside
                nz = e_ref[0, f, part, 2, q] * inside
                hx = fy(vz) - fz(vy)
                hy = fz(vx) - (nz - vz)
                hz = (ny - vy) - fy(vx)
                gy, gz = h_ref[2 * ch], h_ref[2 * ch + 1]
                h_ref[2 * ch] = hy
                h_ref[2 * ch + 1] = hz
                cx = by(hz) - bz(hy)
                cy = bz(hx) - (hz - gz)
                cz = (hy - gy) - by(hx)
                for comp, cv in enumerate((cx, cy, cz)):
                    o = e_ref[0, f, 1 - part, comp, p]
                    r_ref[3 * ch + comp, p] = cv + rotate_add(part, w, o) - s_ref[0, f, part, comp, p]
        return carry

    lax.fori_loop(0, PL, first, 0)
    for i in range(8):
        h_ref[i] = zero

    def second(p, carry):
        sig = c_ref[0, p]
        acc = zero
        for f in range(NF):
            om = om_ref[f]
            tot = zero
            dia = zero
            for part in range(2):
                ch = 2 * f + part
                vx, vy, vz = (r_ref[3 * ch + c, p] for c in range(3))
                ny = r_ref[3 * ch + 1, p + 1]
                nz = r_ref[3 * ch + 2, p + 1]
                hx = fy(vz) - fz(vy)
                hy = fz(vx) - (nz - vz)
                hz = (ny - vy) - fy(vx)
                gy, gz = h_ref[2 * ch], h_ref[2 * ch + 1]
                h_ref[2 * ch] = hy
                h_ref[2 * ch + 1] = hz
                cx = by(hz) - bz(hy)
                cy = bz(hx) - (hz - gz)
                cz = (hy - gy) - by(hx)
                o = [e_ref[0, f, 1 - part, c, p] for c in range(3)]
                s = [e_ref[0, f, part, c, p] for c in range(3)]
                t = o[0] * cx + o[1] * cy + o[2] * cz
                tot = tot + t if part == 1 else tot - t
                dia = dia + (s[0] * vx + s[1] * vy + s[2] * vz)
            acc = acc + (SCALE * om * live) * (tot + (om * sig) * dia)
        loc_ref[pl.ds(pl.multiple_of(p * NY, NY), NY), :] = acc
        return carry

    lax.fori_loop(0, PL, second, 0)

    bt = lax.broadcasted_iota(I32, (DEV, ROWS), 0) == rb_ref[...]
    hot = one_hot(bt)
    before = one_hot(lax.broadcasted_iota(I32, (ROWS, ROWS), 0) < lax.broadcasted_iota(I32, (ROWS, ROWS), 1))
    counts = dot(hot, before)
    rank = jnp.sum(jnp.where(bt, counts, 0.0), axis=0, keepdims=True)
    own8 = jnp.broadcast_to(own_ref[...].astype(F32), (8, DEV)).astype(BF16)
    dest = dot(own8, hot)[0:1]
    base = (dest * SLOTS).astype(I32)
    rank = rank.astype(I32)
    slot = base + rank
    slot_ref[...] = jnp.broadcast_to(slot, (8, ROWS))
    at = lax.broadcasted_iota(I32, (DEV * SLOTS, ROWS), 0)
    codes = jnp.where(lax.broadcasted_iota(I32, (NZ, ROWS), 0) == rank, (ro_ref[...] + 1).astype(F32), 0.0).astype(BF16)
    index = lax.dot_general(one_hot(at == base + CAP), codes, (((1,), (1,)), ((), ())), preferred_element_type=F32)
    out_ref[...] = index + exact_dot(one_hot(at == slot), loc_ref[...])


def finish_kernel(om_ref, tb_ref, elo_ref, ehi_ref, clo_ref, chi_ref, ups_ref, dns_ref, upr_ref, dnr_ref, slot_ref, part_ref, out_ref, loc_ref):
    brick, span = active_of(tb_ref)
    live = jnp.where(brick < span, 1.0, 0.0).astype(F32)
    low = jnp.where(brick > 0, 1.0, 0.0).astype(F32)
    nxt = jnp.where(brick + 1 < span, 1.0, 0.0).astype(F32)
    zero = jnp.zeros((NY, NZ), F32)
    acc = [zero, zero, zero, zero]
    for f in range(NF):
        om = om_ref[f]
        weight = SCALE * om * live
        tot = [zero, zero, zero, zero]
        dia = [zero, zero]
        for part in range(2):
            ch = 2 * f + part
            y, z = 2 * ch, 2 * ch + 1

            def add(which, terms):
                tot[which] = tot[which] + terms if part == 1 else tot[which] - terms

            ey, ez = dns_ref[y], dns_ref[z]
            dry = low * (ey - upr_ref[z])
            drz = low * (ez - upr_ref[y])
            ry, rz = dns_ref[8 + y] + dry, dns_ref[8 + z] + drz
            div = by(ey) + bz(ez)
            qy = upr_ref[8 + y] + fz(div) - ez
            qz = upr_ref[8 + z] + fy(div) - ey
            gy = low * (qy - rz)
            gz = low * (ry - qz)
            hx = fy(drz) - fz(dry)
            ax = -(by(dry) + bz(drz))
            ay = bz(hx) + dry + gz
            az = drz - by(hx) - gy
            o = [elo_ref[0, f, 1 - part, c, 0] for c in range(3)]
            add(0, o[0] * ax + o[1] * ay + o[2] * az)
            dia[0] = dia[0] + (ey * dry + ez * drz)
            add(1, -(elo_ref[0, f, 1 - part, 1, 1] * dry + elo_ref[0, f, 1 - part, 2, 1] * drz))

            ey, ez = nxt * dnr_ref[y], nxt * dnr_ref[z]
            dx = by(ey) + bz(ez)
            ry = nxt * (dnr_ref[8 + y] + (ey - ups_ref[z]))
            rz = nxt * (dnr_ref[8 + z] - (ups_ref[y] - ez))
            hx = fz(ey) - fy(ez)
            hy = fz(dx) - (rz + ez)
            hz = (ry + ey) - fy(dx)
            ax = by(hz) - bz(hy)
            ay = bz(hx) - (hz + ey)
            az = (hy - ez) - by(hx)
            o = [ehi_ref[0, f, 1 - part, c, 1] for c in range(3)]
            s = [ehi_ref[0, f, part, c, 1] for c in range(3)]
            add(3, o[0] * ax + o[1] * ay + o[2] * az)
            dia[1] = dia[1] + (s[0] * dx - s[1] * ey - s[2] * ez)
            o = [ehi_ref[0, f, 1 - part, c, 0] for c in range(3)]
            add(2, o[1] * ey + o[2] * ez - o[0] * dx)
        acc[0] = acc[0] + weight * (tot[0] + (om * clo_ref[0, 0]) * dia[0])
        acc[1] = acc[1] + weight * tot[1]
        acc[2] = acc[2] + weight * tot[2]
        acc[3] = acc[3] + weight * (tot[3] + (om * chi_ref[0, 0]) * dia[1])
    for i in range(4):
        loc_ref[i * NY:(i + 1) * NY, :] = acc[i]
    at = lax.broadcasted_iota(I32, (DEV * SLOTS, 2 * NY), 0)
    hot = jnp.concatenate(
        [one_hot(at == slot_ref[0:1, 0:2 * NY]), one_hot(at == slot_ref[0:1, ROWS - 2 * NY:ROWS])], axis=1
    )
    out_ref[...] = part_ref[...] + exact_dot(hot, loc_ref[...])


def owner_kernel(got_ref, out_ref):
    codes = got_ref[pl.ds(CAP, DEV, stride=SLOTS), :]
    offs = codes.T[0:CAP].astype(I32)
    want = lax.broadcasted_iota(I32, (G_DEV, DEV), 0) + 1
    total = jnp.zeros((G_DEV, NZ), F32)
    for k in range(CAP):
        hot = one_hot(want == offs[k:k + 1])
        total = total + exact_dot(hot, got_ref[pl.ds(k, DEV, stride=SLOTS), :])
    out_ref[...] = total


SMEM = pl.BlockSpec(memory_space=pltpu.SMEM)
LIMIT = 48 * 1024 * 1024


def full(shape):
    return pl.BlockSpec(shape, lambda i: (0,) * len(shape))


def planes(start, count):
    return pl.BlockSpec((1, NF, 2, 3, count, NY, NZ), lambda i: (0, 0, 0, 0, start // count, 0, 0))


def cells(start):
    return pl.BlockSpec((1, 1, NY, NZ), lambda i: (0, start, 0, 0))


def params():
    return pltpu.CompilerParams(vmem_limit_bytes=LIMIT)


def per_device(fields, sources, conductivity, omegas, tx_bricks, owner_map, row_brick, row_offset):
    pay = jax.ShapeDtypeStruct((16, NY, NZ), F32)
    up, dn = pl.pallas_call(
        payload_kernel,
        grid=(1,),
        in_specs=[SMEM, planes(0, 2), planes(6, 2), planes(0, 1), planes(7, 1), cells(0), cells(7)],
        out_specs=[full((16, NY, NZ))] * 2,
        out_shape=[pay, pay],
        compiler_params=params(),
        cost_estimate=pl.CostEstimate(flops=2_000_000, bytes_accessed=3_400_000, transcendentals=0),
        name="payload",
    )(omegas, fields, fields, sources, sources, conductivity, conductivity)
    ring = [(i, (i + 1) % BRICK) for i in range(BRICK)]
    back = [(b, a) for a, b in ring]
    up_got = lax.ppermute(up, "brick", ring)
    dn_got = lax.ppermute(dn, "brick", back)
    part, slot = pl.pallas_call(
        main_kernel,
        grid=(1,),
        in_specs=[
            SMEM,
            SMEM,
            full((1, NF, 2, 3, PL, NY, NZ)),
            full((1, NF, 2, 3, PL, NY, NZ)),
            full((1, PL, NY, NZ)),
            full((1, ROWS)),
            full((1, ROWS)),
            full((1, DEV)),
        ],
        out_specs=[full((DEV * SLOTS, NZ)), full((8, ROWS))],
        out_shape=[
            jax.ShapeDtypeStruct((DEV * SLOTS, NZ), F32),
            jax.ShapeDtypeStruct((8, ROWS), I32),
        ],
        scratch_shapes=[
            pltpu.VMEM((12, PL + 1, NY, NZ), F32),
            pltpu.VMEM((8, NY, NZ), F32),
            pltpu.VMEM((ROWS, NZ), F32),
        ],
        compiler_params=params(),
        cost_estimate=pl.CostEstimate(flops=60_000_000, bytes_accessed=8_000_000, transcendentals=0),
        name="interior",
    )(
        omegas,
        tx_bricks,
        fields,
        sources,
        conductivity,
        row_brick.reshape(1, ROWS),
        row_offset,
        owner_map.reshape(1, DEV),
    )
    packed = pl.pallas_call(
        finish_kernel,
        grid=(1,),
        in_specs=[SMEM, SMEM, planes(0, 2), planes(6, 2), cells(0), cells(7)]
        + [full((16, NY, NZ))] * 4
        + [full((8, ROWS)), full((DEV * SLOTS, NZ))],
        out_specs=full((DEV * SLOTS, NZ)),
        out_shape=jax.ShapeDtypeStruct((DEV * SLOTS, NZ), F32),
        scratch_shapes=[pltpu.VMEM((4 * NY, NZ), F32)],
        compiler_params=params(),
        cost_estimate=pl.CostEstimate(flops=40_000_000, bytes_accessed=4_000_000, transcendentals=0),
        name="finish",
    )(omegas, tx_bricks, fields, fields, conductivity, conductivity, up, dn, up_got, dn_got, slot, part)
    got = lax.all_to_all(
        packed.reshape(DEV, 1, SLOTS * NZ), ("tx", "brick"), 0, 0, tiled=True
    ).reshape(DEV * SLOTS, NZ)
    return pl.pallas_call(
        owner_kernel,
        grid=(1,),
        in_specs=[full((DEV * SLOTS, NZ))],
        out_specs=full((G_DEV, NZ)),
        out_shape=jax.ShapeDtypeStruct((G_DEV, NZ), F32),
        compiler_params=params(),
        name="owner_sum",
    )(got)


def solution(mesh):
    return jax.shard_map(
        per_device,
        mesh=mesh,
        in_specs=(
            P("tx", None, None, None, "brick", None, None),
            P("tx", None, None, None, "brick", None, None),
            P("tx", "brick", None, None),
            P(),
            P(),
            P(),
            P("tx", "brick", None),
            P("tx", "brick"),
        ),
        out_specs=P(("tx", "brick"), None),
        check_vma=False,
    )
```

time: 718 us -> 51.6 us (0.07)
  waiting for transfers between devices: 654 us -> 3.03 us
  other arithmetic: 25.8 us -> 0 us
  blocking collectives: 0 us -> 23.8 us
  between operations: 14.5 us -> 0.04 us
  Pallas kernels: 0 us -> 14.4 us
  local copies, waits for them, and re-layouts: 12.5 us -> 3.51 us
    reduce_scatter x1 -> x0, waiting for transfers between devices: 644 us -> none  [per_device(): lax.psum_scatter(buffer, ('tx', 'brick'), scatter_dimension=0, tiled=True)]
    all_to_all x0 -> x1, blocking collectives: none -> 23.8 us  [per_device(): lax.all_to_all(packed.reshape(DEV, 1, SLOTS * NZ), ('tx', 'brick'), 0, 0,...]
    pallas_call x0 -> x4, Pallas kernels: none -> 14.4 us  [the longest x1 8.79 us: per_device(): pl.pallas_call(main_kernel, grid=(1,), in_specs=[SMEM, SMEM, full((1, NF,...]
    mul x9 -> x0, other arithmetic: 9.22 us -> none  [the longest x2 4.26 us: per_device(): efield = fields[0] * active]
    slice x18 -> x0, local copies, waits for them, and re-layouts: 8.07 us -> none  [the longest x1 4.01 us: apply_crop(): rotated = jnp.stack([-inner[:, 1], inner[:, 0]], axis=1)]
  transfers between devices with their start and end apart: 5 -> 2, of which waited for: 4 -> 1; matrix products, arithmetic and copies ran while one was open for 2% -> 0% of each run, Pallas kernels for 0% -> 17%
where the time goes in v1:
time: 51.6 us; the launch traced here: 51.3 us
  blocking collectives  23.8 us (46%)
  Pallas kernels  14.4 us (28%)
  starting transfers between devices  6.47 us (13%)
  local copies, waits for them, and re-layouts  3.51 us (7%)
  waiting for transfers between devices  3.03 us (6%)
    all_to_all x1, blocking collectives, per_device(): lax.all_to_all(packed.reshape(DEV, 1, SLOTS * NZ), ('tx', 'brick'), 0, 0,...  23.8 us
    pallas_call x1, Pallas kernels, per_device(): pl.pallas_call(main_kernel, grid=(1,), in_specs=[SMEM, SMEM, full((1, NF,...  8.79 us
    ppermute x1, starting transfers between devices, per_device(): dn_got = lax.ppermute(dn, 'brick', back)  4.4 us
    unnamed x16, local copies, waits for them, and re-layouts  3.51 us
    ppermute x1, waiting for transfers between devices, per_device(): up_got = lax.ppermute(up, 'brick', ring)  3.03 us
    pallas_call x1, Pallas kernels, per_device(): pl.pallas_call(finish_kernel, grid=(1,), in_specs=[SMEM, SMEM, planes(0,...  2.73 us
    ppermute x1, starting transfers between devices, per_device(): up_got = lax.ppermute(up, 'brick', ring)  2.07 us
    pallas_call x1, Pallas kernels, per_device(): pl.pallas_call(payload_kernel, grid=(1,), in_specs=[SMEM, planes(0, 2), p...  1.93 us
  transfers between devices with their start and end apart: 2, of which 1 were waited for; matrix products, arithmetic and copies ran while one was open for 0% of the time, Pallas kernels for 17%

profile of v1, /device:TPU:0, one launch (start us, length us, event | category | flops | bytes accessed | tf_op | source)
XLA Modules:
  0.0 51.3 jit_solution(14103978861580323699)
XLA Ops:
  0.0 0.0 copy-start
  0.0 1.9 %copy-done = f32[1,2,2,3,8,64,128]{6,5,4,3,2,1,0:T(8,128)S(1)} copy-done((f32[1,2,2,3,8,64,128]{6,5,4,3,2,1,0:T(8,128)S(1)}, f32[1,2,2,3,8,64,128]{6,5,4,3,2,1,0:T(8,128)}, u32[]{:S(2)}) %copy-start) | copy-done | bytes 3145752
  1.9 0.0 copy-start.1
  1.9 0.9 %copy-done.1 = f32[1,8,64,128]{3,2,1,0:T(8,128)S(1)} copy-done((f32[1,8,64,128]{3,2,1,0:T(8,128)S(1)}, f32[1,8,64,128]{3,2,1,0:T(8,128)}, u32[]{:S(2)}) %copy-start.1) | copy-done | bytes 262168
  2.8 0.0 copy-start.3
  2.8 0.7 %copy-done.3 = f32[2]{0:T(128)S(1)} copy-done((f32[2]{0:T(128)S(1)}, f32[2]{0:T(128)}, u32[]{:S(2)}) %copy-start.3) | copy-done | bytes 32
  3.5 0.0 copy-start.4
  3.5 0.0 copy-start.5
  3.5 0.0 copy-start.6
  3.5 0.0 copy-start.7
  3.5 1.9 %payload.1 = (f32[16,64,128]{2,1,0:T(8,128)S(1)}, f32[16,64,128]{2,1,0:T(8,128)S(1)}) custom-call(f32[2]{0:T(128)S(1)} %copy-done.3, f32[1,2,2,3,8,64,128]{6,5,4,3,2,1,0:T(8,128)S(1)} %copy-done, f32[1,2,2,3,8,64,128]{6,5,4,3,2,1,0:T(8,128)S(1)} %copy-done, f32[1,2,2,3,8,64,128]{6,5,4,3,2,1,0:T(8,128)} %s_ref.1, f32[1,2,2,3,8,64,128]{6,5,4,3,2,1,0:T(8,128)} %s_ref.1, ...), custom_call_target="tpu_custom_call" | custom-call | flops 2000000 | bytes 3400000 | tf_op jit(solution)/shard_map/payload/pallas_call | solution.py:312
  5.4 2.1 %collective-permute-start = (f32[16,64,128]{2,1,0:T(8,128)S(1)}, f32[16,64,128]{2,1,0:T(8,128)S(1)}, u32[]{:S(2)}, u32[]{:S(2)}) collective-permute-start(f32[16,64,128]{2,1,0:T(8,128)S(1)} %get-tuple-element.9.ups_ref), channel_id=1, source_target_pairs={{0,1},{1,2},{2,3},{3,4},{4,5},{5,6},{6,7},{7,8},{8,9},{9,10},{10,1... | collective-permute-start | bytes 1572872 | tf_op jit(solution)/shard_map/ppermute | solution.py:324
  7.5 4.4 %collective-permute-start.1 = (f32[16,64,128]{2,1,0:T(8,128)S(1)}, f32[16,64,128]{2,1,0:T(8,128)S(1)}, u32[]{:S(2)}, u32[]{:S(2)}) collective-permute-start(f32[16,64,128]{2,1,0:T(8,128)S(1)} %get-tuple-element.10.dns_ref), channel_id=1, source_target_pairs={{1,0},{2,1},{3,2},{4,3},{5,4},{6,5},{7,6},{8,7},{9,8},{10,9},{11,1... | collective-permute-start | bytes 1572872 | tf_op jit(solution)/shard_map/ppermute | solution.py:325
  11.9 0.0 copy-done.4
  11.9 0.0 copy-done.5
  11.9 0.0 copy-done.6
  11.9 0.0 copy-done.7
  11.9 0.0 copy-start.2
  11.9 8.8 %interior.1 = (f32[1152,128]{1,0:T(8,128)S(1)}, s32[8,512]{1,0:T(8,128)S(1)}) custom-call(f32[2]{0:T(128)S(1)} %copy-done.3, s32[8]{0:T(128)S(1)} %copy-done.6, f32[1,2,2,3,8,64,128]{6,5,4,3,2,1,0:T(8,128)S(1)} %copy-done, f32[1,2,2,3,8,64,128]{6,5,4,3,2,1,0:T(8,128)} %s_ref.1, f32[1,8,64,128]{3,2,1,0:T(8,128)S(1)} %copy-done.1, s32[1,512]{1,0:T(1,128)S(1)} %bitcast.6, ...), custom_call_target="tpu_custom_call" | custom-call | flops 60000000 | bytes 8000000 | tf_op jit(solution)/shard_map/interior/pallas_call | solution.py:326
  20.7 3.0 %collective-permute-done.upr_ref = f32[16,64,128]{2,1,0:T(8,128)S(1)} collective-permute-done((f32[16,64,128]{2,1,0:T(8,128)S(1)}, f32[16,64,128]{2,1,0:T(8,128)S(1)}, u32[]{:S(2)}, u32[]{:S(2)}) %collective-permute-start) | collective-permute-done | bytes 524320 | tf_op jit(solution)/shard_map/ppermute | solution.py:324
  23.8 0.0 collective-permute-done.1.dnr_ref
  23.8 0.0 copy-done.2
  23.8 2.7 %finish.1 = f32[1152,128]{1,0:T(8,128)S(1)} custom-call(f32[2]{0:T(128)S(1)} %copy-done.3, s32[8]{0:T(128)S(1)} %copy-done.6, f32[1,2,2,3,8,64,128]{6,5,4,3,2,1,0:T(8,128)} %ehi_ref.3, f32[1,2,2,3,8,64,128]{6,5,4,3,2,1,0:T(8,128)} %ehi_ref.3, f32[1,8,64,128]{3,2,1,0:T(8,128)S(1)} %copy-done.2, f32[1,8,64,128]{3,2,1,0:T(8,128)S(1)} %copy-done.2, ...), custom_call_target="tpu_custom_call" | custom-call | flops 40000000 | bytes 4000000 | tf_op jit(solution)/shard_map/finish/pallas_call | solution.py:362
  26.5 23.8 %all_to_all.5 = f32[128,1,1152]{2,1,0:T(1,128)S(1)} all-to-all(f32[128,1,1152]{2,1,0:T(1,128)S(1)} %bitcast.5), channel_id=1, replica_groups=mesh['tx'=8,'brick'=16] {'tx','brick'}, dimensions={0} | all-to-all | bytes 1179648 | tf_op jit(solution)/shard_map/all_to_all | solution.py:375
  50.3 1.0 %owner_sum.1 = f32[32,128]{1,0:T(8,128)} custom-call(f32[1152,128]{1,0:T(8,128)S(1)} %bitcast.4), custom_call_target="tpu_custom_call" | custom-call | tf_op jit(solution)/shard_map/owner_sum/pallas_call | solution.py:378
Async XLA Ops:
  0.0 1.9 %copy-start = (f32[1,2,2,3,8,64,128]{6,5,4,3,2,1,0:T(8,128)S(1)}, f32[1,2,2,3,8,64,128]{6,5,4,3,2,1,0:T(8,128)}, u32[]{:S(2)}) copy-start(f32[1,2,2,3,8,64,128]{6,5,4,3,2,1,0:T(8,128)} %ehi_ref.3) | copy-start | bytes 9437188
  1.9 0.9 %copy-start.1 = (f32[1,8,64,128]{3,2,1,0:T(8,128)S(1)}, f32[1,8,64,128]{3,2,1,0:T(8,128)}, u32[]{:S(2)}) copy-start(f32[1,8,64,128]{3,2,1,0:T(8,128)} %chi_ref.3) | copy-start | bytes 786436
  2.8 0.7 %copy-start.3 = (f32[2]{0:T(128)S(1)}, f32[2]{0:T(128)}, u32[]{:S(2)}) copy-start(f32[2]{0:T(128)} %om_ref.5) | copy-start | bytes 28
  3.5 8.4 %copy-start.4 = (s32[1,512,1]{1,2,0:T(1,128)S(1)}, s32[1,512,1]{1,2,0:T(1,128)}, u32[]{:S(2)}) copy-start(s32[1,512,1]{1,2,0:T(1,128)} %param.14) | copy-start | bytes 6148
  3.5 8.4 %copy-start.5 = (s32[1,512]{1,0:T(1,128)S(1)}, s32[1,512]{1,0:T(1,128)}, u32[]{:S(2)}) copy-start(s32[1,512]{1,0:T(1,128)} %ro_ref.1) | copy-start | bytes 6148
  3.5 8.4 %copy-start.6 = (s32[8]{0:T(128)S(1)}, s32[8]{0:T(128)}, u32[]{:S(2)}) copy-start(s32[8]{0:T(128)} %tb_ref.3) | copy-start | bytes 100
  3.5 8.4 %copy-start.7 = (s32[128]{0:T(128)S(1)}, s32[128]{0:T(128)}, u32[]{:S(2)}) copy-start(s32[128]{0:T(128)} %param.13) | copy-start | bytes 1540
  5.4 18.3 %collective-permute-start = (f32[16,64,128]{2,1,0:T(8,128)S(1)}, f32[16,64,128]{2,1,0:T(8,128)S(1)}, u32[]{:S(2)}, u32[]{:S(2)}) collective-permute-start(f32[16,64,128]{2,1,0:T(8,128)S(1)} %get-tuple-element.9.ups_ref), channel_id=1, source_target_pairs={{0,1},{1,2},{2,3},{3,4},{4,5},{5,6},{6,7},{7,8},{8,9},{9,10},{10,1... | collective-permute-start | bytes 1572872 | tf_op jit(solution)/shard_map/ppermute | solution.py:324
  7.5 16.2 %collective-permute-start.1 = (f32[16,64,128]{2,1,0:T(8,128)S(1)}, f32[16,64,128]{2,1,0:T(8,128)S(1)}, u32[]{:S(2)}, u32[]{:S(2)}) collective-permute-start(f32[16,64,128]{2,1,0:T(8,128)S(1)} %get-tuple-element.10.dns_ref), channel_id=1, source_target_pairs={{1,0},{2,1},{3,2},{4,3},{5,4},{6,5},{7,6},{8,7},{9,8},{10,9},{11,1... | collective-permute-start | bytes 1572872 | tf_op jit(solution)/shard_map/ppermute | solution.py:325
  11.9 11.8 %copy-start.2 = (f32[1,8,64,128]{3,2,1,0:T(8,128)S(1)}, f32[1,8,64,128]{3,2,1,0:T(8,128)}, u32[]{:S(2)}) copy-start(f32[1,8,64,128]{3,2,1,0:T(8,128)} %chi_ref.3) | copy-start | bytes 786436

commit v2 on v0

v2 whole, which is shorter than its diff:
```python
import jax
import jax.numpy as jnp
from jax import lax
from jax.experimental import pallas as pl
from jax.experimental.pallas import tpu as pltpu
from jax.sharding import PartitionSpec as P

PL, NY, NZ, NF = 8, 64, 128, 2
ROWS = PL * NY
G_DEV = 32
CAP = 8
DEV = 128
SLOTS = CAP + 1
BRICK = 16
PAD = 8
CH = 32
F32, BF16, I32 = jnp.float32, jnp.bfloat16, jnp.int32
SCALE = 0.003


def fy(v):
    rows = lax.broadcasted_iota(I32, v.shape, 0)
    return jnp.where(rows == NY - 1, 0.0, pltpu.roll(v, NY - 1, 0)) - v


def by(v):
    rows = lax.broadcasted_iota(I32, v.shape, 0)
    return v - jnp.where(rows == 0, 0.0, pltpu.roll(v, 1, 0))


def fz(v):
    lanes = lax.broadcasted_iota(I32, v.shape, 1)
    return jnp.where(lanes == NZ - 1, 0.0, pltpu.roll(v, NZ - 1, 1)) - v


def bz(v):
    lanes = lax.broadcasted_iota(I32, v.shape, 1)
    return v - jnp.where(lanes == 0, 0.0, pltpu.roll(v, 1, 1))


def q_of(vx, vy, vz):
    return fz(vx) + vz, vy + fy(vx)


def rotate(curl, part, weight, other):
    return curl - weight * other if part == 0 else curl + weight * other


def signed(part, value):
    return value if part == 1 else -value


def halo_kernel(
    om_hbm, e_hbm, s_hbm, c_hbm, up_ref, dn_ref, upr_ref, dnr_ref,
    om_ref, elo_ref, ehi_ref, slo_ref, shi_ref, cc_ref, sems,
):
    small = [
        pltpu.make_async_copy(om_hbm, om_ref, sems.at[8]),
        pltpu.make_async_copy(c_hbm.at[0, 0], cc_ref.at[0], sems.at[9]),
        pltpu.make_async_copy(c_hbm.at[0, PL - 1], cc_ref.at[1], sems.at[10]),
    ]
    big = [
        [
            pltpu.make_async_copy(e_hbm.at[0, f, :, :, pl.ds(PL - 2, 2)], ehi_ref.at[f], sems.at[4 * f]),
            pltpu.make_async_copy(s_hbm.at[0, f, :, :, PL - 1], shi_ref.at[f], sems.at[4 * f + 1]),
            pltpu.make_async_copy(e_hbm.at[0, f, :, :, pl.ds(0, 2)], elo_ref.at[f], sems.at[4 * f + 2]),
            pltpu.make_async_copy(s_hbm.at[0, f, :, pl.ds(1, 2), 0], slo_ref.at[f], sems.at[4 * f + 3]),
        ]
        for f in range(NF)
    ]
    for copy in small + big[0] + big[1]:
        copy.start()
    for copy in small:
        copy.wait()
    for f in range(NF):
        om = om_ref[f]
        big[f][0].wait()
        big[f][1].wait()
        for part in range(2):
            ch = 2 * f + part
            ux, uy, uz = (ehi_ref[f, part, c, 0] for c in range(3))
            vx, vy, vz = (ehi_ref[f, part, c, 1] for c in range(3))
            hy, qz = q_of(vx, vy, vz)
            up_ref[2 * ch] = hy
            up_ref[2 * ch + 1] = qz
            hz = -qz
            hx = fy(vz) - fz(vy)
            gy = fz(ux) - (vz - uz)
            gz = (vy - uy) - fy(ux)
            w = om * cc_ref[1]
            o = [ehi_ref[f, 1 - part, c, 1] for c in range(3)]
            rx = rotate(by(hz) - bz(hy), part, w, o[0]) - shi_ref[f, part, 0]
            ry = rotate(bz(hx) - (hz - gz), part, w, o[1]) - shi_ref[f, part, 1]
            rz = rotate((hy - gy) - by(hx), part, w, o[2]) - shi_ref[f, part, 2]
            sy, sz = q_of(rx, ry, rz)
            upr_ref[2 * ch] = sy
            upr_ref[2 * ch + 1] = sz
        big[f][2].wait()
        big[f][3].wait()
        for part in range(2):
            ch = 2 * f + part
            vx, vy, vz = (elo_ref[f, part, c, 0] for c in range(3))
            dn_ref[2 * ch] = vy
            dn_ref[2 * ch + 1] = vz
            hx = fy(vz) - fz(vy)
            hy = fz(vx) - (elo_ref[f, part, 2, 1] - vz)
            hz = (elo_ref[f, part, 1, 1] - vy) - fy(vx)
            w = om * cc_ref[0]
            dnr_ref[2 * ch] = rotate(bz(hx) - hz, part, w, elo_ref[f, 1 - part, 1, 0]) - slo_ref[f, part, 0]
            dnr_ref[2 * ch + 1] = rotate(hy - by(hx), part, w, elo_ref[f, 1 - part, 2, 0]) - slo_ref[f, part, 1]


def one_hot(cond):
    return jnp.where(cond, 1.0, 0.0).astype(BF16)


def dot(a, b):
    return jnp.dot(a, b, preferred_element_type=F32)


def pick(hot, v):
    hi = v.astype(BF16)
    low = (v - hi.astype(F32)).astype(BF16)
    both = dot(hot, jnp.concatenate([hi, low], axis=1))
    return both[:, 0:NZ] + both[:, NZ:2 * NZ]


def place(tb_ref):
    brick = lax.axis_index("brick")
    span = tb_ref[lax.axis_index("tx")]
    live = jnp.where(brick < span, 1.0, 0.0).astype(F32)
    low = jnp.where(brick > 0, 1.0, 0.0).astype(F32)
    nxt = jnp.where(brick + 1 < span, 1.0, 0.0).astype(F32)
    return live, low, nxt


EDGE = (0, 1, PL - 2, PL - 1)


def main_kernel(
    om_ref, tb_ref, e_hbm, s_hbm, c_hbm, rb_ref, ro_ref, own_ref,
    part_ref, slot_ref, loc_ref, edge_ref, sig_ref, own_r_ref,
    e_ref, s_ref, c_ref, r_ref, h_ref, g_ref, sems,
):
    cp = pltpu.make_async_copy(c_hbm.at[0], c_ref, sems.at[2 * PL])
    cp.start()

    def fetch_e(p):
        return pltpu.make_async_copy(e_hbm.at[0, :, :, :, p], e_ref.at[:, :, :, p, pl.ds(0, NY)], sems.at[p])

    def fetch_s(p):
        return pltpu.make_async_copy(s_hbm.at[0, :, :, :, p], s_ref.at[:, :, :, p], sems.at[PL + p])

    for p in range(PL):
        fetch_e(p).start()
        fetch_s(p).start()

    live, _, _ = place(tb_ref)
    zero = jnp.zeros((NY, NZ), F32)
    zpad = jnp.zeros((PAD, NZ), F32)
    for f in range(NF):
        for part in range(2):
            for c in range(3):
                i = 3 * (2 * f + part) + c
                r_ref[i, PL, 0:NY] = zero
                e_ref[f, part, c, PL, 0:NY] = zero
                for p in range(PL):
                    r_ref[i, p, NY:NY + PAD] = zpad
                    e_ref[f, part, c, p, NY:NY + PAD] = zpad
    for i in range(8):
        h_ref[i, 0:PAD] = zpad
        h_ref[i, PAD:PAD + NY] = zero
    for i in range(4):
        g_ref[i] = zero

    bt = lax.broadcasted_iota(I32, (DEV, ROWS), 0) == rb_ref[...]
    hot = one_hot(bt)
    before = one_hot(lax.broadcasted_iota(I32, (ROWS, ROWS), 0) < lax.broadcasted_iota(I32, (ROWS, ROWS), 1))
    counts = dot(hot, before)
    rank = jnp.sum(jnp.where(bt, counts, 0.0), axis=0, keepdims=True)
    own8 = jnp.broadcast_to(own_ref[...].astype(F32), (8, DEV)).astype(BF16)
    dest = dot(own8, hot)[0:1].astype(I32)
    rank = rank.astype(I32)
    slot = dest * SLOTS + rank
    slot_ref[...] = jnp.broadcast_to(slot, (8, ROWS))
    codes = jnp.where(lax.broadcasted_iota(I32, (NZ, ROWS), 0) == rank, (ro_ref[...] + 1).astype(F32), 0.0).astype(BF16)
    mine = one_hot(lax.broadcasted_iota(I32, (DEV, ROWS), 0) == dest)
    index = lax.dot_general(mine, codes, (((1,), (1,)), ((), ())), preferred_element_type=F32)

    def curl(get, at, p, y, ch):
        lanes = lax.broadcasted_iota(I32, (CH, NZ), 1)

        def nz_(v):
            return jnp.where(lanes == NZ - 1, 0.0, pltpu.roll(v, NZ - 1, 1))

        def pz_(v):
            return jnp.where(lanes == 0, 0.0, pltpu.roll(v, 1, 1))

        vx, vy, vz = (get(c, p, y) for c in range(3))
        hx = (get(2, p, y + 1) - vz) - (nz_(vy) - vy)
        hy = (nz_(vx) - vx) - (get(2, p + 1, y) - vz)
        hz = (get(1, p + 1, y) - vy) - (get(0, p, y + 1) - vx)
        gy = g_ref[ch, y:y + CH]
        gz = h_ref[2 * ch + 1, PAD + y:PAD + y + CH]
        h_ref[2 * ch, PAD + y:PAD + y + CH] = hx
        h_ref[2 * ch + 1, PAD + y:PAD + y + CH] = hz
        g_ref[ch, y:y + CH] = hy
        hxp = h_ref[2 * ch, PAD + y - 1:PAD + y - 1 + CH]
        hzp = h_ref[2 * ch + 1, PAD + y - 1:PAD + y - 1 + CH]
        cx = (hz - hzp) - (hy - pz_(hy))
        cy = (hx - pz_(hx)) - (hz - gz)
        cz = (hy - gy) - (hx - hxp)
        return (vx, vy, vz), (cx, cy, cz)

    cp.wait()
    fetch_e(0).wait()

    def first(p, carry):
        @pl.when(p < PL - 1)
        def _():
            fetch_e(p + 1).wait()

        fetch_s(p).wait()
        for y in range(0, NY, CH):
            sig = c_ref[p, y:y + CH]
            for f in range(NF):
                w = om_ref[f] * sig
                for part in range(2):
                    _, cs = curl(lambda c, q, r: e_ref[f, part, c, q, r:r + CH], 0, p, y, 2 * f + part)
                    for c in range(3):
                        o = e_ref[f, 1 - part, c, p, y:y + CH]
                        r_ref[3 * (2 * f + part) + c, p, y:y + CH] = rotate(cs[c], part, w, o) - s_ref[f, part, c, p, y:y + CH]
        return carry

    lax.fori_loop(0, PL, first, 0)
    for i in range(4):
        h_ref[2 * i + 1, PAD:PAD + NY] = zero
        g_ref[i] = zero

    def second(p, carry):
        for y in range(0, NY, CH):
            sig = c_ref[p, y:y + CH]
            acc = jnp.zeros((CH, NZ), F32)
            for f in range(NF):
                om = om_ref[f]
                tot = jnp.zeros((CH, NZ), F32)
                dia = jnp.zeros((CH, NZ), F32)
                for part in range(2):
                    ch = 2 * f + part
                    vs, cs = curl(lambda c, q, r: r_ref[3 * ch + c, q, r:r + CH], 0, p, y, ch)
                    o = [e_ref[f, 1 - part, c, p, y:y + CH] for c in range(3)]
                    s = [e_ref[f, part, c, p, y:y + CH] for c in range(3)]
                    tot = tot + signed(part, o[0] * cs[0] + o[1] * cs[1] + o[2] * cs[2])
                    dia = dia + (s[0] * vs[0] + s[1] * vs[1] + s[2] * vs[2])
                acc = acc + (SCALE * om * live) * (tot + (om * sig) * dia)
            loc_ref[pl.ds(pl.multiple_of(p * NY + y, CH), CH), :] = acc
        return carry

    lax.fori_loop(0, PL, second, 0)

    for f in range(NF):
        for part in range(2):
            for c in range(3):
                for i, p in enumerate(EDGE):
                    edge_ref[3 * (2 * f + part) + c, i] = e_ref[f, part, c, p, 0:NY]
    for ch in range(4):
        own_r_ref[2 * ch] = r_ref[3 * ch + 1, 0, 0:NY]
        own_r_ref[2 * ch + 1] = r_ref[3 * ch + 2, 0, 0:NY]
    sig_ref[0] = c_ref[0]
    sig_ref[1] = c_ref[PL - 1]
    lo, hi = 2 * NY, ROWS - 2 * NY
    at = lax.broadcasted_iota(I32, (DEV * SLOTS, hi - lo), 0)
    part_ref[...] = pick(one_hot(at == slot[:, lo:hi]), loc_ref[lo:hi])
    part_ref[pl.ds(CAP, DEV, stride=SLOTS), :] = index


def field_fix_kernel(
    om_ref, tb_ref, edge_ref, sig_ref, loc_ref, ups_ref, dns_ref, dnr_ref, upg_ref, dng_ref, slot_ref, part_ref,
    out_ref, rest_ref, fac_ref, two_ref,
):
    live, low, nxt = place(tb_ref)
    zero = jnp.zeros((NY, NZ), F32)
    acc = [zero] * 4
    for f in range(NF):
        om = om_ref[f]
        weight = SCALE * om * live
        tot = [zero] * 4
        dia = [zero, zero]
        for part in range(2):
            ch = 2 * f + part
            mine, other = 3 * ch, 3 * (2 * f + 1 - part)
            y, z = 2 * ch, 2 * ch + 1

            def add(which, terms):
                tot[which] = tot[which] + signed(part, terms)

            ey, ez = dns_ref[y], dns_ref[z]
            dry = low * (ey - upg_ref[z])
            drz = low * (ez - upg_ref[y])
            ry, rz = dnr_ref[y] + dry, dnr_ref[z] + drz
            div = by(ey) + bz(ez)
            gy = low * (fz(div) - ez - rz)
            gz = low * (ry - fy(div) + ey)
            hx = fy(drz) - fz(dry)
            ax = -(by(dry) + bz(drz))
            ay = bz(hx) + dry + gz
            az = drz - by(hx) - gy
            o = [edge_ref[other + c, 0] for c in range(3)]
            add(0, o[0] * ax + o[1] * ay + o[2] * az)
            dia[0] = dia[0] + (ey * dry + ez * drz)
            add(1, -(edge_ref[other + 1, 1] * dry + edge_ref[other + 2, 1] * drz))
            scale = signed(part, weight) * low
            fac_ref[2 * ch] = -scale * o[2]
            fac_ref[2 * ch + 1] = -scale * o[1]

            ey, ez = nxt * dng_ref[y], nxt * dng_ref[z]
            dx = by(ey) + bz(ez)
            ry = nxt * (ey - ups_ref[z])
            rz = nxt * (ez - ups_ref[y])
            hx = fz(ey) - fy(ez)
            hy = fz(dx) - (rz + ez)
            hz = (ry + ey) - fy(dx)
            ax = by(hz) - bz(hy)
            ay = bz(hx) - (hz + ey)
            az = (hy - ez) - by(hx)
            o = [edge_ref[other + c, 3] for c in range(3)]
            s = [edge_ref[mine + c, 3] for c in range(3)]
            add(3, o[0] * ax + o[1] * ay + o[2] * az)
            dia[1] = dia[1] + (s[0] * dx - s[1] * ey - s[2] * ez)
            scale = signed(part, weight) * nxt
            for c in range(3):
                fac_ref[8 + 3 * ch + c] = scale * o[c]
            o = [edge_ref[other + c, 2] for c in range(3)]
            add(2, o[1] * ey + o[2] * ez - o[0] * dx)
        acc[0] = acc[0] + weight * (tot[0] + (om * sig_ref[0]) * dia[0])
        acc[1] = acc[1] + weight * tot[1]
        acc[2] = acc[2] + weight * tot[2]
        acc[3] = acc[3] + weight * (tot[3] + (om * sig_ref[1]) * dia[1])
    rest_ref[0] = loc_ref[0:NY] + acc[0]
    rest_ref[1] = loc_ref[ROWS - NY:ROWS] + acc[3]
    two_ref[0:NY] = loc_ref[NY:2 * NY] + acc[1]
    two_ref[NY:2 * NY] = loc_ref[ROWS - 2 * NY:ROWS - NY] + acc[2]
    at = lax.broadcasted_iota(I32, (DEV * SLOTS, NY), 0)
    hot = jnp.concatenate(
        [one_hot(at == slot_ref[0:1, NY:2 * NY]), one_hot(at == slot_ref[0:1, ROWS - 2 * NY:ROWS - NY])], axis=1
    )
    out_ref[...] = part_ref[...] + pick(hot, two_ref[...])


def residual_fix_kernel(fac_ref, rest_ref, upg_ref, dng_ref, slot_ref, part_ref, out_ref, two_ref):
    low, high = rest_ref[0], rest_ref[1]
    for ch in range(4):
        low = low + (fac_ref[2 * ch] * upg_ref[2 * ch] + fac_ref[2 * ch + 1] * upg_ref[2 * ch + 1])
        ry, rz = dng_ref[2 * ch], dng_ref[2 * ch + 1]
        o = [fac_ref[8 + 3 * ch + c] for c in range(3)]
        high = high + (o[0] * (by(ry) + bz(rz)) - o[1] * ry - o[2] * rz)
    two_ref[0:NY] = low
    two_ref[NY:2 * NY] = high
    at = lax.broadcasted_iota(I32, (DEV * SLOTS, NY), 0)
    hot = jnp.concatenate([one_hot(at == slot_ref[0:1, 0:NY]), one_hot(at == slot_ref[0:1, ROWS - NY:ROWS])], axis=1)
    out_ref[...] = part_ref[...] + pick(hot, two_ref[...])


def owner_kernel(got_ref, out_ref):
    codes = got_ref[pl.ds(CAP, DEV, stride=SLOTS), :]
    offs = codes.T[0:CAP].astype(I32)
    want = lax.broadcasted_iota(I32, (G_DEV, DEV), 0) + 1
    total = jnp.zeros((G_DEV, NZ), F32)
    for k in range(CAP):
        total = total + pick(one_hot(want == offs[k:k + 1]), got_ref[pl.ds(k, DEV, stride=SLOTS), :])
    out_ref[...] = total


SMEM = pl.BlockSpec(memory_space=pltpu.SMEM)
VMEM = pl.BlockSpec(memory_space=pltpu.VMEM)
HBM = pl.BlockSpec(memory_space=pltpu.HBM)
LIMIT = 40 * 1024 * 1024


def f32(*shape):
    return jax.ShapeDtypeStruct(shape, F32)


def call(kernel, name, ins, outs, scratch, flops, moved):
    return pl.pallas_call(
        kernel,
        in_specs=ins,
        out_specs=[VMEM] * len(outs),
        out_shape=outs,
        scratch_shapes=scratch,
        compiler_params=pltpu.CompilerParams(vmem_limit_bytes=LIMIT),
        cost_estimate=pl.CostEstimate(flops=flops, bytes_accessed=moved, transcendentals=0),
        name=name,
    )


def per_device(fields, sources, conductivity, omegas, tx_bricks, owner_map, row_brick, row_offset):
    omegas_in = omegas
    fields, sources, conductivity, omegas = (
        pltpu.with_memory_space_constraint(x, pltpu.HBM) for x in (fields, sources, conductivity, omegas)
    )
    ring = [(i, (i + 1) % BRICK) for i in range(BRICK)]
    back = [(b, a) for a, b in ring]
    pay = f32(8, NY, NZ)
    packed = f32(DEV * SLOTS, NZ)
    dma = pltpu.SemaphoreType.DMA
    up_e, dn_e, up_r, dn_r = call(
        halo_kernel, "halo", [HBM] * 4, [pay] * 4,
        [
            pltpu.SMEM((NF,), F32),
            pltpu.VMEM((NF, 2, 3, 2, NY, NZ), F32),
            pltpu.VMEM((NF, 2, 3, 2, NY, NZ), F32),
            pltpu.VMEM((NF, 2, 2, NY, NZ), F32),
            pltpu.VMEM((NF, 2, 3, NY, NZ), F32),
            pltpu.VMEM((2, NY, NZ), F32),
            dma((11,)),
        ], 2_000_000, 3_000_000,
    )(omegas, fields, sources, conductivity)
    upg_e = lax.ppermute(up_e, "brick", ring)
    dng_e = lax.ppermute(dn_e, "brick", back)
    upg_r = lax.ppermute(up_r, "brick", ring)
    dng_r = lax.ppermute(dn_r, "brick", back)
    part, slot, loc, edge, sig, own_r = call(
        main_kernel, "interior", [SMEM, SMEM, HBM, HBM, HBM, VMEM, VMEM, VMEM],
        [packed, jax.ShapeDtypeStruct((8, ROWS), I32), f32(ROWS, NZ), f32(12, 4, NY, NZ), f32(2, NY, NZ), pay],
        [
            pltpu.VMEM((NF, 2, 3, PL + 1, NY + PAD, NZ), F32),
            pltpu.VMEM((NF, 2, 3, PL, NY, NZ), F32),
            pltpu.VMEM((PL, NY, NZ), F32),
            pltpu.VMEM((12, PL + 1, NY + PAD, NZ), F32),
            pltpu.VMEM((8, PAD + NY, NZ), F32),
            pltpu.VMEM((4, NY, NZ), F32),
            dma((2 * PL + 1,)),
        ], 60_000_000, 8_000_000,
    )(
        omegas_in, tx_bricks, fields, sources, conductivity,
        row_brick.reshape(1, ROWS), row_offset, owner_map.reshape(1, DEV),
    )
    part, rest, fac = call(
        field_fix_kernel, "field_fix", [SMEM, SMEM] + [VMEM] * 10,
        [packed, f32(2, NY, NZ), f32(20, NY, NZ)], [pltpu.VMEM((2 * NY, NZ), F32)], 20_000_000, 4_000_000,
    )(omegas_in, tx_bricks, edge, sig, loc, up_e, dn_e, own_r, upg_e, dng_e, slot, part)
    (send,) = call(
        residual_fix_kernel, "residual_fix", [VMEM] * 6, [packed], [pltpu.VMEM((2 * NY, NZ), F32)], 20_000_000, 3_000_000,
    )(fac, rest, upg_r, dng_r, slot, part)
    got = lax.all_to_all(send.reshape(DEV, 1, SLOTS * NZ), ("tx", "brick"), 0, 0, tiled=True).reshape(DEV * SLOTS, NZ)
    return pl.pallas_call(
        owner_kernel,
        in_specs=[VMEM],
        out_specs=VMEM,
        out_shape=f32(G_DEV, NZ),
        compiler_params=pltpu.CompilerParams(vmem_limit_bytes=LIMIT),
        name="owner_sum",
    )(got)


def solution(mesh):
    return jax.shard_map(
        per_device,
        mesh=mesh,
        in_specs=(
            P("tx", None, None, None, "brick", None, None),
            P("tx", None, None, None, "brick", None, None),
            P("tx", "brick", None, None),
            P(),
            P(),
            P(),
            P("tx", "brick", None),
            P("tx", "brick"),
        ),
        out_specs=P(("tx", "brick"), None),
        check_vma=False,
    )
```

time: 718 us -> 45.8 us (0.06)
  waiting for transfers between devices: 654 us -> 0.01 us
  other arithmetic: 25.8 us -> 0 us
  blocking collectives: 0 us -> 20.8 us
  between operations: 14.5 us -> 0.08 us
  Pallas kernels: 0 us -> 12.7 us
  local copies, waits for them, and re-layouts: 12.5 us -> 0.02 us
    reduce_scatter x1 -> x0, waiting for transfers between devices: 644 us -> none  [per_device(): lax.psum_scatter(buffer, ('tx', 'brick'), scatter_dimension=0, tiled=True)]
    all_to_all x0 -> x1, blocking collectives: none -> 20.8 us  [per_device(): lax.all_to_all(send.reshape(DEV, 1, SLOTS * NZ), ('tx', 'brick'), 0, 0, t...]
    pallas_call x0 -> x5, Pallas kernels: none -> 12.7 us  [the longest x1 7.59 us: per_device(): call(main_kernel, 'interior', [SMEM, SMEM, HBM, HBM, HBM, VMEM, VMEM, VME...]
    ppermute x4, waiting for transfers between devices: 9.93 us -> 0.01 us  [the longest x1 0.01 us: per_device(): upg_e = lax.ppermute(up_e, 'brick', ring)]
    mul x9 -> x0, other arithmetic: 9.22 us -> none  [the longest x2 4.26 us: per_device(): efield = fields[0] * active]
    slice x18 -> x0, local copies, waits for them, and re-layouts: 8.07 us -> none  [the longest x1 4.01 us: apply_crop(): rotated = jnp.stack([-inner[:, 1], inner[:, 0]], axis=1)]
  transfers between devices with their start and end apart: 5 -> 4, of which waited for: 4 -> 0; matrix products, arithmetic and copies ran while one was open for 2% -> 0% of each run, Pallas kernels for 0% -> 21%
where the time goes in v2:
time: 45.8 us; the launch traced here: 45.5 us
  blocking collectives  20.8 us (45%)
  Pallas kernels  12.7 us (28%)
  starting transfers between devices  11.8 us (26%)
    all_to_all x1, blocking collectives, per_device(): lax.all_to_all(send.reshape(DEV, 1, SLOTS * NZ), ('tx', 'brick'), 0, 0, t...  20.8 us
    pallas_call x1, Pallas kernels, per_device(): call(main_kernel, 'interior', [SMEM, SMEM, HBM, HBM, HBM, VMEM, VMEM, VME...  7.59 us
    ppermute x1, starting transfers between devices, per_device(): dng_r = lax.ppermute(dn_r, 'brick', back)  5.34 us
    ppermute x1, starting transfers between devices, per_device(): dng_e = lax.ppermute(dn_e, 'brick', back)  4.4 us
    ppermute x1, starting transfers between devices, per_device(): upg_e = lax.ppermute(up_e, 'brick', ring)  2.07 us
    pallas_call x1, Pallas kernels, per_device(): call(halo_kernel, 'halo', [HBM] * 4, [pay] * 4, [pltpu.SMEM((NF,), F32),...  2.05 us
    pallas_call x1, Pallas kernels, per_device(): call(field_fix_kernel, 'field_fix', [SMEM, SMEM] + [VMEM] * 10, [packed,...  1.79 us
  transfers between devices with their start and end apart: 4, of which 0 were waited for; matrix products, arithmetic and copies ran while one was open for 0% of the time, Pallas kernels for 21%

profile of v2, /device:TPU:0, one launch (start us, length us, event | category | flops | bytes accessed | tf_op | source)
XLA Modules:
  0.0 45.5 jit_solution(7322089248658382061)
XLA Ops:
  0.0 0.0 copy-start
  0.0 0.0 copy-start.3
  0.0 0.0 copy-start.2
  0.0 0.0 copy-start.1
  0.0 0.0 copy-start.4
  0.0 2.1 %halo.1 = (f32[8,64,128]{2,1,0:T(8,128)S(1)}, f32[8,64,128]{2,1,0:T(8,128)S(1)}, f32[8,64,128]{2,1,0:T(8,128)S(1)}, f32[8,64,128]{2,1,0:T(8,128)S(1)}) custom-call(f32[2]{0:T(128)} %om_ref.3, f32[1,2,2,3,8,64,128]{6,5,4,3,2,1,0:T(8,128)} %e_hbm.3, f32[1,2,2,3,8,64,128]{6,5,4,3,2,1,0:T(8,128)} %s_hbm.3, f32[1,8,64,128]{3,2,1,0:T(8,128)} %c_hbm.3), custom_call_target="tpu_custom_call" | custom-call | flops 2000000 | bytes 3000000 | tf_op jit(solution)/shard_map/halo/pallas_call | solution.py:407
  2.1 2.1 %collective-permute-start = (f32[8,64,128]{2,1,0:T(8,128)S(1)}, f32[8,64,128]{2,1,0:T(8,128)S(1)}, u32[]{:S(2)}, u32[]{:S(2)}) collective-permute-start(f32[8,64,128]{2,1,0:T(8,128)S(1)} %get-tuple-element.21.ups_ref), channel_id=1, source_target_pairs={{0,1},{1,2},{2,3},{3,4},{4,5},{5,6},{6,7},{7,8},{8,9},{9,10},{10,1... | collective-permute-start | bytes 786440 | tf_op jit(solution)/shard_map/ppermute | solution.py:419
  4.1 4.4 %collective-permute-start.1 = (f32[8,64,128]{2,1,0:T(8,128)S(1)}, f32[8,64,128]{2,1,0:T(8,128)S(1)}, u32[]{:S(2)}, u32[]{:S(2)}) collective-permute-start(f32[8,64,128]{2,1,0:T(8,128)S(1)} %get-tuple-element.22.dns_ref), channel_id=1, source_target_pairs={{1,0},{2,1},{3,2},{4,3},{5,4},{6,5},{7,6},{8,7},{9,8},{10,9},{11,1... | collective-permute-start | bytes 786440 | tf_op jit(solution)/shard_map/ppermute | solution.py:420
  8.5 0.0 collective-permute-start.2
  8.5 5.3 %collective-permute-start.3 = (f32[8,64,128]{2,1,0:T(8,128)S(1)}, f32[8,64,128]{2,1,0:T(8,128)S(1)}, u32[]{:S(2)}, u32[]{:S(2)}) collective-permute-start(f32[8,64,128]{2,1,0:T(8,128)S(1)} %get-tuple-element.29), channel_id=1, source_target_pairs={{1,0},{2,1},{3,2},{4,3},{5,4},{6,5},{7,6},{8,7},{9,8},{10,9},{11,1... | collective-permute-start | bytes 786440 | tf_op jit(solution)/shard_map/ppermute | solution.py:422
  13.9 0.0 copy-done
  13.9 0.0 copy-done.3
  13.9 0.0 copy-done.2
  13.9 0.0 copy-done.1
  13.9 0.0 copy-done.4
  13.9 7.6 %interior.1 = (f32[1152,128]{1,0:T(8,128)S(1)}, s32[8,512]{1,0:T(8,128)S(1)}, f32[512,128]{1,0:T(8,128)S(1)}, f32[12,4,64,128]{3,2,1,0:T(8,128)S(1)}, f32[2,64,1...) custom-call(f32[2]{0:T(128)S(1)} %copy-done, s32[8]{0:T(128)S(1)} %copy-done.3, f32[1,2,2,3,8,64,128]{6,5,4,3,2,1,0:T(8,128)} %e_hbm.3, ...), custom_call_target="tpu_custom_call" | custom-call | flops 60000000 | bytes 8000000 | tf_op jit(solution)/shard_map/interior/pallas_call | solution.py:423
  21.5 0.0 collective-permute-done.upg_ref
  21.5 0.0 collective-permute-done.1.dng_ref
  21.5 1.8 %field_fix.1 = (f32[1152,128]{1,0:T(8,128)S(1)}, f32[2,64,128]{2,1,0:T(8,128)S(1)}, f32[20,64,128]{2,1,0:T(8,128)S(1)}) custom-call(f32[2]{0:T(128)S(1)} %copy-done, s32[8]{0:T(128)S(1)} %copy-done.3, f32[12,4,64,128]{3,2,1,0:T(8,128)S(1)} %get-tuple-element.18.edge_ref, f32[2,64,128]{2,1,0:T(8,128)S(1)} %get-tuple-element.19.sig_ref, ...), custom_call_target="tpu_custom_call" | custom-call | flops 20000000 | bytes 4000000 | tf_op jit(solution)/shard_map/field_fix/pallas_call | solution.py:439
  23.3 0.0 collective-permute-done.2.upg_ref
  23.3 0.0 collective-permute-done.3.dng_ref
  23.4 0.4 residual_fix.1
  23.8 20.8 %all_to_all.5 = f32[128,1,1152]{2,1,0:T(1,128)S(1)} all-to-all(f32[128,1,1152]{2,1,0:T(1,128)S(1)} %bitcast.5), channel_id=1, replica_groups=mesh['tx'=8,'brick'=16] {'tx','brick'}, dimensions={0} | all-to-all | bytes 1179648 | tf_op jit(solution)/shard_map/all_to_all | solution.py:446
  44.6 0.9 %owner_sum.1 = f32[32,128]{1,0:T(8,128)} custom-call(f32[1152,128]{1,0:T(8,128)S(1)} %bitcast.4), custom_call_target="tpu_custom_call" | custom-call | tf_op jit(solution)/shard_map/owner_sum/pallas_call | solution.py:447
Async XLA Ops:
  0.0 13.9 %copy-start = (f32[2]{0:T(128)S(1)}, f32[2]{0:T(128)}, u32[]{:S(2)}) copy-start(f32[2]{0:T(128)} %om_ref.3) | copy-start | bytes 28
  0.0 13.9 %copy-start.3 = (s32[8]{0:T(128)S(1)}, s32[8]{0:T(128)}, u32[]{:S(2)}) copy-start(s32[8]{0:T(128)} %tb_ref.3) | copy-start | bytes 100
  0.0 13.9 %copy-start.2 = (s32[1,512]{1,0:T(1,128)S(1)}, s32[1,512]{1,0:T(1,128)}, u32[]{:S(2)}) copy-start(s32[1,512]{1,0:T(1,128)} %ro_ref.1) | copy-start | bytes 6148
  0.0 13.9 %copy-start.1 = (s32[1,512,1]{1,2,0:T(1,128)S(1)}, s32[1,512,1]{1,2,0:T(1,128)}, u32[]{:S(2)}) copy-start(s32[1,512,1]{1,2,0:T(1,128)} %param.14) | copy-start | bytes 6148
  0.0 13.9 %copy-start.4 = (s32[128]{0:T(128)S(1)}, s32[128]{0:T(128)}, u32[]{:S(2)}) copy-start(s32[128]{0:T(128)} %param.13) | copy-start | bytes 1540
  2.1 19.4 %collective-permute-start = (f32[8,64,128]{2,1,0:T(8,128)S(1)}, f32[8,64,128]{2,1,0:T(8,128)S(1)}, u32[]{:S(2)}, u32[]{:S(2)}) collective-permute-start(f32[8,64,128]{2,1,0:T(8,128)S(1)} %get-tuple-element.21.ups_ref), channel_id=1, source_target_pairs={{0,1},{1,2},{2,3},{3,4},{4,5},{5,6},{6,7},{7,8},{8,9},{9,10},{10,1... | collective-permute-start | bytes 786440 | tf_op jit(solution)/shard_map/ppermute | solution.py:419
  4.1 17.4 %collective-permute-start.1 = (f32[8,64,128]{2,1,0:T(8,128)S(1)}, f32[8,64,128]{2,1,0:T(8,128)S(1)}, u32[]{:S(2)}, u32[]{:S(2)}) collective-permute-start(f32[8,64,128]{2,1,0:T(8,128)S(1)} %get-tuple-element.22.dns_ref), channel_id=1, source_target_pairs={{1,0},{2,1},{3,2},{4,3},{5,4},{6,5},{7,6},{8,7},{9,8},{10,9},{11,1... | collective-permute-start | bytes 786440 | tf_op jit(solution)/shard_map/ppermute | solution.py:420
  8.5 14.8 %collective-permute-start.2 = (f32[8,64,128]{2,1,0:T(8,128)S(1)}, f32[8,64,128]{2,1,0:T(8,128)S(1)}, u32[]{:S(2)}, u32[]{:S(2)}) collective-permute-start(f32[8,64,128]{2,1,0:T(8,128)S(1)} %get-tuple-element.28), channel_id=1, source_target_pairs={{0,1},{1,2},{2,3},{3,4},{4,5},{5,6},{6,7},{7,8},{8,9},{9,10},{10,1... | collective-permute-start | bytes 786440 | tf_op jit(solution)/shard_map/ppermute | solution.py:421
  8.5 14.8 %collective-permute-start.3 = (f32[8,64,128]{2,1,0:T(8,128)S(1)}, f32[8,64,128]{2,1,0:T(8,128)S(1)}, u32[]{:S(2)}, u32[]{:S(2)}) collective-permute-start(f32[8,64,128]{2,1,0:T(8,128)S(1)} %get-tuple-element.29), channel_id=1, source_target_pairs={{1,0},{2,1},{3,2},{4,3},{5,4},{6,5},{7,6},{8,7},{9,8},{10,9},{11,1... | collective-permute-start | bytes 786440 | tf_op jit(solution)/shard_map/ppermute | solution.py:422

commit v3 on v2

v3 whole, which is shorter than its diff:
```python
import jax
import jax.numpy as jnp
from jax import lax
from jax.experimental import pallas as pl
from jax.experimental.pallas import tpu as pltpu
from jax.sharding import Mesh, PartitionSpec as P

PL, NY, NZ, NF = 8, 64, 128, 2
ROWS = PL * NY
G_DEV = 32
CAP = 8
DEV = 128
SLOTS = CAP + 1
BRICK = 16
TX_AXES, BRICK_AXES = ("y", "core"), ("x", "z")
SWAP_AXES = ("core", "x", "z", "y")
PAD = 8
CH = 16
F32, BF16, I32 = jnp.float32, jnp.bfloat16, jnp.int32
SCALE = 0.003


def fy(v):
    rows = lax.broadcasted_iota(I32, v.shape, 0)
    return jnp.where(rows == NY - 1, 0.0, pltpu.roll(v, NY - 1, 0)) - v


def by(v):
    rows = lax.broadcasted_iota(I32, v.shape, 0)
    return v - jnp.where(rows == 0, 0.0, pltpu.roll(v, 1, 0))


def fz(v):
    lanes = lax.broadcasted_iota(I32, v.shape, 1)
    return jnp.where(lanes == NZ - 1, 0.0, pltpu.roll(v, NZ - 1, 1)) - v


def bz(v):
    lanes = lax.broadcasted_iota(I32, v.shape, 1)
    return v - jnp.where(lanes == 0, 0.0, pltpu.roll(v, 1, 1))


def q_of(vx, vy, vz):
    return fz(vx) + vz, vy + fy(vx)


def rotate(curl, part, weight, other):
    return curl - weight * other if part == 0 else curl + weight * other


def signed(part, value):
    return value if part == 1 else -value


def odd_brick():
    return (lax.axis_index(BRICK_AXES) & 1) == 1


def field_halo_kernel(e_hbm, one_ref, two_ref, lo_ref, hi_ref, sems):
    odd = odd_brick()
    lo = [pltpu.make_async_copy(e_hbm.at[0, f, :, pl.ds(1, 2), 0], lo_ref.at[f], sems.at[f]) for f in range(NF)]
    hi = [pltpu.make_async_copy(e_hbm.at[0, f, :, :, PL - 1], hi_ref.at[f], sems.at[NF + f]) for f in range(NF)]
    for f in range(NF):
        hi[f].start()
        lo[f].start()
    for f in range(NF):
        hi[f].wait()
        lo[f].wait()
        for part in range(2):
            q = q_of(*(hi_ref[f, part, c] for c in range(3)))
            for c in range(2):
                at = 2 * (2 * f + part) + c
                one_ref[at] = jnp.where(odd, q[c], lo_ref[f, part, c])
                two_ref[at] = jnp.where(odd, lo_ref[f, part, c], q[c])


def residual_halo_kernel(om_hbm, e_hbm, s_hbm, c_hbm, one_ref, two_ref, om_ref, elo_ref, ehi_ref, slo_ref, shi_ref, cc_ref, sems):
    odd = odd_brick()
    small = [
        pltpu.make_async_copy(om_hbm, om_ref, sems.at[8]),
        pltpu.make_async_copy(c_hbm.at[0, 0], cc_ref.at[0], sems.at[9]),
        pltpu.make_async_copy(c_hbm.at[0, PL - 1], cc_ref.at[1], sems.at[10]),
    ]
    big = [
        [
            pltpu.make_async_copy(e_hbm.at[0, f, :, :, pl.ds(0, 2)], elo_ref.at[f], sems.at[4 * f]),
            pltpu.make_async_copy(s_hbm.at[0, f, :, pl.ds(1, 2), 0], slo_ref.at[f], sems.at[4 * f + 1]),
            pltpu.make_async_copy(e_hbm.at[0, f, :, :, pl.ds(PL - 2, 2)], ehi_ref.at[f], sems.at[4 * f + 2]),
            pltpu.make_async_copy(s_hbm.at[0, f, :, :, PL - 1], shi_ref.at[f], sems.at[4 * f + 3]),
        ]
        for f in range(NF)
    ]
    for copy in small + big[0] + big[1]:
        copy.start()
    for copy in small:
        copy.wait()
    for f in range(NF):
        for copy in big[f]:
            copy.wait()
        om = om_ref[f]
        for part in range(2):
            ch = 2 * f + part
            vx, vy, vz = (elo_ref[f, part, c, 0] for c in range(3))
            hx = fy(vz) - fz(vy)
            hy = fz(vx) - (elo_ref[f, part, 2, 1] - vz)
            hz = (elo_ref[f, part, 1, 1] - vy) - fy(vx)
            w = om * cc_ref[0]
            dy = rotate(bz(hx) - hz, part, w, elo_ref[f, 1 - part, 1, 0]) - slo_ref[f, part, 0]
            dz = rotate(hy - by(hx), part, w, elo_ref[f, 1 - part, 2, 0]) - slo_ref[f, part, 1]
            ux, uy, uz = (ehi_ref[f, part, c, 0] for c in range(3))
            vx, vy, vz = (ehi_ref[f, part, c, 1] for c in range(3))
            hy, qz = q_of(vx, vy, vz)
            hz = -qz
            hx = fy(vz) - fz(vy)
            gy = fz(ux) - (vz - uz)
            gz = (vy - uy) - fy(ux)
            w = om * cc_ref[1]
            o = [ehi_ref[f, 1 - part, c, 1] for c in range(3)]
            rx = rotate(by(hz) - bz(hy), part, w, o[0]) - shi_ref[f, part, 0]
            ry = rotate(bz(hx) - (hz - gz), part, w, o[1]) - shi_ref[f, part, 1]
            rz = rotate((hy - gy) - by(hx), part, w, o[2]) - shi_ref[f, part, 2]
            sy, sz = q_of(rx, ry, rz)
            one_ref[2 * ch] = jnp.where(odd, sy, dy)
            one_ref[2 * ch + 1] = jnp.where(odd, sz, dz)
            two_ref[2 * ch] = jnp.where(odd, dy, sy)
            two_ref[2 * ch + 1] = jnp.where(odd, dz, sz)


def one_hot(cond):
    return jnp.where(cond, 1.0, 0.0).astype(BF16)


def dot(a, b):
    return jnp.dot(a, b, preferred_element_type=F32)


def pick(hot, v):
    hi = v.astype(BF16)
    low = (v - hi.astype(F32)).astype(BF16)
    both = dot(hot, jnp.concatenate([hi, low], axis=1))
    return both[:, 0:NZ] + both[:, NZ:2 * NZ]


def place(tb_ref):
    brick = lax.axis_index(BRICK_AXES)
    span = tb_ref[lax.axis_index(TX_AXES)]
    live = jnp.where(brick < span, 1.0, 0.0).astype(F32)
    low = jnp.where(brick > 0, 1.0, 0.0).astype(F32)
    nxt = jnp.where(brick + 1 < span, 1.0, 0.0).astype(F32)
    return live, low, nxt


def main_kernel(
    om_ref, tb_ref, e_ref, s_ref, c_ref, rb_ref, ro_ref, own_ref,
    part_ref, slot_ref, loc_ref, own_r_ref,
    r_ref, h_ref, g_ref,
):
    live, _, _ = place(tb_ref)
    zero = jnp.zeros((NY, NZ), F32)
    zpad = jnp.zeros((PAD, NZ), F32)
    for i in range(12):
        r_ref[i, PL, 0:NY] = zero
        for p in range(PL):
            r_ref[i, p, NY:NY + PAD] = zpad
    for i in range(8):
        h_ref[i, 0:PAD] = zpad
        h_ref[i, PAD:PAD + NY] = zero
    for i in range(4):
        g_ref[i] = zero

    bt = lax.broadcasted_iota(I32, (DEV, ROWS), 0) == rb_ref[...]
    hot = one_hot(bt)
    before = one_hot(lax.broadcasted_iota(I32, (ROWS, ROWS), 0) < lax.broadcasted_iota(I32, (ROWS, ROWS), 1))
    counts = dot(hot, before)
    rank = jnp.sum(jnp.where(bt, counts, 0.0), axis=0, keepdims=True)
    own8 = jnp.broadcast_to(own_ref[...].astype(F32), (8, DEV)).astype(BF16)
    dest = dot(own8, hot)[0:1].astype(I32)
    dest = ((dest >> 4) & 1) * 64 + ((dest >> 2) & 3) * 16 + (dest & 3) * 4 + (dest >> 5)
    rank = rank.astype(I32)
    slot = dest * SLOTS + rank
    slot_ref[...] = jnp.broadcast_to(slot, (8, ROWS))
    codes = jnp.where(lax.broadcasted_iota(I32, (NZ, ROWS), 0) == rank, (ro_ref[...] + 1).astype(F32), 0.0).astype(BF16)
    mine = one_hot(lax.broadcasted_iota(I32, (DEV, ROWS), 0) == dest)
    index = lax.dot_general(mine, codes, (((1,), (1,)), ((), ())), preferred_element_type=F32)

    def curl(get, p, y, ch):
        lanes = lax.broadcasted_iota(I32, (CH, NZ), 1)

        def nz_(v):
            return jnp.where(lanes == NZ - 1, 0.0, pltpu.roll(v, NZ - 1, 1))

        def pz_(v):
            return jnp.where(lanes == 0, 0.0, pltpu.roll(v, 1, 1))

        vx, vy, vz = (get(c, p, y) for c in range(3))
        hx = (get(2, p, y + 1) - vz) - (nz_(vy) - vy)
        hy = (nz_(vx) - vx) - (get(2, p + 1, y) - vz)
        hz = (get(1, p + 1, y) - vy) - (get(0, p, y + 1) - vx)
        gy = g_ref[ch, y:y + CH]
        gz = h_ref[2 * ch + 1, PAD + y:PAD + y + CH]
        h_ref[2 * ch, PAD + y:PAD + y + CH] = hx
        h_ref[2 * ch + 1, PAD + y:PAD + y + CH] = hz
        g_ref[ch, y:y + CH] = hy
        hxp = h_ref[2 * ch, PAD + y - 1:PAD + y - 1 + CH]
        hzp = h_ref[2 * ch + 1, PAD + y - 1:PAD + y - 1 + CH]
        cx = (hz - hzp) - (hy - pz_(hy))
        cy = (hx - pz_(hx)) - (hz - gz)
        cz = (hy - gy) - (hx - hxp)
        return (vx, vy, vz), (cx, cy, cz)

    rows = lax.broadcasted_iota(I32, (CH, NZ), 0)

    def first(p, carry):
        after = jnp.minimum(p + 1, PL - 1)
        inside = jnp.where(p < PL - 1, 1.0, 0.0).astype(F32)
        for y in range(0, NY, CH):
            sig = c_ref[0, p, y:y + CH]
            for f in range(NF):
                w = om_ref[f] * sig
                for part in range(2):

                    def get(c, q, r):
                        if q is not p:
                            return e_ref[0, f, part, c, after, r:r + CH] * inside
                        if r + CH <= NY:
                            return e_ref[0, f, part, c, p, r:r + CH]
                        last = e_ref[0, f, part, c, p, NY - CH:NY]
                        return jnp.where(rows == CH - 1, 0.0, pltpu.roll(last, CH - 1, 0))

                    _, cs = curl(get, p, y, 2 * f + part)
                    for c in range(3):
                        o = e_ref[0, f, 1 - part, c, p, y:y + CH]
                        r_ref[3 * (2 * f + part) + c, p, y:y + CH] = rotate(cs[c], part, w, o) - s_ref[0, f, part, c, p, y:y + CH]
        return carry

    lax.fori_loop(0, PL, first, 0)
    for i in range(4):
        h_ref[2 * i + 1, PAD:PAD + NY] = zero
        g_ref[i] = zero

    def second(p, carry):
        for y in range(0, NY, CH):
            sig = c_ref[0, p, y:y + CH]
            acc = jnp.zeros((CH, NZ), F32)
            for f in range(NF):
                om = om_ref[f]
                tot = jnp.zeros((CH, NZ), F32)
                dia = jnp.zeros((CH, NZ), F32)
                for part in range(2):
                    ch = 2 * f + part
                    vs, cs = curl(lambda c, q, r: r_ref[3 * ch + c, q, r:r + CH], p, y, ch)
                    o = [e_ref[0, f, 1 - part, c, p, y:y + CH] for c in range(3)]
                    s = [e_ref[0, f, part, c, p, y:y + CH] for c in range(3)]
                    tot = tot + signed(part, o[0] * cs[0] + o[1] * cs[1] + o[2] * cs[2])
                    dia = dia + (s[0] * vs[0] + s[1] * vs[1] + s[2] * vs[2])
                acc = acc + (SCALE * om * live) * (tot + (om * sig) * dia)
            loc_ref[pl.ds(pl.multiple_of(p * NY + y, CH), CH), :] = acc
        return carry

    lax.fori_loop(0, PL, second, 0)

    for ch in range(4):
        own_r_ref[2 * ch] = r_ref[3 * ch + 1, 0, 0:NY]
        own_r_ref[2 * ch + 1] = r_ref[3 * ch + 2, 0, 0:NY]
    lo, hi = 2 * NY, ROWS - 2 * NY
    at = lax.broadcasted_iota(I32, (DEV * SLOTS, hi - lo), 0)
    part_ref[...] = pick(one_hot(at == slot[:, lo:hi]), loc_ref[lo:hi])
    part_ref[pl.ds(CAP, DEV, stride=SLOTS), :] = index


def field_fix_kernel(
    om_ref, tb_ref, e_ref, c_ref, loc_ref, one_ref, two_ref, dnr_ref, gone_ref, gtwo_ref, slot_ref, part_ref,
    out_ref, rest_ref, fac_ref, rows_ref,
):
    odd = odd_brick()
    live, low, nxt = place(tb_ref)
    zero = jnp.zeros((NY, NZ), F32)
    acc = [zero] * 4
    for f in range(NF):
        om = om_ref[f]
        weight = SCALE * om * live
        tot = [zero] * 4
        dia = [zero, zero]
        for part in range(2):
            ch = 2 * f + part
            y, z = 2 * ch, 2 * ch + 1

            def add(which, terms):
                tot[which] = tot[which] + signed(part, terms)

            ey, ez = e_ref[0, f, part, 1, 0], e_ref[0, f, part, 2, 0]
            qy = jnp.where(odd, gtwo_ref[y], gone_ref[y])
            qz = jnp.where(odd, gtwo_ref[z], gone_ref[z])
            dry = low * (ey - qz)
            drz = low * (ez - qy)
            ry, rz = dnr_ref[y] + dry, dnr_ref[z] + drz
            div = by(ey) + bz(ez)
            gy = low * (fz(div) - ez - rz)
            gz = low * (ry - fy(div) + ey)
            hx = fy(drz) - fz(dry)
            ax = -(by(dry) + bz(drz))
            ay = bz(hx) + dry + gz
            az = drz - by(hx) - gy
            o = [e_ref[0, f, 1 - part, c, 0] for c in range(3)]
            add(0, o[0] * ax + o[1] * ay + o[2] * az)
            dia[0] = dia[0] + (ey * dry + ez * drz)
            add(1, -(e_ref[0, f, 1 - part, 1, 1] * dry + e_ref[0, f, 1 - part, 2, 1] * drz))
            scale = signed(part, weight) * low
            fac_ref[2 * ch] = -scale * o[2]
            fac_ref[2 * ch + 1] = -scale * o[1]

            ey = nxt * jnp.where(odd, gone_ref[y], gtwo_ref[y])
            ez = nxt * jnp.where(odd, gone_ref[z], gtwo_ref[z])
            qy = jnp.where(odd, one_ref[y], two_ref[y])
            qz = jnp.where(odd, one_ref[z], two_ref[z])
            dx = by(ey) + bz(ez)
            ry = nxt * (ey - qz)
            rz = nxt * (ez - qy)
            hx = fz(ey) - fy(ez)
            hy = fz(dx) - (rz + ez)
            hz = (ry + ey) - fy(dx)
            ax = by(hz) - bz(hy)
            ay = bz(hx) - (hz + ey)
            az = (hy - ez) - by(hx)
            o = [e_ref[0, f, 1 - part, c, PL - 1] for c in range(3)]
            s = [e_ref[0, f, part, c, PL - 1] for c in range(3)]
            add(3, o[0] * ax + o[1] * ay + o[2] * az)
            dia[1] = dia[1] + (s[0] * dx - s[1] * ey - s[2] * ez)
            scale = signed(part, weight) * nxt
            for c in range(3):
                fac_ref[8 + 3 * ch + c] = scale * o[c]
            o = [e_ref[0, f, 1 - part, c, PL - 2] for c in range(3)]
            add(2, o[1] * ey + o[2] * ez - o[0] * dx)
        acc[0] = acc[0] + weight * (tot[0] + (om * c_ref[0, 0]) * dia[0])
        acc[1] = acc[1] + weight * tot[1]
        acc[2] = acc[2] + weight * tot[2]
        acc[3] = acc[3] + weight * (tot[3] + (om * c_ref[0, PL - 1]) * dia[1])
    rest_ref[0] = loc_ref[0:NY] + acc[0]
    rest_ref[1] = loc_ref[ROWS - NY:ROWS] + acc[3]
    rows_ref[0:NY] = loc_ref[NY:2 * NY] + acc[1]
    rows_ref[NY:2 * NY] = loc_ref[ROWS - 2 * NY:ROWS - NY] + acc[2]
    at = lax.broadcasted_iota(I32, (DEV * SLOTS, NY), 0)
    hot = jnp.concatenate(
        [one_hot(at == slot_ref[0:1, NY:2 * NY]), one_hot(at == slot_ref[0:1, ROWS - 2 * NY:ROWS - NY])], axis=1
    )
    out_ref[...] = part_ref[...] + pick(hot, rows_ref[...])


def residual_fix_kernel(fac_ref, rest_ref, gone_ref, gtwo_ref, slot_ref, part_ref, out_ref, two_ref):
    odd = odd_brick()
    low, high = rest_ref[0], rest_ref[1]
    for ch in range(4):
        first = [gone_ref[2 * ch + c] for c in range(2)]
        second = [gtwo_ref[2 * ch + c] for c in range(2)]
        qy, qz = (jnp.where(odd, second[c], first[c]) for c in range(2))
        ry, rz = (jnp.where(odd, first[c], second[c]) for c in range(2))
        low = low + (fac_ref[2 * ch] * qy + fac_ref[2 * ch + 1] * qz)
        o = [fac_ref[8 + 3 * ch + c] for c in range(3)]
        high = high + (o[0] * (by(ry) + bz(rz)) - o[1] * ry - o[2] * rz)
    two_ref[0:NY] = low
    two_ref[NY:2 * NY] = high
    at = lax.broadcasted_iota(I32, (DEV * SLOTS, NY), 0)
    hot = jnp.concatenate([one_hot(at == slot_ref[0:1, 0:NY]), one_hot(at == slot_ref[0:1, ROWS - NY:ROWS])], axis=1)
    out_ref[...] = part_ref[...] + pick(hot, two_ref[...])


def owner_kernel(got_ref, out_ref):
    codes = got_ref[pl.ds(CAP, DEV, stride=SLOTS), :]
    offs = codes.T[0:CAP].astype(I32)
    want = lax.broadcasted_iota(I32, (G_DEV, DEV), 0) + 1
    hot = jnp.concatenate([one_hot(want == offs[k:k + 1]) for k in range(CAP)], axis=1)
    out_ref[...] = pick(hot, jnp.concatenate([got_ref[pl.ds(k, DEV, stride=SLOTS), :] for k in range(CAP)], axis=0))


SMEM = pl.BlockSpec(memory_space=pltpu.SMEM)
VMEM = pl.BlockSpec(memory_space=pltpu.VMEM)
HBM = pl.BlockSpec(memory_space=pltpu.HBM)
LIMIT = 40 * 1024 * 1024


def f32(*shape):
    return jax.ShapeDtypeStruct(shape, F32)


def call(kernel, name, ins, outs, scratch, flops, moved):
    return pl.pallas_call(
        kernel,
        in_specs=ins,
        out_specs=[VMEM] * len(outs),
        out_shape=outs,
        scratch_shapes=scratch,
        compiler_params=pltpu.CompilerParams(vmem_limit_bytes=LIMIT),
        cost_estimate=pl.CostEstimate(flops=flops, bytes_accessed=moved, transcendentals=0),
        name=name,
    )


def per_device(fields, sources, conductivity, omegas, tx_bricks, owner_map, row_brick, row_offset):
    fields_in, sources_in, conductivity_in, omegas_in = fields, sources, conductivity, omegas
    fields, sources, conductivity, omegas = (
        pltpu.with_memory_space_constraint(x, pltpu.HBM) for x in (fields, sources, conductivity, omegas)
    )
    with_next = [(i, (i + 1) % BRICK) for i in range(1, BRICK, 2)]
    with_last = [(i, i + 1) for i in range(0, BRICK, 2)]
    with_next, with_last = (pairs + [(b, a) for a, b in pairs] for pairs in (with_next, with_last))
    pay = f32(8, NY, NZ)
    packed = f32(DEV * SLOTS, NZ)
    dma = pltpu.SemaphoreType.DMA
    one_e, two_e = call(
        field_halo_kernel, "field_halo", [HBM], [pay, pay],
        [pltpu.VMEM((NF, 2, 2, NY, NZ), F32), pltpu.VMEM((NF, 2, 3, NY, NZ), F32), dma((2 * NF,))], 400_000, 1_200_000,
    )(fields)
    gone_e = lax.ppermute(one_e, BRICK_AXES, with_next)
    gtwo_e = lax.ppermute(two_e, BRICK_AXES, with_last)
    one_r, two_r = call(
        residual_halo_kernel, "residual_halo", [HBM] * 4, [pay, pay],
        [
            pltpu.SMEM((NF,), F32),
            pltpu.VMEM((NF, 2, 3, 2, NY, NZ), F32),
            pltpu.VMEM((NF, 2, 3, 2, NY, NZ), F32),
            pltpu.VMEM((NF, 2, 2, NY, NZ), F32),
            pltpu.VMEM((NF, 2, 3, NY, NZ), F32),
            pltpu.VMEM((2, NY, NZ), F32),
            dma((11,)),
        ], 2_000_000, 3_000_000,
    )(omegas, fields, sources, conductivity)
    gone_r = lax.ppermute(one_r, BRICK_AXES, with_next)
    gtwo_r = lax.ppermute(two_r, BRICK_AXES, with_last)
    fields_v, sources_v, conductivity_v, _ = lax.optimization_barrier((fields_in, sources_in, conductivity_in, two_r))
    fields_v, sources_v, conductivity_v = (
        pltpu.with_memory_space_constraint(x, pltpu.VMEM) for x in (fields_v, sources_v, conductivity_v)
    )
    part, slot, loc, own_r = call(
        main_kernel, "interior", [SMEM, SMEM] + [VMEM] * 6,
        [packed, jax.ShapeDtypeStruct((8, ROWS), I32), f32(ROWS, NZ), pay],
        [
            pltpu.VMEM((12, PL + 1, NY + PAD, NZ), F32),
            pltpu.VMEM((8, PAD + NY, NZ), F32),
            pltpu.VMEM((4, NY, NZ), F32),
        ], 60_000_000, 8_000_000,
    )(
        omegas_in, tx_bricks, fields_v, sources_v, conductivity_v,
        row_brick.reshape(1, ROWS), row_offset, owner_map.reshape(1, DEV),
    )
    part, rest, fac = call(
        field_fix_kernel, "field_fix", [SMEM, SMEM] + [VMEM] * 10,
        [packed, f32(2, NY, NZ), f32(20, NY, NZ)], [pltpu.VMEM((2 * NY, NZ), F32)], 20_000_000, 4_000_000,
    )(omegas_in, tx_bricks, fields_v, conductivity_v, loc, one_e, two_e, own_r, gone_e, gtwo_e, slot, part)
    (send,) = call(
        residual_fix_kernel, "residual_fix", [VMEM] * 6, [packed], [pltpu.VMEM((2 * NY, NZ), F32)], 20_000_000, 3_000_000,
    )(fac, rest, gone_r, gtwo_r, slot, part)
    got = lax.all_to_all(send.reshape(DEV, 1, SLOTS * NZ), SWAP_AXES, 0, 0, tiled=True).reshape(DEV * SLOTS, NZ)
    return pl.pallas_call(
        owner_kernel,
        in_specs=[VMEM],
        out_specs=VMEM,
        out_shape=f32(G_DEV, NZ),
        compiler_params=pltpu.CompilerParams(vmem_limit_bytes=LIMIT),
        name="owner_sum",
    )(got)


def solution(mesh):
    grid = Mesh(mesh.devices.reshape(4, 2, 4, 4), ("y", "core", "x", "z"))
    return jax.shard_map(
        per_device,
        mesh=grid,
        in_specs=(
            P(TX_AXES, None, None, None, BRICK_AXES, None, None),
            P(TX_AXES, None, None, None, BRICK_AXES, None, None),
            P(TX_AXES, BRICK_AXES, None, None),
            P(),
            P(),
            P(),
            P(TX_AXES, BRICK_AXES, None),
            P(TX_AXES, BRICK_AXES),
        ),
        out_specs=P(TX_AXES + BRICK_AXES, None),
        check_vma=False,
    )
```

time: 45.8 us -> 45.3 us (0.989)
  starting transfers between devices: 11.8 us -> 8.52 us
  blocking collectives: 20.8 us -> 22.1 us
  waiting for transfers between devices: 0.01 us -> 0.78 us
    ppermute x4, starting transfers between devices: 11.8 us -> 8.52 us  [the longest x1 6.39 us: per_device(): gone_e = lax.ppermute(one_e, BRICK_AXES, with_next)]
    all_to_all x1, blocking collectives: 20.8 us -> 22.1 us  [per_device(): lax.all_to_all(send.reshape(DEV, 1, SLOTS * NZ), SWAP_AXES, 0, 0, tiled=T...]
    ppermute x4, waiting for transfers between devices: 0.01 us -> 0.78 us  [the longest x1 0.74 us: per_device(): gone_r = lax.ppermute(one_r, BRICK_AXES, with_next)]
    pallas_call x2 -> x3, Pallas kernels: 9.65 us -> 9.92 us  [the longest x1 6.47 us: per_device(): call(main_kernel, 'interior', [SMEM, SMEM] + [VMEM] * 6, [packed, jax.Sha...]
  transfers between devices with their start and end apart: 4 -> 4, of which waited for: 0 -> 1; matrix products, arithmetic and copies ran while one was open for 0% -> 0% of each run, Pallas kernels for 21% -> 23%
where the time goes in v3:
time: 45.3 us; the launch traced here: 44.6 us
  blocking collectives  22.1 us (49%)
  Pallas kernels  13 us (29%)
  starting transfers between devices  8.52 us (19%)
  waiting for transfers between devices  0.78 us (2%)
    all_to_all x1, blocking collectives, per_device(): lax.all_to_all(send.reshape(DEV, 1, SLOTS * NZ), SWAP_AXES, 0, 0, tiled=T...  22.1 us
    pallas_call x1, Pallas kernels, per_device(): call(main_kernel, 'interior', [SMEM, SMEM] + [VMEM] * 6, [packed, jax.Sha...  6.47 us
    ppermute x1, starting transfers between devices, per_device(): gone_e = lax.ppermute(one_e, BRICK_AXES, with_next)  6.39 us
    pallas_call x1, Pallas kernels, per_device(): call(residual_halo_kernel, 'residual_halo', [HBM] * 4, [pay, pay], [pltpu...  2.16 us
    pallas_call x1, Pallas kernels, per_device(): call(field_fix_kernel, 'field_fix', [SMEM, SMEM] + [VMEM] * 10, [packed,...  1.83 us
    ppermute x1, starting transfers between devices, per_device(): gtwo_r = lax.ppermute(two_r, BRICK_AXES, with_last)  1.31 us
    pallas_call x1, Pallas kernels, per_device(): call(field_halo_kernel, 'field_halo', [HBM], [pay, pay], [pltpu.VMEM((NF,...  1.29 us
  transfers between devices with their start and end apart: 4, of which 1 were waited for; matrix products, arithmetic and copies ran while one was open for 0% of the time, Pallas kernels for 23%

profile of v3, /device:TPU:0, one launch (start us, length us, event | category | flops | bytes accessed | tf_op | source)
XLA Modules:
  0.0 44.6 jit_solution(8596933192454497247)
XLA Ops:
  0.0 1.3 %field_halo.1 = (f32[8,64,128]{2,1,0:T(8,128)S(1)}, f32[8,64,128]{2,1,0:T(8,128)S(1)}) custom-call(f32[1,2,2,3,8,64,128]{6,5,4,3,2,1,0:T(8,128)} %e_ref.1), custom_call_target="tpu_custom_call" | custom-call | flops 400000 | bytes 1200000 | tf_op jit(solution)/shard_map/field_halo/pallas_call | solution.py:409
  1.3 6.4 %collective-permute-start = (f32[8,64,128]{2,1,0:T(8,128)S(1)}, f32[8,64,128]{2,1,0:T(8,128)S(1)}, u32[]{:S(2)}, u32[]{:S(2)}) collective-permute-start(f32[8,64,128]{2,1,0:T(8,128)S(1)} %get-tuple-element.24.one_ref), channel_id=1, source_target_pairs={{1,2},{3,4},{5,6},{7,8},{9,10},{11,12},{13,14},{15,0},{2,1},{4,3},... | collective-permute-start | bytes 786440 | tf_op jit(solution)/shard_map/ppermute | solution.py:413
  7.7 0.0 copy-start
  7.7 0.0 copy-start.1
  7.7 0.0 copy-start.2
  7.7 0.0 copy-start.3
  7.7 0.0 copy-start.4
  7.7 0.0 copy-start.5
  7.7 0.0 copy-start.6
  7.7 0.0 copy-start.7
  7.7 0.1 collective-permute-start.1
  7.8 2.2 %residual_halo.1 = (f32[8,64,128]{2,1,0:T(8,128)S(1)}, f32[8,64,128]{2,1,0:T(8,128)S(1)}) custom-call(f32[2]{0:T(128)} %om_ref.3, f32[1,2,2,3,8,64,128]{6,5,4,3,2,1,0:T(8,128)} %e_ref.1, f32[1,2,2,3,8,64,128]{6,5,4,3,2,1,0:T(8,128)} %s_ref, f32[1,8,64,128]{3,2,1,0:T(8,128)} %c_ref.1), custom_call_target="tpu_custom_call" | custom-call | flops 2000000 | bytes 3000000 | tf_op jit(solution)/shard_map/residual_halo/pallas_call | solution.py:415
  10.0 0.7 %collective-permute-start.2 = (f32[8,64,128]{2,1,0:T(8,128)S(1)}, f32[8,64,128]{2,1,0:T(8,128)S(1)}, u32[]{:S(2)}, u32[]{:S(2)}) collective-permute-start(f32[8,64,128]{2,1,0:T(8,128)S(1)} %get-tuple-element.31), channel_id=1, source_target_pairs={{1,2},{3,4},{5,6},{7,8},{9,10},{11,12},{13,14},{15,0},{2,1},{4,3},... | collective-permute-start | bytes 786440 | tf_op jit(solution)/shard_map/ppermute | solution.py:427
  10.7 1.3 %collective-permute-start.3 = (f32[8,64,128]{2,1,0:T(8,128)S(1)}, f32[8,64,128]{2,1,0:T(8,128)S(1)}, u32[]{:S(2)}, u32[]{:S(2)}) collective-permute-start(f32[8,64,128]{2,1,0:T(8,128)S(1)} %get-tuple-element.19), channel_id=1, source_target_pairs={{0,1},{2,3},{4,5},{6,7},{8,9},{10,11},{12,13},{14,15},{1,0},{3,2},... | collective-permute-start | bytes 786440 | tf_op jit(solution)/shard_map/ppermute | solution.py:428
  12.0 0.0 copy-done
  12.0 0.0 copy-done.1
  12.1 0.0 copy-done.2
  12.1 0.0 copy-done.3
  12.1 0.0 copy-done.4
  12.1 0.0 copy-done.5
  12.1 0.0 copy-done.6
  12.1 0.0 copy-done.7
  12.1 6.5 %interior.1 = (f32[1152,128]{1,0:T(8,128)S(1)}, s32[8,512]{1,0:T(8,128)S(1)}, f32[512,128]{1,0:T(8,128)S(1)}, f32[8,64,128]{2,1,0:T(8,128)S(1)}) custom-call(f32[2]{0:T(128)S(1)} %copy-done.3, s32[8]{0:T(128)S(1)} %copy-done.6, f32[1,2,2,3,8,64,128]{6,5,4,3,2,1,0:T(8,128)S(1)} %copy-done, f32[1,2,2,3,8,64,128]{6,5,4,3,2,1,0:T(8,128)S(1)} %copy-done.1, ...), custom_call_target="tpu_custom_call" | custom-call | flops 60000000 | bytes 8000000 | tf_op jit(solution)/shard_map/interior/pallas_call | solution.py:433
  18.6 0.0 collective-permute-done.gone_ref
  18.6 0.0 collective-permute-done.1.gtwo_ref
  18.6 1.8 %field_fix.1 = (f32[1152,128]{1,0:T(8,128)S(1)}, f32[2,64,128]{2,1,0:T(8,128)S(1)}, f32[20,64,128]{2,1,0:T(8,128)S(1)}) custom-call(f32[2]{0:T(128)S(1)} %copy-done.3, s32[8]{0:T(128)S(1)} %copy-done.6, f32[1,2,2,3,8,64,128]{6,5,4,3,2,1,0:T(8,128)S(1)} %copy-done, f32[1,8,64,128]{3,2,1,0:T(8,128)S(1)} %copy-done.2, ...), custom_call_target="tpu_custom_call" | custom-call | flops 20000000 | bytes 4000000 | tf_op jit(solution)/shard_map/field_fix/pallas_call | solution.py:445
  20.4 0.7 %collective-permute-done.2.gone_ref = f32[8,64,128]{2,1,0:T(8,128)S(1)} collective-permute-done((f32[8,64,128]{2,1,0:T(8,128)S(1)}, f32[8,64,128]{2,1,0:T(8,128)S(1)}, u32[]{:S(2)}, u32[]{:S(2)}) %collective-permute-start.2) | collective-permute-done | bytes 262176 | tf_op jit(solution)/shard_map/ppermute | solution.py:427
  21.2 0.0 collective-permute-done.3.gtwo_ref
  21.2 0.4 residual_fix.1
  21.7 22.1 %all_to_all.5 = f32[128,1,1152]{2,1,0:T(1,128)S(1)} all-to-all(f32[128,1,1152]{2,1,0:T(1,128)S(1)} %bitcast.5), channel_id=1, replica_groups=mesh['y'=4,'core'=2,'x'=4,'z'=4] {'core','x','z','y'}, dimensions={0} | all-to-all | bytes 1179648 | tf_op jit(solution)/shard_map/all_to_all | solution.py:452
  43.8 0.8 %owner_sum.1 = f32[32,128]{1,0:T(8,128)} custom-call(f32[1152,128]{1,0:T(8,128)S(1)} %bitcast.4), custom_call_target="tpu_custom_call" | custom-call | tf_op jit(solution)/shard_map/owner_sum/pallas_call | solution.py:453
Async XLA Ops:
  1.3 17.3 %collective-permute-start = (f32[8,64,128]{2,1,0:T(8,128)S(1)}, f32[8,64,128]{2,1,0:T(8,128)S(1)}, u32[]{:S(2)}, u32[]{:S(2)}) collective-permute-start(f32[8,64,128]{2,1,0:T(8,128)S(1)} %get-tuple-element.24.one_ref), channel_id=1, source_target_pairs={{1,2},{3,4},{5,6},{7,8},{9,10},{11,12},{13,14},{15,0},{2,1},{4,3},... | collective-permute-start | bytes 786440 | tf_op jit(solution)/shard_map/ppermute | solution.py:413
  7.7 4.4 %copy-start = (f32[1,2,2,3,8,64,128]{6,5,4,3,2,1,0:T(8,128)S(1)}, f32[1,2,2,3,8,64,128]{6,5,4,3,2,1,0:T(8,128)}, u32[]{:S(2)}) copy-start(f32[1,2,2,3,8,64,128]{6,5,4,3,2,1,0:T(8,128)} %e_ref.1) | copy-start | bytes 9437188
  7.7 4.4 %copy-start.1 = (f32[1,2,2,3,8,64,128]{6,5,4,3,2,1,0:T(8,128)S(1)}, f32[1,2,2,3,8,64,128]{6,5,4,3,2,1,0:T(8,128)}, u32[]{:S(2)}) copy-start(f32[1,2,2,3,8,64,128]{6,5,4,3,2,1,0:T(8,128)} %s_ref) | copy-start | bytes 9437188
  7.7 4.4 %copy-start.2 = (f32[1,8,64,128]{3,2,1,0:T(8,128)S(1)}, f32[1,8,64,128]{3,2,1,0:T(8,128)}, u32[]{:S(2)}) copy-start(f32[1,8,64,128]{3,2,1,0:T(8,128)} %c_ref.1) | copy-start | bytes 786436
  7.7 4.4 %copy-start.3 = (f32[2]{0:T(128)S(1)}, f32[2]{0:T(128)}, u32[]{:S(2)}) copy-start(f32[2]{0:T(128)} %om_ref.3) | copy-start | bytes 28
  7.7 4.4 %copy-start.4 = (s32[1,512,1]{1,2,0:T(1,128)S(1)}, s32[1,512,1]{1,2,0:T(1,128)}, u32[]{:S(2)}) copy-start(s32[1,512,1]{1,2,0:T(1,128)} %param.14) | copy-start | bytes 6148
  7.7 4.4 %copy-start.5 = (s32[1,512]{1,0:T(1,128)S(1)}, s32[1,512]{1,0:T(1,128)}, u32[]{:S(2)}) copy-start(s32[1,512]{1,0:T(1,128)} %ro_ref.1) | copy-start | bytes 6148
  7.7 4.4 %copy-start.6 = (s32[8]{0:T(128)S(1)}, s32[8]{0:T(128)}, u32[]{:S(2)}) copy-start(s32[8]{0:T(128)} %tb_ref.3) | copy-start | bytes 100
  7.7 4.4 %copy-start.7 = (s32[128]{0:T(128)S(1)}, s32[128]{0:T(128)}, u32[]{:S(2)}) copy-start(s32[128]{0:T(128)} %param.13) | copy-start | bytes 1540
  7.7 10.8 %collective-permute-start.1 = (f32[8,64,128]{2,1,0:T(8,128)S(1)}, f32[8,64,128]{2,1,0:T(8,128)S(1)}, u32[]{:S(2)}, u32[]{:S(2)}) collective-permute-start(f32[8,64,128]{2,1,0:T(8,128)S(1)} %get-tuple-element.25.two_ref), channel_id=1, source_target_pairs={{0,1},{2,3},{4,5},{6,7},{8,9},{10,11},{12,13},{14,15},{1,0},{3,2},... | collective-permute-start | bytes 786440 | tf_op jit(solution)/shard_map/ppermute | solution.py:414
  10.0 11.2 %collective-permute-start.2 = (f32[8,64,128]{2,1,0:T(8,128)S(1)}, f32[8,64,128]{2,1,0:T(8,128)S(1)}, u32[]{:S(2)}, u32[]{:S(2)}) collective-permute-start(f32[8,64,128]{2,1,0:T(8,128)S(1)} %get-tuple-element.31), channel_id=1, source_target_pairs={{1,2},{3,4},{5,6},{7,8},{9,10},{11,12},{13,14},{15,0},{2,1},{4,3},... | collective-permute-start | bytes 786440 | tf_op jit(solution)/shard_map/ppermute | solution.py:427
  10.7 10.5 %collective-permute-start.3 = (f32[8,64,128]{2,1,0:T(8,128)S(1)}, f32[8,64,128]{2,1,0:T(8,128)S(1)}, u32[]{:S(2)}, u32[]{:S(2)}) collective-permute-start(f32[8,64,128]{2,1,0:T(8,128)S(1)} %get-tuple-element.19), channel_id=1, source_target_pairs={{0,1},{2,3},{4,5},{6,7},{8,9},{10,11},{12,13},{14,15},{1,0},{3,2},... | collective-permute-start | bytes 786440 | tf_op jit(solution)/shard_map/ppermute | solution.py:428

commit v4 on v3

--- a/solution.py
+++ b/solution.py
@@ -150,16 +150,36 @@
     return live, low, nxt
 
 
-def main_kernel(
-    om_ref, tb_ref, e_ref, s_ref, c_ref, rb_ref, ro_ref, own_ref,
-    part_ref, slot_ref, loc_ref, own_r_ref,
-    r_ref, h_ref, g_ref,
-):
-    live, _, _ = place(tb_ref)
+def curl(get, h_ref, g_ref, p, y, ch):
+    lanes = lax.broadcasted_iota(I32, (CH, NZ), 1)
+
+    def nz_(v):
+        return jnp.where(lanes == NZ - 1, 0.0, pltpu.roll(v, NZ - 1, 1))
+
+    def pz_(v):
+        return jnp.where(lanes == 0, 0.0, pltpu.roll(v, 1, 1))
+
+    vx, vy, vz = (get(c, p, y) for c in range(3))
+    hx = (get(2, p, y + 1) - vz) - (nz_(vy) - vy)
+    hy = (nz_(vx) - vx) - (get(2, p + 1, y) - vz)
+    hz = (get(1, p + 1, y) - vy) - (get(0, p, y + 1) - vx)
+    gy = g_ref[ch, y:y + CH]
+    gz = h_ref[2 * ch + 1, PAD + y:PAD + y + CH]
+    h_ref[2 * ch, PAD + y:PAD + y + CH] = hx
+    h_ref[2 * ch + 1, PAD + y:PAD + y + CH] = hz
+    g_ref[ch, y:y + CH] = hy
+    hxp = h_ref[2 * ch, PAD + y - 1:PAD + y - 1 + CH]
+    hzp = h_ref[2 * ch + 1, PAD + y - 1:PAD + y - 1 + CH]
+    cx = (hz - hzp) - (hy - pz_(hy))
+    cy = (hx - pz_(hx)) - (hz - gz)
+    cz = (hy - gy) - (hx - hxp)
+    return (vx, vy, vz), (cx, cy, cz)
+
+
+def residual_kernel(om_ref, e_ref, s_ref, c_ref, rb_ref, ro_ref, own_ref, r_ref, slot_ref, index_ref, h_ref, g_ref):
     zero = jnp.zeros((NY, NZ), F32)
     zpad = jnp.zeros((PAD, NZ), F32)
     for i in range(12):
-        r_ref[i, PL, 0:NY] = zero
         for p in range(PL):
             r_ref[i, p, NY:NY + PAD] = zpad
     for i in range(8):
@@ -181,36 +201,11 @@
     slot_ref[...] = jnp.broadcast_to(slot, (8, ROWS))
     codes = jnp.where(lax.broadcasted_iota(I32, (NZ, ROWS), 0) == rank, (ro_ref[...] + 1).astype(F32), 0.0).astype(BF16)
     mine = one_hot(lax.broadcasted_iota(I32, (DEV, ROWS), 0) == dest)
-    index = lax.dot_general(mine, codes, (((1,), (1,)), ((), ())), preferred_element_type=F32)
-
-    def curl(get, p, y, ch):
-        lanes = lax.broadcasted_iota(I32, (CH, NZ), 1)
-
-        def nz_(v):
-            return jnp.where(lanes == NZ - 1, 0.0, pltpu.roll(v, NZ - 1, 1))
-
-        def pz_(v):
-            return jnp.where(lanes == 0, 0.0, pltpu.roll(v, 1, 1))
-
-        vx, vy, vz = (get(c, p, y) for c in range(3))
-        hx = (get(2, p, y + 1) - vz) - (nz_(vy) - vy)
-        hy = (nz_(vx) - vx) - (get(2, p + 1, y) - vz)
-        hz = (get(1, p + 1, y) - vy) - (get(0, p, y + 1) - vx)
-        gy = g_ref[ch, y:y + CH]
-        gz = h_ref[2 * ch + 1, PAD + y:PAD + y + CH]
-        h_ref[2 * ch, PAD + y:PAD + y + CH] = hx
-        h_ref[2 * ch + 1, PAD + y:PAD + y + CH] = hz
-        g_ref[ch, y:y + CH] = hy
-        hxp = h_ref[2 * ch, PAD + y - 1:PAD + y - 1 + CH]
-        hzp = h_ref[2 * ch + 1, PAD + y - 1:PAD + y - 1 + CH]
-        cx = (hz - hzp) - (hy - pz_(hy))
-        cy = (hx - pz_(hx)) - (hz - gz)
-        cz = (hy - gy) - (hx - hxp)
-        return (vx, vy, vz), (cx, cy, cz)
+    index_ref[...] = lax.dot_general(mine, codes, (((1,), (1,)), ((), ())), preferred_element_type=F32)
 
     rows = lax.broadcasted_iota(I32, (CH, NZ), 0)
 
-    def first(p, carry):
+    def step(p, carry):
         after = jnp.minimum(p + 1, PL - 1)
         inside = jnp.where(p < PL - 1, 1.0, 0.0).astype(F32)
         for y in range(0, NY, CH):
@@ -218,6 +213,7 @@
             for f in range(NF):
                 w = om_ref[f] * sig
                 for part in range(2):
+                    ch = 2 * f + part
 
                     def get(c, q, r):
                         if q is not p:
@@ -227,18 +223,58 @@
                         last = e_ref[0, f, part, c, p, NY - CH:NY]
                         return jnp.where(rows == CH - 1, 0.0, pltpu.roll(last, CH - 1, 0))
 
-                    _, cs = curl(get, p, y, 2 * f + part)
+                    _, cs = curl(get, h_ref, g_ref, p, y, ch)
                     for c in range(3):
                         o = e_ref[0, f, 1 - part, c, p, y:y + CH]
-                        r_ref[3 * (2 * f + part) + c, p, y:y + CH] = rotate(cs[c], part, w, o) - s_ref[0, f, part, c, p, y:y + CH]
+                        r_ref[3 * ch + c, p, y:y + CH] = rotate(cs[c], part, w, o) - s_ref[0, f, part, c, p, y:y + CH]
         return carry
 
-    lax.fori_loop(0, PL, first, 0)
-    for i in range(4):
-        h_ref[2 * i + 1, PAD:PAD + NY] = zero
-        g_ref[i] = zero
-
-    def second(p, carry):
+    lax.fori_loop(0, PL, step, 0)
+    for ch in range(4):
+        r_ref[3 * ch + 1, PL, 0:NY] = h_ref[2 * ch + 1, PAD:PAD + NY]
+        r_ref[3 * ch + 2, PL, 0:NY] = -g_ref[ch]
+
+
+def adjoint_kernel(
+    om_ref, tb_ref, e_ref, c_ref, slot_ref, index_ref, gone_ref, gtwo_ref, rin_ref,
+    part_ref, rest_ref, fac_ref, r_ref, h_ref, g_ref, loc_ref,
+):
+    live, low, nxt = place(tb_ref)
+    odd = odd_brick()
+    end = PL - 1
+    zpad = jnp.zeros((PAD, NZ), F32)
+    for i in range(8):
+        h_ref[i, 0:PAD] = zpad
+    for f in range(NF):
+        weight = SCALE * om_ref[f] * live
+        for part in range(2):
+            ch = 2 * f + part
+            x, y, z = 3 * ch, 3 * ch + 1, 3 * ch + 2
+            ey, ez = e_ref[0, f, part, 1, 0], e_ref[0, f, part, 2, 0]
+            first = [gone_ref[2 * ch + c] for c in range(2)]
+            second = [gtwo_ref[2 * ch + c] for c in range(2)]
+            qy, qz = (jnp.where(odd, second[c], first[c]) for c in range(2))
+            ry = rin_ref[y, 0, 0:NY] + low * (ey - qz)
+            rz = rin_ref[z, 0, 0:NY] + low * (ez - qy)
+            r_ref[y, 0, 0:NY] = ry
+            r_ref[z, 0, 0:NY] = rz
+            div = by(ey) + bz(ez)
+            g_ref[ch] = low * (fz(div) - ez - rz)
+            h_ref[2 * ch + 1, PAD:PAD + NY] = low * (ry - fy(div) + ey)
+            ey, ez = (nxt * jnp.where(odd, first[c], second[c]) for c in range(2))
+            r_ref[x, end, 0:NY] = rin_ref[x, end, 0:NY] + (by(ey) + bz(ez))
+            r_ref[y, end, 0:NY] = rin_ref[y, end, 0:NY] - ey
+            r_ref[z, end, 0:NY] = rin_ref[z, end, 0:NY] - ez
+            r_ref[y, PL, 0:NY] = nxt * rin_ref[y, PL, 0:NY] + ey
+            r_ref[z, PL, 0:NY] = nxt * rin_ref[z, PL, 0:NY] + ez
+            scale = -signed(part, weight) * low
+            fac_ref[2 * ch] = scale * e_ref[0, f, 1 - part, 2, 0]
+            fac_ref[2 * ch + 1] = scale * e_ref[0, f, 1 - part, 1, 0]
+            scale = signed(part, weight) * nxt
+            for c in range(3):
+                fac_ref[8 + 3 * ch + c] = scale * e_ref[0, f, 1 - part, c, end]
+
+    def step(p, carry):
         for y in range(0, NY, CH):
             sig = c_ref[0, p, y:y + CH]
             acc = jnp.zeros((CH, NZ), F32)
@@ -248,7 +284,7 @@
                 dia = jnp.zeros((CH, NZ), F32)
                 for part in range(2):
                     ch = 2 * f + part
-                    vs, cs = curl(lambda c, q, r: r_ref[3 * ch + c, q, r:r + CH], p, y, ch)
+                    vs, cs = curl(lambda c, q, r: r_ref[3 * ch + c, q, r:r + CH], h_ref, g_ref, p, y, ch)
                     o = [e_ref[0, f, 1 - part, c, p, y:y + CH] for c in range(3)]
                     s = [e_ref[0, f, part, c, p, y:y + CH] for c in range(3)]
                     tot = tot + signed(part, o[0] * cs[0] + o[1] * cs[1] + o[2] * cs[2])
@@ -257,93 +293,14 @@
             loc_ref[pl.ds(pl.multiple_of(p * NY + y, CH), CH), :] = acc
         return carry
 
-    lax.fori_loop(0, PL, second, 0)
-
-    for ch in range(4):
-        own_r_ref[2 * ch] = r_ref[3 * ch + 1, 0, 0:NY]
-        own_r_ref[2 * ch + 1] = r_ref[3 * ch + 2, 0, 0:NY]
-    lo, hi = 2 * NY, ROWS - 2 * NY
+    lax.fori_loop(0, PL, step, 0)
+
+    rest_ref[0] = loc_ref[0:NY]
+    rest_ref[1] = loc_ref[ROWS - NY:ROWS]
+    lo, hi = NY, ROWS - NY
     at = lax.broadcasted_iota(I32, (DEV * SLOTS, hi - lo), 0)
-    part_ref[...] = pick(one_hot(at == slot[:, lo:hi]), loc_ref[lo:hi])
-    part_ref[pl.ds(CAP, DEV, stride=SLOTS), :] = index
-
-
-def field_fix_kernel(
-    om_ref, tb_ref, e_ref, c_ref, loc_ref, one_ref, two_ref, dnr_ref, gone_ref, gtwo_ref, slot_ref, part_ref,
-    out_ref, rest_ref, fac_ref, rows_ref,
-):
-    odd = odd_brick()
-    live, low, nxt = place(tb_ref)
-    zero = jnp.zeros((NY, NZ), F32)
-    acc = [zero] * 4
-    for f in range(NF):
-        om = om_ref[f]
-        weight = SCALE * om * live
-        tot = [zero] * 4
-        dia = [zero, zero]
-        for part in range(2):
-            ch = 2 * f + part
-            y, z = 2 * ch, 2 * ch + 1
-
-            def add(which, terms):
-                tot[which] = tot[which] + signed(part, terms)
-
-            ey, ez = e_ref[0, f, part, 1, 0], e_ref[0, f, part, 2, 0]
-            qy = jnp.where(odd, gtwo_ref[y], gone_ref[y])
-            qz = jnp.where(odd, gtwo_ref[z], gone_ref[z])
-            dry = low * (ey - qz)
-            drz = low * (ez - qy)
-            ry, rz = dnr_ref[y] + dry, dnr_ref[z] + drz
-            div = by(ey) + bz(ez)
-            gy = low * (fz(div) - ez - rz)
-            gz = low * (ry - fy(div) + ey)
-            hx = fy(drz) - fz(dry)
-            ax = -(by(dry) + bz(drz))
-            ay = bz(hx) + dry + gz
-            az = drz - by(hx) - gy
-            o = [e_ref[0, f, 1 - part, c, 0] for c in range(3)]
-            add(0, o[0] * ax + o[1] * ay + o[2] * az)
-            dia[0] = dia[0] + (ey * dry + ez * drz)
-            add(1, -(e_ref[0, f, 1 - part, 1, 1] * dry + e_ref[0, f, 1 - part, 2, 1] * drz))
-            scale = signed(part, weight) * low
-            fac_ref[2 * ch] = -scale * o[2]
-            fac_ref[2 * ch + 1] = -scale * o[1]
-
-            ey = nxt * jnp.where(odd, gone_ref[y], gtwo_ref[y])
-            ez = nxt * jnp.where(odd, gone_ref[z], gtwo_ref[z])
-            qy = jnp.where(odd, one_ref[y], two_ref[y])
-            qz = jnp.where(odd, one_ref[z], two_ref[z])
-            dx = by(ey) + bz(ez)
-            ry = nxt * (ey - qz)
-            rz = nxt * (ez - qy)
-            hx = fz(ey) - fy(ez)
-            hy = fz(dx) - (rz + ez)
-            hz = (ry + ey) - fy(dx)
-            ax = by(hz) - bz(hy)
-            ay = bz(hx) - (hz + ey)
-            az = (hy - ez) - by(hx)
-            o = [e_ref[0, f, 1 - part, c, PL - 1] for c in range(3)]
-            s = [e_ref[0, f, part, c, PL - 1] for c in range(3)]
-            add(3, o[0] * ax + o[1] * ay + o[2] * az)
-            dia[1] = dia[1] + (s[0] * dx - s[1] * ey - s[2] * ez)
-            scale = signed(part, weight) * nxt
-            for c in range(3):
-                fac_ref[8 + 3 * ch + c] = scale * o[c]
-            o = [e_ref[0, f, 1 - part, c, PL - 2] for c in range(3)]
-            add(2, o[1] * ey + o[2] * ez - o[0] * dx)
-        acc[0] = acc[0] + weight * (tot[0] + (om * c_ref[0, 0]) * dia[0])
-        acc[1] = acc[1] + weight * tot[1]
-        acc[2] = acc[2] + weight * tot[2]
-        acc[3] = acc[3] + weight * (tot[3] + (om * c_ref[0, PL - 1]) * dia[1])
-    rest_ref[0] = loc_ref[0:NY] + acc[0]
-    rest_ref[1] = loc_ref[ROWS - NY:ROWS] + acc[3]
-    rows_ref[0:NY] = loc_ref[NY:2 * NY] + acc[1]
-    rows_ref[NY:2 * NY] = loc_ref[ROWS - 2 * NY:ROWS - NY] + acc[2]
-    at = lax.broadcasted_iota(I32, (DEV * SLOTS, NY), 0)
-    hot = jnp.concatenate(
-        [one_hot(at == slot_ref[0:1, NY:2 * NY]), one_hot(at == slot_ref[0:1, ROWS - 2 * NY:ROWS - NY])], axis=1
-    )
-    out_ref[...] = part_ref[...] + pick(hot, rows_ref[...])
+    part_ref[...] = pick(one_hot(at == slot_ref[0:1, lo:hi]), loc_ref[lo:hi])
+    part_ref[pl.ds(CAP, DEV, stride=SLOTS), :] = index_ref[...]
 
 
 def residual_fix_kernel(fac_ref, rest_ref, gone_ref, gtwo_ref, slot_ref, part_ref, out_ref, two_ref):
@@ -430,22 +387,26 @@
     fields_v, sources_v, conductivity_v = (
         pltpu.with_memory_space_constraint(x, pltpu.VMEM) for x in (fields_v, sources_v, conductivity_v)
     )
-    part, slot, loc, own_r = call(
-        main_kernel, "interior", [SMEM, SMEM] + [VMEM] * 6,
-        [packed, jax.ShapeDtypeStruct((8, ROWS), I32), f32(ROWS, NZ), pay],
-        [
-            pltpu.VMEM((12, PL + 1, NY + PAD, NZ), F32),
-            pltpu.VMEM((8, PAD + NY, NZ), F32),
-            pltpu.VMEM((4, NY, NZ), F32),
-        ], 60_000_000, 8_000_000,
+    halo = [pltpu.VMEM((8, PAD + NY, NZ), F32), pltpu.VMEM((4, NY, NZ), F32)]
+    r, slot, index = call(
+        residual_kernel, "residual", [SMEM] + [VMEM] * 6,
+        [f32(12, PL + 1, NY + PAD, NZ), jax.ShapeDtypeStruct((8, ROWS), I32), f32(DEV, NZ)],
+        halo, 30_000_000, 8_000_000,
     )(
-        omegas_in, tx_bricks, fields_v, sources_v, conductivity_v,
+        omegas_in, fields_v, sources_v, conductivity_v,
         row_brick.reshape(1, ROWS), row_offset, owner_map.reshape(1, DEV),
     )
-    part, rest, fac = call(
-        field_fix_kernel, "field_fix", [SMEM, SMEM] + [VMEM] * 10,
-        [packed, f32(2, NY, NZ), f32(20, NY, NZ)], [pltpu.VMEM((2 * NY, NZ), F32)], 20_000_000, 4_000_000,
-    )(omegas_in, tx_bricks, fields_v, conductivity_v, loc, one_e, two_e, own_r, gone_e, gtwo_e, slot, part)
+    part, rest, fac, _ = pl.pallas_call(
+        adjoint_kernel,
+        in_specs=[SMEM, SMEM] + [VMEM] * 7,
+        out_specs=[VMEM] * 4,
+        out_shape=[packed, f32(2, NY, NZ), f32(20, NY, NZ), f32(12, PL + 1, NY + PAD, NZ)],
+        input_output_aliases={8: 3},
+        scratch_shapes=halo + [pltpu.VMEM((ROWS, NZ), F32)],
+        compiler_params=pltpu.CompilerParams(vmem_limit_bytes=LIMIT),
+        cost_estimate=pl.CostEstimate(flops=40_000_000, bytes_accessed=8_000_000, transcendentals=0),
+        name="adjoint",
+    )(omegas_in, tx_bricks, fields_v, conductivity_v, slot, index, gone_e, gtwo_e, r)
     (send,) = call(
         residual_fix_kernel, "residual_fix", [VMEM] * 6, [packed], [pltpu.VMEM((2 * NY, NZ), F32)], 20_000_000, 3_000_000,
     )(fac, rest, gone_r, gtwo_r, slot, part)

time: 45.3 us -> 44.8 us (0.989)
  Pallas kernels: 13 us -> 11.9 us
  waiting for transfers between devices: 0.78 us -> 1.75 us
  blocking collectives: 22.1 us -> 21.6 us
    ppermute x1, waiting for transfers between devices: 0.01 us -> 1.46 us  [per_device(): gtwo_e = lax.ppermute(two_e, BRICK_AXES, with_last)]
    pallas_call x2, Pallas kernels: 8.3 us -> 7.34 us  [the longest x1 3.85 us: per_device(): pl.pallas_call(adjoint_kernel, in_specs=[SMEM, SMEM] + [VMEM] * 7, out_sp...]
    ppermute x1, waiting for transfers between devices: 0.74 us -> 0.11 us  [per_device(): gone_r = lax.ppermute(one_r, BRICK_AXES, with_next)]
    all_to_all x1, blocking collectives: 22.1 us -> 21.6 us  [per_device(): lax.all_to_all(send.reshape(DEV, 1, SLOTS * NZ), SWAP_AXES, 0, 0, tiled=T...]
  transfers between devices with their start and end apart: 4 -> 4, of which waited for: 1 -> 3; matrix products, arithmetic and copies ran while one was open for 0% -> 0% of each run, Pallas kernels for 23% -> 21%
where the time goes in v4:
time: 44.8 us; the launch traced here: 44.1 us
  blocking collectives  21.6 us (48%)
  Pallas kernels  11.9 us (27%)
  starting transfers between devices  8.59 us (19%)
  waiting for transfers between devices  1.75 us (4%)
    all_to_all x1, blocking collectives, per_device(): lax.all_to_all(send.reshape(DEV, 1, SLOTS * NZ), SWAP_AXES, 0, 0, tiled=T...  21.6 us
    ppermute x1, starting transfers between devices, per_device(): gone_e = lax.ppermute(one_e, BRICK_AXES, with_next)  6.39 us
    pallas_call x1, Pallas kernels, per_device(): pl.pallas_call(adjoint_kernel, in_specs=[SMEM, SMEM] + [VMEM] * 7, out_sp...  3.85 us
    pallas_call x1, Pallas kernels, per_device(): call(residual_kernel, 'residual', [SMEM] + [VMEM] * 6, [f32(12, PL + 1, N...  3.48 us
    pallas_call x1, Pallas kernels, per_device(): call(residual_halo_kernel, 'residual_halo', [HBM] * 4, [pay, pay], [pltpu...  2.01 us
    ppermute x1, waiting for transfers between devices, per_device(): gtwo_e = lax.ppermute(two_e, BRICK_AXES, with_last)  1.46 us
    ppermute x1, starting transfers between devices, per_device(): gtwo_r = lax.ppermute(two_r, BRICK_AXES, with_last)  1.29 us
    pallas_call x1, Pallas kernels, per_device(): call(field_halo_kernel, 'field_halo', [HBM], [pay, pay], [pltpu.VMEM((NF,...  1.29 us
  transfers between devices with their start and end apart: 4, of which 3 were waited for; matrix products, arithmetic and copies ran while one was open for 0% of the time, Pallas kernels for 21%

profile of v4, /device:TPU:0, one launch (start us, length us, event | category | flops | bytes accessed | tf_op | source)
XLA Modules:
  0.0 44.1 jit_solution(7297539309486530948)
XLA Ops:
  0.0 1.3 %field_halo.1 = (f32[8,64,128]{2,1,0:T(8,128)S(1)}, f32[8,64,128]{2,1,0:T(8,128)S(1)}) custom-call(f32[1,2,2,3,8,64,128]{6,5,4,3,2,1,0:T(8,128)} %e_ref.1), custom_call_target="tpu_custom_call" | custom-call | flops 400000 | bytes 1200000 | tf_op jit(solution)/shard_map/field_halo/pallas_call | solution.py:366
  1.3 0.0 copy-start
  1.3 0.0 copy-start.1
  1.3 0.0 copy-start.2
  1.3 0.0 copy-start.3
  1.3 0.0 copy-start.4
  1.4 0.0 copy-start.5
  1.4 0.0 copy-start.6
  1.4 6.4 %collective-permute-start = (f32[8,64,128]{2,1,0:T(8,128)S(1)}, f32[8,64,128]{2,1,0:T(8,128)S(1)}, u32[]{:S(2)}, u32[]{:S(2)}) collective-permute-start(f32[8,64,128]{2,1,0:T(8,128)S(1)} %get-tuple-element.24), channel_id=1, source_target_pairs={{1,2},{3,4},{5,6},{7,8},{9,10},{11,12},{13,14},{15,0},{2,1},{4,3},... | collective-permute-start | bytes 786440 | tf_op jit(solution)/shard_map/ppermute | solution.py:370
  7.8 0.0 collective-permute-start.1
  7.8 2.0 %residual_halo.1 = (f32[8,64,128]{2,1,0:T(8,128)S(1)}, f32[8,64,128]{2,1,0:T(8,128)S(1)}) custom-call(f32[2]{0:T(128)} %om_ref.3, f32[1,2,2,3,8,64,128]{6,5,4,3,2,1,0:T(8,128)} %e_ref.1, f32[1,2,2,3,8,64,128]{6,5,4,3,2,1,0:T(8,128)} %s_ref, f32[1,8,64,128]{3,2,1,0:T(8,128)} %c_ref.1), custom_call_target="tpu_custom_call" | custom-call | flops 2000000 | bytes 3000000 | tf_op jit(solution)/shard_map/residual_halo/pallas_call | solution.py:372
  9.8 0.0 copy-start.7
  9.8 0.9 %collective-permute-start.2 = (f32[8,64,128]{2,1,0:T(8,128)S(1)}, f32[8,64,128]{2,1,0:T(8,128)S(1)}, u32[]{:S(2)}, u32[]{:S(2)}) collective-permute-start(f32[8,64,128]{2,1,0:T(8,128)S(1)} %get-tuple-element.29), channel_id=1, source_target_pairs={{1,2},{3,4},{5,6},{7,8},{9,10},{11,12},{13,14},{15,0},{2,1},{4,3},... | collective-permute-start | bytes 786440 | tf_op jit(solution)/shard_map/ppermute | solution.py:384
  10.7 1.3 %collective-permute-start.3 = (f32[8,64,128]{2,1,0:T(8,128)S(1)}, f32[8,64,128]{2,1,0:T(8,128)S(1)}, u32[]{:S(2)}, u32[]{:S(2)}) collective-permute-start(f32[8,64,128]{2,1,0:T(8,128)S(1)} %get-tuple-element.18), channel_id=1, source_target_pairs={{0,1},{2,3},{4,5},{6,7},{8,9},{10,11},{12,13},{14,15},{1,0},{3,2},... | collective-permute-start | bytes 786440 | tf_op jit(solution)/shard_map/ppermute | solution.py:385
  12.0 0.0 copy-done
  12.0 0.0 copy-done.1
  12.0 0.0 copy-done.2
  12.0 0.0 copy-done.3
  12.0 0.0 copy-done.4
  12.0 0.0 copy-done.5
  12.0 0.0 copy-done.6
  12.0 3.5 %residual.1 = (f32[12,9,72,128]{3,2,1,0:T(8,128)S(1)}, s32[8,512]{1,0:T(8,128)S(1)}, f32[128,128]{1,0:T(8,128)S(1)}) custom-call(f32[2]{0:T(128)S(1)} %copy-done.3, f32[1,2,2,3,8,64,128]{6,5,4,3,2,1,0:T(8,128)S(1)} %copy-done, f32[1,2,2,3,8,64,128]{6,5,4,3,2,1,0:T(8,128)S(1)} %copy-done.1, f32[1,8,64,128]{3,2,1,0:T(8,128)S(1)} %copy-done.2, ...), custom_call_target="tpu_custom_call" | custom-call | flops 30000000 | bytes 8000000 | tf_op jit(solution)/shard_map/residual/pallas_call | solution.py:391
  15.5 0.0 collective-permute-done.gone_ref
  15.5 1.5 %collective-permute-done.1.gtwo_ref = f32[8,64,128]{2,1,0:T(8,128)S(1)} collective-permute-done((f32[8,64,128]{2,1,0:T(8,128)S(1)}, f32[8,64,128]{2,1,0:T(8,128)S(1)}, u32[]{:S(2)}, u32[]{:S(2)}) %collective-permute-start.1) | collective-permute-done | bytes 262176 | tf_op jit(solution)/shard_map/ppermute | solution.py:371
  17.0 0.0 copy-done.7
  17.0 3.9 %adjoint.1 = (f32[1152,128]{1,0:T(8,128)S(1)}, f32[2,64,128]{2,1,0:T(8,128)S(1)}, f32[20,64,128]{2,1,0:T(8,128)S(1)}, f32[12,9,72,128]{3,2,1,0:T(8,128)S(1)}) custom-call(f32[2]{0:T(128)S(1)} %copy-done.3, s32[8]{0:T(128)S(1)} %copy-done.7, f32[1,2,2,3,8,64,128]{6,5,4,3,2,1,0:T(8,128)S(1)} %copy-done, ...), custom_call_target="tpu_custom_call", output_to_operand_aliasing={{3}: (8, {})} | custom-call | flops 40000000 | bytes 8000000 | tf_op jit(solution)/shard_map/adjoint/pallas_call | solution.py:399
  20.9 0.1 collective-permute-done.2.gone_ref
  21.0 0.2 collective-permute-done.3.gtwo_ref
  21.2 0.4 residual_fix.1
  21.6 21.6 %all_to_all.5 = f32[128,1,1152]{2,1,0:T(1,128)S(1)} all-to-all(f32[128,1,1152]{2,1,0:T(1,128)S(1)} %bitcast.5), channel_id=1, replica_groups=mesh['y'=4,'core'=2,'x'=4,'z'=4] {'core','x','z','y'}, dimensions={0} | all-to-all | bytes 1179648 | tf_op jit(solution)/shard_map/all_to_all | solution.py:413
  43.2 0.8 %owner_sum.1 = f32[32,128]{1,0:T(8,128)} custom-call(f32[1152,128]{1,0:T(8,128)S(1)} %bitcast.4), custom_call_target="tpu_custom_call" | custom-call | tf_op jit(solution)/shard_map/owner_sum/pallas_call | solution.py:414
Async XLA Ops:
  1.3 10.7 %copy-start = (f32[1,2,2,3,8,64,128]{6,5,4,3,2,1,0:T(8,128)S(1)}, f32[1,2,2,3,8,64,128]{6,5,4,3,2,1,0:T(8,128)}, u32[]{:S(2)}) copy-start(f32[1,2,2,3,8,64,128]{6,5,4,3,2,1,0:T(8,128)} %e_ref.1) | copy-start | bytes 9437188
  1.3 10.7 %copy-start.1 = (f32[1,2,2,3,8,64,128]{6,5,4,3,2,1,0:T(8,128)S(1)}, f32[1,2,2,3,8,64,128]{6,5,4,3,2,1,0:T(8,128)}, u32[]{:S(2)}) copy-start(f32[1,2,2,3,8,64,128]{6,5,4,3,2,1,0:T(8,128)} %s_ref) | copy-start | bytes 9437188
  1.3 10.7 %copy-start.2 = (f32[1,8,64,128]{3,2,1,0:T(8,128)S(1)}, f32[1,8,64,128]{3,2,1,0:T(8,128)}, u32[]{:S(2)}) copy-start(f32[1,8,64,128]{3,2,1,0:T(8,128)} %c_ref.1) | copy-start | bytes 786436
  1.3 10.7 %copy-start.3 = (f32[2]{0:T(128)S(1)}, f32[2]{0:T(128)}, u32[]{:S(2)}) copy-start(f32[2]{0:T(128)} %om_ref.3) | copy-start | bytes 28
  1.3 10.7 %copy-start.4 = (s32[1,512,1]{1,2,0:T(1,128)S(1)}, s32[1,512,1]{1,2,0:T(1,128)}, u32[]{:S(2)}) copy-start(s32[1,512,1]{1,2,0:T(1,128)} %param.14) | copy-start | bytes 6148
  1.4 10.7 %copy-start.5 = (s32[1,512]{1,0:T(1,128)S(1)}, s32[1,512]{1,0:T(1,128)}, u32[]{:S(2)}) copy-start(s32[1,512]{1,0:T(1,128)} %ro_ref.1) | copy-start | bytes 6148
  1.4 10.7 %copy-start.6 = (s32[128]{0:T(128)S(1)}, s32[128]{0:T(128)}, u32[]{:S(2)}) copy-start(s32[128]{0:T(128)} %param.13) | copy-start | bytes 1540
  1.4 14.2 %collective-permute-start = (f32[8,64,128]{2,1,0:T(8,128)S(1)}, f32[8,64,128]{2,1,0:T(8,128)S(1)}, u32[]{:S(2)}, u32[]{:S(2)}) collective-permute-start(f32[8,64,128]{2,1,0:T(8,128)S(1)} %get-tuple-element.24), channel_id=1, source_target_pairs={{1,2},{3,4},{5,6},{7,8},{9,10},{11,12},{13,14},{15,0},{2,1},{4,3},... | collective-permute-start | bytes 786440 | tf_op jit(solution)/shard_map/ppermute | solution.py:370
  7.8 9.2 %collective-permute-start.1 = (f32[8,64,128]{2,1,0:T(8,128)S(1)}, f32[8,64,128]{2,1,0:T(8,128)S(1)}, u32[]{:S(2)}, u32[]{:S(2)}) collective-permute-start(f32[8,64,128]{2,1,0:T(8,128)S(1)} %get-tuple-element.25), channel_id=1, source_target_pairs={{0,1},{2,3},{4,5},{6,7},{8,9},{10,11},{12,13},{14,15},{1,0},{3,2},... | collective-permute-start | bytes 786440 | tf_op jit(solution)/shard_map/ppermute | solution.py:371
  9.8 7.2 %copy-start.7 = (s32[8]{0:T(128)S(1)}, s32[8]{0:T(128)}, u32[]{:S(2)}) copy-start(s32[8]{0:T(128)} %tb_ref.1) | copy-start | bytes 100
  9.8 11.2 %collective-permute-start.2 = (f32[8,64,128]{2,1,0:T(8,128)S(1)}, f32[8,64,128]{2,1,0:T(8,128)S(1)}, u32[]{:S(2)}, u32[]{:S(2)}) collective-permute-start(f32[8,64,128]{2,1,0:T(8,128)S(1)} %get-tuple-element.29), channel_id=1, source_target_pairs={{1,2},{3,4},{5,6},{7,8},{9,10},{11,12},{13,14},{15,0},{2,1},{4,3},... | collective-permute-start | bytes 786440 | tf_op jit(solution)/shard_map/ppermute | solution.py:384
  10.7 10.4 %collective-permute-start.3 = (f32[8,64,128]{2,1,0:T(8,128)S(1)}, f32[8,64,128]{2,1,0:T(8,128)S(1)}, u32[]{:S(2)}, u32[]{:S(2)}) collective-permute-start(f32[8,64,128]{2,1,0:T(8,128)S(1)} %get-tuple-element.18), channel_id=1, source_target_pairs={{0,1},{2,3},{4,5},{6,7},{8,9},{10,11},{12,13},{14,15},{1,0},{3,2},... | collective-permute-start | bytes 786440 | tf_op jit(solution)/shard_map/ppermute | solution.py:385

commit v5 on v4

--- a/solution.py
+++ b/solution.py
@@ -13,7 +13,7 @@
 SLOTS = CAP + 1
 BRICK = 16
 TX_AXES, BRICK_AXES = ("y", "core"), ("x", "z")
-SWAP_AXES = ("core", "x", "z", "y")
+SWAP_AXES = ("core", "y", "x", "z")
 PAD = 8
 CH = 16
 F32, BF16, I32 = jnp.float32, jnp.bfloat16, jnp.int32
@@ -195,7 +195,7 @@
     rank = jnp.sum(jnp.where(bt, counts, 0.0), axis=0, keepdims=True)
     own8 = jnp.broadcast_to(own_ref[...].astype(F32), (8, DEV)).astype(BF16)
     dest = dot(own8, hot)[0:1].astype(I32)
-    dest = ((dest >> 4) & 1) * 64 + ((dest >> 2) & 3) * 16 + (dest & 3) * 4 + (dest >> 5)
+    dest = (dest & 3) * 1 + ((dest >> 2) & 3) * 4 + (dest >> 5) * 16 + ((dest >> 4) & 1) * 64
     rank = rank.astype(I32)
     slot = dest * SLOTS + rank
     slot_ref[...] = jnp.broadcast_to(slot, (8, ROWS))

time: 44.8 us -> 44.5 us (level)
  no operation moved by 1% of the time
where the time goes in v5:
time: 44.5 us; the launch traced here: 43.8 us
  blocking collectives  21.4 us (48%)
  Pallas kernels  11.9 us (27%)
  starting transfers between devices  8.59 us (19%)
  waiting for transfers between devices  1.75 us (4%)
    all_to_all x1, blocking collectives, per_device(): lax.all_to_all(send.reshape(DEV, 1, SLOTS * NZ), SWAP_AXES, 0, 0, tiled=T...  21.4 us
    ppermute x1, starting transfers between devices, per_device(): gone_e = lax.ppermute(one_e, BRICK_AXES, with_next)  6.39 us
    pallas_call x1, Pallas kernels, per_device(): pl.pallas_call(adjoint_kernel, in_specs=[SMEM, SMEM] + [VMEM] * 7, out_sp...  3.85 us
    pallas_call x1, Pallas kernels, per_device(): call(residual_kernel, 'residual', [SMEM] + [VMEM] * 6, [f32(12, PL + 1, N...  3.48 us
    pallas_call x1, Pallas kernels, per_device(): call(residual_halo_kernel, 'residual_halo', [HBM] * 4, [pay, pay], [pltpu...  2.01 us
    ppermute x1, waiting for transfers between devices, per_device(): gtwo_e = lax.ppermute(two_e, BRICK_AXES, with_last)  1.46 us
    ppermute x1, starting transfers between devices, per_device(): gtwo_r = lax.ppermute(two_r, BRICK_AXES, with_last)  1.29 us
    pallas_call x1, Pallas kernels, per_device(): call(field_halo_kernel, 'field_halo', [HBM], [pay, pay], [pltpu.VMEM((NF,...  1.29 us
  transfers between devices with their start and end apart: 4, of which 3 were waited for; matrix products, arithmetic and copies ran while one was open for 0% of the time, Pallas kernels for 21%

profile of v5, /device:TPU:0, one launch (start us, length us, event | category | flops | bytes accessed | tf_op | source)
XLA Modules:
  0.0 43.8 jit_solution(14064389758028624321)
XLA Ops:
  0.0 1.3 %field_halo.1 = (f32[8,64,128]{2,1,0:T(8,128)S(1)}, f32[8,64,128]{2,1,0:T(8,128)S(1)}) custom-call(f32[1,2,2,3,8,64,128]{6,5,4,3,2,1,0:T(8,128)} %e_ref.1), custom_call_target="tpu_custom_call" | custom-call | flops 400000 | bytes 1200000 | tf_op jit(solution)/shard_map/field_halo/pallas_call | solution.py:366
  1.3 0.0 copy-start
  1.3 0.0 copy-start.1
  1.3 0.0 copy-start.2
  1.3 0.0 copy-start.3
  1.3 0.0 copy-start.4
  1.4 0.0 copy-start.5
  1.4 0.0 copy-start.6
  1.4 6.4 %collective-permute-start = (f32[8,64,128]{2,1,0:T(8,128)S(1)}, f32[8,64,128]{2,1,0:T(8,128)S(1)}, u32[]{:S(2)}, u32[]{:S(2)}) collective-permute-start(f32[8,64,128]{2,1,0:T(8,128)S(1)} %get-tuple-element.24), channel_id=1, source_target_pairs={{1,2},{3,4},{5,6},{7,8},{9,10},{11,12},{13,14},{15,0},{2,1},{4,3},... | collective-permute-start | bytes 786440 | tf_op jit(solution)/shard_map/ppermute | solution.py:370
  7.8 0.0 collective-permute-start.1
  7.8 2.0 %residual_halo.1 = (f32[8,64,128]{2,1,0:T(8,128)S(1)}, f32[8,64,128]{2,1,0:T(8,128)S(1)}) custom-call(f32[2]{0:T(128)} %om_ref.3, f32[1,2,2,3,8,64,128]{6,5,4,3,2,1,0:T(8,128)} %e_ref.1, f32[1,2,2,3,8,64,128]{6,5,4,3,2,1,0:T(8,128)} %s_ref, f32[1,8,64,128]{3,2,1,0:T(8,128)} %c_ref.1), custom_call_target="tpu_custom_call" | custom-call | flops 2000000 | bytes 3000000 | tf_op jit(solution)/shard_map/residual_halo/pallas_call | solution.py:372
  9.8 0.0 copy-start.7
  9.8 0.9 %collective-permute-start.2 = (f32[8,64,128]{2,1,0:T(8,128)S(1)}, f32[8,64,128]{2,1,0:T(8,128)S(1)}, u32[]{:S(2)}, u32[]{:S(2)}) collective-permute-start(f32[8,64,128]{2,1,0:T(8,128)S(1)} %get-tuple-element.29), channel_id=1, source_target_pairs={{1,2},{3,4},{5,6},{7,8},{9,10},{11,12},{13,14},{15,0},{2,1},{4,3},... | collective-permute-start | bytes 786440 | tf_op jit(solution)/shard_map/ppermute | solution.py:384
  10.7 1.3 %collective-permute-start.3 = (f32[8,64,128]{2,1,0:T(8,128)S(1)}, f32[8,64,128]{2,1,0:T(8,128)S(1)}, u32[]{:S(2)}, u32[]{:S(2)}) collective-permute-start(f32[8,64,128]{2,1,0:T(8,128)S(1)} %get-tuple-element.18), channel_id=1, source_target_pairs={{0,1},{2,3},{4,5},{6,7},{8,9},{10,11},{12,13},{14,15},{1,0},{3,2},... | collective-permute-start | bytes 786440 | tf_op jit(solution)/shard_map/ppermute | solution.py:385
  12.0 0.0 copy-done
  12.0 0.0 copy-done.1
  12.0 0.0 copy-done.2
  12.0 0.0 copy-done.3
  12.0 0.0 copy-done.4
  12.0 0.0 copy-done.5
  12.0 0.0 copy-done.6
  12.0 3.5 %residual.1 = (f32[12,9,72,128]{3,2,1,0:T(8,128)S(1)}, s32[8,512]{1,0:T(8,128)S(1)}, f32[128,128]{1,0:T(8,128)S(1)}) custom-call(f32[2]{0:T(128)S(1)} %copy-done.3, f32[1,2,2,3,8,64,128]{6,5,4,3,2,1,0:T(8,128)S(1)} %copy-done, f32[1,2,2,3,8,64,128]{6,5,4,3,2,1,0:T(8,128)S(1)} %copy-done.1, f32[1,8,64,128]{3,2,1,0:T(8,128)S(1)} %copy-done.2, ...), custom_call_target="tpu_custom_call" | custom-call | flops 30000000 | bytes 8000000 | tf_op jit(solution)/shard_map/residual/pallas_call | solution.py:391
  15.5 0.0 collective-permute-done.gone_ref
  15.5 1.5 %collective-permute-done.1.gtwo_ref = f32[8,64,128]{2,1,0:T(8,128)S(1)} collective-permute-done((f32[8,64,128]{2,1,0:T(8,128)S(1)}, f32[8,64,128]{2,1,0:T(8,128)S(1)}, u32[]{:S(2)}, u32[]{:S(2)}) %collective-permute-start.1) | collective-permute-done | bytes 262176 | tf_op jit(solution)/shard_map/ppermute | solution.py:371
  17.0 0.0 copy-done.7
  17.0 3.9 %adjoint.1 = (f32[1152,128]{1,0:T(8,128)S(1)}, f32[2,64,128]{2,1,0:T(8,128)S(1)}, f32[20,64,128]{2,1,0:T(8,128)S(1)}, f32[12,9,72,128]{3,2,1,0:T(8,128)S(1)}) custom-call(f32[2]{0:T(128)S(1)} %copy-done.3, s32[8]{0:T(128)S(1)} %copy-done.7, f32[1,2,2,3,8,64,128]{6,5,4,3,2,1,0:T(8,128)S(1)} %copy-done, ...), custom_call_target="tpu_custom_call", output_to_operand_aliasing={{3}: (8, {})} | custom-call | flops 40000000 | bytes 8000000 | tf_op jit(solution)/shard_map/adjoint/pallas_call | solution.py:399
  20.9 0.1 collective-permute-done.2.gone_ref
  21.0 0.2 collective-permute-done.3.gtwo_ref
  21.2 0.4 residual_fix.1
  21.6 21.4 %all_to_all.5 = f32[128,1,1152]{2,1,0:T(1,128)S(1)} all-to-all(f32[128,1,1152]{2,1,0:T(1,128)S(1)} %bitcast.5), channel_id=1, replica_groups=mesh['y'=4,'core'=2,'x'=4,'z'=4] {'core','y','x','z'}, dimensions={0} | all-to-all | bytes 1179648 | tf_op jit(solution)/shard_map/all_to_all | solution.py:413
  43.0 0.8 %owner_sum.1 = f32[32,128]{1,0:T(8,128)} custom-call(f32[1152,128]{1,0:T(8,128)S(1)} %bitcast.4), custom_call_target="tpu_custom_call" | custom-call | tf_op jit(solution)/shard_map/owner_sum/pallas_call | solution.py:414
Async XLA Ops:
  1.3 10.7 %copy-start = (f32[1,2,2,3,8,64,128]{6,5,4,3,2,1,0:T(8,128)S(1)}, f32[1,2,2,3,8,64,128]{6,5,4,3,2,1,0:T(8,128)}, u32[]{:S(2)}) copy-start(f32[1,2,2,3,8,64,128]{6,5,4,3,2,1,0:T(8,128)} %e_ref.1) | copy-start | bytes 9437188
  1.3 10.7 %copy-start.1 = (f32[1,2,2,3,8,64,128]{6,5,4,3,2,1,0:T(8,128)S(1)}, f32[1,2,2,3,8,64,128]{6,5,4,3,2,1,0:T(8,128)}, u32[]{:S(2)}) copy-start(f32[1,2,2,3,8,64,128]{6,5,4,3,2,1,0:T(8,128)} %s_ref) | copy-start | bytes 9437188
  1.3 10.7 %copy-start.2 = (f32[1,8,64,128]{3,2,1,0:T(8,128)S(1)}, f32[1,8,64,128]{3,2,1,0:T(8,128)}, u32[]{:S(2)}) copy-start(f32[1,8,64,128]{3,2,1,0:T(8,128)} %c_ref.1) | copy-start | bytes 786436
  1.3 10.7 %copy-start.3 = (f32[2]{0:T(128)S(1)}, f32[2]{0:T(128)}, u32[]{:S(2)}) copy-start(f32[2]{0:T(128)} %om_ref.3) | copy-start | bytes 28
  1.3 10.7 %copy-start.4 = (s32[1,512,1]{1,2,0:T(1,128)S(1)}, s32[1,512,1]{1,2,0:T(1,128)}, u32[]{:S(2)}) copy-start(s32[1,512,1]{1,2,0:T(1,128)} %param.14) | copy-start | bytes 6148
  1.4 10.7 %copy-start.5 = (s32[1,512]{1,0:T(1,128)S(1)}, s32[1,512]{1,0:T(1,128)}, u32[]{:S(2)}) copy-start(s32[1,512]{1,0:T(1,128)} %ro_ref.1) | copy-start | bytes 6148
  1.4 10.7 %copy-start.6 = (s32[128]{0:T(128)S(1)}, s32[128]{0:T(128)}, u32[]{:S(2)}) copy-start(s32[128]{0:T(128)} %param.13) | copy-start | bytes 1540
  1.4 14.2 %collective-permute-start = (f32[8,64,128]{2,1,0:T(8,128)S(1)}, f32[8,64,128]{2,1,0:T(8,128)S(1)}, u32[]{:S(2)}, u32[]{:S(2)}) collective-permute-start(f32[8,64,128]{2,1,0:T(8,128)S(1)} %get-tuple-element.24), channel_id=1, source_target_pairs={{1,2},{3,4},{5,6},{7,8},{9,10},{11,12},{13,14},{15,0},{2,1},{4,3},... | collective-permute-start | bytes 786440 | tf_op jit(solution)/shard_map/ppermute | solution.py:370
  7.8 9.2 %collective-permute-start.1 = (f32[8,64,128]{2,1,0:T(8,128)S(1)}, f32[8,64,128]{2,1,0:T(8,128)S(1)}, u32[]{:S(2)}, u32[]{:S(2)}) collective-permute-start(f32[8,64,128]{2,1,0:T(8,128)S(1)} %get-tuple-element.25), channel_id=1, source_target_pairs={{0,1},{2,3},{4,5},{6,7},{8,9},{10,11},{12,13},{14,15},{1,0},{3,2},... | collective-permute-start | bytes 786440 | tf_op jit(solution)/shard_map/ppermute | solution.py:371
  9.8 7.2 %copy-start.7 = (s32[8]{0:T(128)S(1)}, s32[8]{0:T(128)}, u32[]{:S(2)}) copy-start(s32[8]{0:T(128)} %tb_ref.1) | copy-start | bytes 100
  9.8 11.2 %collective-permute-start.2 = (f32[8,64,128]{2,1,0:T(8,128)S(1)}, f32[8,64,128]{2,1,0:T(8,128)S(1)}, u32[]{:S(2)}, u32[]{:S(2)}) collective-permute-start(f32[8,64,128]{2,1,0:T(8,128)S(1)} %get-tuple-element.29), channel_id=1, source_target_pairs={{1,2},{3,4},{5,6},{7,8},{9,10},{11,12},{13,14},{15,0},{2,1},{4,3},... | collective-permute-start | bytes 786440 | tf_op jit(solution)/shard_map/ppermute | solution.py:384
  10.7 10.4 %collective-permute-start.3 = (f32[8,64,128]{2,1,0:T(8,128)S(1)}, f32[8,64,128]{2,1,0:T(8,128)S(1)}, u32[]{:S(2)}, u32[]{:S(2)}) collective-permute-start(f32[8,64,128]{2,1,0:T(8,128)S(1)} %get-tuple-element.18), channel_id=1, source_target_pairs={{0,1},{2,3},{4,5},{6,7},{8,9},{10,11},{12,13},{14,15},{1,0},{3,2},... | collective-permute-start | bytes 786440 | tf_op jit(solution)/shard_map/ppermute | solution.py:385

commit v6 on v5

--- a/solution.py
+++ b/solution.py
@@ -58,14 +58,13 @@
 
 def field_halo_kernel(e_hbm, one_ref, two_ref, lo_ref, hi_ref, sems):
     odd = odd_brick()
-    lo = [pltpu.make_async_copy(e_hbm.at[0, f, :, pl.ds(1, 2), 0], lo_ref.at[f], sems.at[f]) for f in range(NF)]
-    hi = [pltpu.make_async_copy(e_hbm.at[0, f, :, :, PL - 1], hi_ref.at[f], sems.at[NF + f]) for f in range(NF)]
+    hi = pltpu.make_async_copy(e_hbm.at[0, :, :, :, PL - 1], hi_ref, sems.at[0])
+    lo = pltpu.make_async_copy(e_hbm.at[0, :, :, pl.ds(1, 2), 0], lo_ref, sems.at[1])
+    hi.start()
+    lo.start()
+    hi.wait()
+    lo.wait()
     for f in range(NF):
-        hi[f].start()
-        lo[f].start()
-    for f in range(NF):
-        hi[f].wait()
-        lo[f].wait()
         for part in range(2):
             q = q_of(*(hi_ref[f, part, c] for c in range(3)))
             for c in range(2):
@@ -74,39 +73,64 @@
                 two_ref[at] = jnp.where(odd, lo_ref[f, part, c], q[c])
 
 
-def residual_halo_kernel(om_hbm, e_hbm, s_hbm, c_hbm, one_ref, two_ref, om_ref, elo_ref, ehi_ref, slo_ref, shi_ref, cc_ref, sems):
+def one_hot(cond):
+    return jnp.where(cond, 1.0, 0.0).astype(BF16)
+
+
+def dot(a, b):
+    return jnp.dot(a, b, preferred_element_type=F32)
+
+
+def row_slots(rb_ref, ro_ref, own_ref, slot_ref, index_ref):
+    bt = lax.broadcasted_iota(I32, (DEV, ROWS), 0) == rb_ref[...]
+    hot = one_hot(bt)
+    before = one_hot(lax.broadcasted_iota(I32, (ROWS, ROWS), 0) < lax.broadcasted_iota(I32, (ROWS, ROWS), 1))
+    counts = dot(hot, before)
+    rank = jnp.sum(jnp.where(bt, counts, 0.0), axis=0, keepdims=True)
+    own8 = jnp.broadcast_to(own_ref[...].astype(F32), (8, DEV)).astype(BF16)
+    dest = dot(own8, hot)[0:1].astype(I32)
+    dest = (dest & 3) * 1 + ((dest >> 2) & 3) * 4 + (dest >> 5) * 16 + ((dest >> 4) & 1) * 64
+    rank = rank.astype(I32)
+    slot = dest * SLOTS + rank
+    slot_ref[...] = jnp.broadcast_to(slot, (8, ROWS))
+    codes = jnp.where(lax.broadcasted_iota(I32, (NZ, ROWS), 0) == rank, (ro_ref[...] + 1).astype(F32), 0.0).astype(BF16)
+    mine = one_hot(lax.broadcasted_iota(I32, (DEV, ROWS), 0) == dest)
+    index_ref[...] = lax.dot_general(mine, codes, (((1,), (1,)), ((), ())), preferred_element_type=F32)
+
+
+def residual_halo_kernel(
+    om_hbm, e_hbm, s_hbm, c_hbm, rb_hbm, ro_hbm, own_hbm, one_ref, two_ref, slot_ref, index_ref,
+    om_ref, rb_ref, ro_ref, own_ref, elo_ref, ehi_ref, slo_ref, shi_ref, cc_ref, sems,
+):
     odd = odd_brick()
-    small = [
-        pltpu.make_async_copy(om_hbm, om_ref, sems.at[8]),
-        pltpu.make_async_copy(c_hbm.at[0, 0], cc_ref.at[0], sems.at[9]),
-        pltpu.make_async_copy(c_hbm.at[0, PL - 1], cc_ref.at[1], sems.at[10]),
+    few = [
+        pltpu.make_async_copy(rb_hbm, rb_ref, sems.at[8]),
+        pltpu.make_async_copy(ro_hbm, ro_ref, sems.at[9]),
+        pltpu.make_async_copy(own_hbm, own_ref, sems.at[10]),
+        pltpu.make_async_copy(om_hbm, om_ref, sems.at[11]),
+        pltpu.make_async_copy(c_hbm.at[0, 0], cc_ref.at[0], sems.at[12]),
+        pltpu.make_async_copy(c_hbm.at[0, PL - 1], cc_ref.at[1], sems.at[13]),
     ]
     big = [
         [
-            pltpu.make_async_copy(e_hbm.at[0, f, :, :, pl.ds(0, 2)], elo_ref.at[f], sems.at[4 * f]),
-            pltpu.make_async_copy(s_hbm.at[0, f, :, pl.ds(1, 2), 0], slo_ref.at[f], sems.at[4 * f + 1]),
-            pltpu.make_async_copy(e_hbm.at[0, f, :, :, pl.ds(PL - 2, 2)], ehi_ref.at[f], sems.at[4 * f + 2]),
-            pltpu.make_async_copy(s_hbm.at[0, f, :, :, PL - 1], shi_ref.at[f], sems.at[4 * f + 3]),
+            pltpu.make_async_copy(e_hbm.at[0, f, :, :, pl.ds(PL - 2, 2)], ehi_ref.at[f], sems.at[4 * f]),
+            pltpu.make_async_copy(s_hbm.at[0, f, :, :, PL - 1], shi_ref.at[f], sems.at[4 * f + 1]),
+            pltpu.make_async_copy(e_hbm.at[0, f, :, :, pl.ds(0, 2)], elo_ref.at[f], sems.at[4 * f + 2]),
+            pltpu.make_async_copy(s_hbm.at[0, f, :, pl.ds(1, 2), 0], slo_ref.at[f], sems.at[4 * f + 3]),
         ]
         for f in range(NF)
     ]
-    for copy in small + big[0] + big[1]:
+    for copy in few + big[0] + big[1]:
         copy.start()
-    for copy in small:
+    for copy in few:
         copy.wait()
+    row_slots(rb_ref, ro_ref, own_ref, slot_ref, index_ref)
     for f in range(NF):
-        for copy in big[f]:
-            copy.wait()
         om = om_ref[f]
+        big[f][0].wait()
+        big[f][1].wait()
         for part in range(2):
             ch = 2 * f + part
-            vx, vy, vz = (elo_ref[f, part, c, 0] for c in range(3))
-            hx = fy(vz) - fz(vy)
-            hy = fz(vx) - (elo_ref[f, part, 2, 1] - vz)
-            hz = (elo_ref[f, part, 1, 1] - vy) - fy(vx)
-            w = om * cc_ref[0]
-            dy = rotate(bz(hx) - hz, part, w, elo_ref[f, 1 - part, 1, 0]) - slo_ref[f, part, 0]
-            dz = rotate(hy - by(hx), part, w, elo_ref[f, 1 - part, 2, 0]) - slo_ref[f, part, 1]
             ux, uy, uz = (ehi_ref[f, part, c, 0] for c in range(3))
             vx, vy, vz = (ehi_ref[f, part, c, 1] for c in range(3))
             hy, qz = q_of(vx, vy, vz)
@@ -119,19 +143,24 @@
             rx = rotate(by(hz) - bz(hy), part, w, o[0]) - shi_ref[f, part, 0]
             ry = rotate(bz(hx) - (hz - gz), part, w, o[1]) - shi_ref[f, part, 1]
             rz = rotate((hy - gy) - by(hx), part, w, o[2]) - shi_ref[f, part, 2]
-            sy, sz = q_of(rx, ry, rz)
-            one_ref[2 * ch] = jnp.where(odd, sy, dy)
-            one_ref[2 * ch + 1] = jnp.where(odd, sz, dz)
-            two_ref[2 * ch] = jnp.where(odd, dy, sy)
-            two_ref[2 * ch + 1] = jnp.where(odd, dz, sz)
-
-
-def one_hot(cond):
-    return jnp.where(cond, 1.0, 0.0).astype(BF16)
-
-
-def dot(a, b):
-    return jnp.dot(a, b, preferred_element_type=F32)
+            one_ref[2 * ch], one_ref[2 * ch + 1] = q_of(rx, ry, rz)
+        big[f][2].wait()
+        big[f][3].wait()
+        for part in range(2):
+            ch = 2 * f + part
+            vx, vy, vz = (elo_ref[f, part, c, 0] for c in range(3))
+            hx = fy(vz) - fz(vy)
+            hy = fz(vx) - (elo_ref[f, part, 2, 1] - vz)
+            hz = (elo_ref[f, part, 1, 1] - vy) - fy(vx)
+            w = om * cc_ref[0]
+            dn = [
+                rotate(bz(hx) - hz, part, w, elo_ref[f, 1 - part, 1, 0]) - slo_ref[f, part, 0],
+                rotate(hy - by(hx), part, w, elo_ref[f, 1 - part, 2, 0]) - slo_ref[f, part, 1],
+            ]
+            for c in range(2):
+                up = one_ref[2 * ch + c]
+                one_ref[2 * ch + c] = jnp.where(odd, up, dn[c])
+                two_ref[2 * ch + c] = jnp.where(odd, dn[c], up)
 
 
 def pick(hot, v):
@@ -176,7 +205,7 @@
     return (vx, vy, vz), (cx, cy, cz)
 
 
-def residual_kernel(om_ref, e_ref, s_ref, c_ref, rb_ref, ro_ref, own_ref, r_ref, slot_ref, index_ref, h_ref, g_ref):
+def residual_kernel(om_ref, e_ref, s_ref, c_ref, r_ref, h_ref, g_ref):
     zero = jnp.zeros((NY, NZ), F32)
     zpad = jnp.zeros((PAD, NZ), F32)
     for i in range(12):
@@ -187,21 +216,6 @@
         h_ref[i, PAD:PAD + NY] = zero
     for i in range(4):
         g_ref[i] = zero
-
-    bt = lax.broadcasted_iota(I32, (DEV, ROWS), 0) == rb_ref[...]
-    hot = one_hot(bt)
-    before = one_hot(lax.broadcasted_iota(I32, (ROWS, ROWS), 0) < lax.broadcasted_iota(I32, (ROWS, ROWS), 1))
-    counts = dot(hot, before)
-    rank = jnp.sum(jnp.where(bt, counts, 0.0), axis=0, keepdims=True)
-    own8 = jnp.broadcast_to(own_ref[...].astype(F32), (8, DEV)).astype(BF16)
-    dest = dot(own8, hot)[0:1].astype(I32)
-    dest = (dest & 3) * 1 + ((dest >> 2) & 3) * 4 + (dest >> 5) * 16 + ((dest >> 4) & 1) * 64
-    rank = rank.astype(I32)
-    slot = dest * SLOTS + rank
-    slot_ref[...] = jnp.broadcast_to(slot, (8, ROWS))
-    codes = jnp.where(lax.broadcasted_iota(I32, (NZ, ROWS), 0) == rank, (ro_ref[...] + 1).astype(F32), 0.0).astype(BF16)
-    mine = one_hot(lax.broadcasted_iota(I32, (DEV, ROWS), 0) == dest)
-    index_ref[...] = lax.dot_general(mine, codes, (((1,), (1,)), ((), ())), preferred_element_type=F32)
 
     rows = lax.broadcasted_iota(I32, (CH, NZ), 0)
 
@@ -369,18 +383,28 @@
     )(fields)
     gone_e = lax.ppermute(one_e, BRICK_AXES, with_next)
     gtwo_e = lax.ppermute(two_e, BRICK_AXES, with_last)
-    one_r, two_r = call(
-        residual_halo_kernel, "residual_halo", [HBM] * 4, [pay, pay],
+    one_r, two_r, slot, index = call(
+        residual_halo_kernel, "residual_halo", [HBM] * 7,
+        [pay, pay, jax.ShapeDtypeStruct((8, ROWS), I32), f32(DEV, NZ)],
         [
             pltpu.SMEM((NF,), F32),
+            pltpu.VMEM((1, ROWS), I32),
+            pltpu.VMEM((1, ROWS), I32),
+            pltpu.VMEM((1, DEV), I32),
             pltpu.VMEM((NF, 2, 3, 2, NY, NZ), F32),
             pltpu.VMEM((NF, 2, 3, 2, NY, NZ), F32),
             pltpu.VMEM((NF, 2, 2, NY, NZ), F32),
             pltpu.VMEM((NF, 2, 3, NY, NZ), F32),
             pltpu.VMEM((2, NY, NZ), F32),
-            dma((11,)),
+            dma((14,)),
         ], 2_000_000, 3_000_000,
-    )(omegas, fields, sources, conductivity)
+    )(
+        omegas, fields, sources, conductivity,
+        *(
+            pltpu.with_memory_space_constraint(x, pltpu.HBM)
+            for x in (row_brick.reshape(1, ROWS), row_offset, owner_map.reshape(1, DEV))
+        ),
+    )
     gone_r = lax.ppermute(one_r, BRICK_AXES, with_next)
     gtwo_r = lax.ppermute(two_r, BRICK_AXES, with_last)
     fields_v, sources_v, conductivity_v, _ = lax.optimization_barrier((fields_in, sources_in, conductivity_in, two_r))
@@ -388,14 +412,9 @@
         pltpu.with_memory_space_constraint(x, pltpu.VMEM) for x in (fields_v, sources_v, conductivity_v)
     )
     halo = [pltpu.VMEM((8, PAD + NY, NZ), F32), pltpu.VMEM((4, NY, NZ), F32)]
-    r, slot, index = call(
-        residual_kernel, "residual", [SMEM] + [VMEM] * 6,
-        [f32(12, PL + 1, NY + PAD, NZ), jax.ShapeDtypeStruct((8, ROWS), I32), f32(DEV, NZ)],
-        halo, 30_000_000, 8_000_000,
-    )(
-        omegas_in, fields_v, sources_v, conductivity_v,
-        row_brick.reshape(1, ROWS), row_offset, owner_map.reshape(1, DEV),
-    )
+    (r,) = call(
+        residual_kernel, "residual", [SMEM] + [VMEM] * 3, [f32(12, PL + 1, NY + PAD, NZ)], halo, 30_000_000, 8_000_000,
+    )(omegas_in, fields_v, sources_v, conductivity_v)
     part, rest, fac, _ = pl.pallas_call(
         adjoint_kernel,
         in_specs=[SMEM, SMEM] + [VMEM] * 7,

time: 44.5 us -> 44.4 us (level)
  transfers between devices with their start and end apart: 4 -> 4, of which waited for: 3 -> 2; matrix products, arithmetic and copies ran while one was open for 0% -> 0% of each run, Pallas kernels for 21% -> 21%
where the time goes in v6:
time: 44.4 us; the launch traced here: 43.7 us
  blocking collectives  21.3 us (48%)
  Pallas kernels  11.9 us (27%)
  starting transfers between devices  8.6 us (19%)
  waiting for transfers between devices  1.76 us (4%)
    all_to_all x1, blocking collectives, per_device(): lax.all_to_all(send.reshape(DEV, 1, SLOTS * NZ), SWAP_AXES, 0, 0, tiled=T...  21.3 us
    ppermute x1, starting transfers between devices, per_device(): gone_e = lax.ppermute(one_e, BRICK_AXES, with_next)  6.39 us
    pallas_call x1, Pallas kernels, per_device(): pl.pallas_call(adjoint_kernel, in_specs=[SMEM, SMEM] + [VMEM] * 7, out_sp...  3.97 us
    pallas_call x1, Pallas kernels, per_device(): call(residual_kernel, 'residual', [SMEM] + [VMEM] * 3, [f32(12, PL + 1, N...  3.19 us
    pallas_call x1, Pallas kernels, per_device(): call(residual_halo_kernel, 'residual_halo', [HBM] * 7, [pay, pay, jax.Sha...  2.21 us
    ppermute x1, waiting for transfers between devices, per_device(): gtwo_e = lax.ppermute(two_e, BRICK_AXES, with_last)  1.58 us
    ppermute x1, starting transfers between devices, per_device(): gtwo_r = lax.ppermute(two_r, BRICK_AXES, with_last)  1.31 us
    pallas_call x1, Pallas kernels, per_device(): call(field_halo_kernel, 'field_halo', [HBM], [pay, pay], [pltpu.VMEM((NF,...  1.21 us
  transfers between devices with their start and end apart: 4, of which 2 were waited for; matrix products, arithmetic and copies ran while one was open for 0% of the time, Pallas kernels for 21%

profile of v6, /device:TPU:0, one launch (start us, length us, event | category | flops | bytes accessed | tf_op | source)
XLA Modules:
  0.0 43.7 jit_solution(18254776352638737441)
XLA Ops:
  0.0 1.2 %field_halo.1 = (f32[8,64,128]{2,1,0:T(8,128)S(1)}, f32[8,64,128]{2,1,0:T(8,128)S(1)}) custom-call(f32[1,2,2,3,8,64,128]{6,5,4,3,2,1,0:T(8,128)} %e_ref.1), custom_call_target="tpu_custom_call" | custom-call | flops 400000 | bytes 1200000 | tf_op jit(solution)/shard_map/field_halo/pallas_call | solution.py:380
  1.2 0.0 copy-start
  1.2 0.0 copy-start.1
  1.2 0.0 copy-start.2
  1.3 0.0 copy-start.3
  1.3 6.4 %collective-permute-start = (f32[8,64,128]{2,1,0:T(8,128)S(1)}, f32[8,64,128]{2,1,0:T(8,128)S(1)}, u32[]{:S(2)}, u32[]{:S(2)}) collective-permute-start(f32[8,64,128]{2,1,0:T(8,128)S(1)} %get-tuple-element.22), channel_id=1, source_target_pairs={{1,2},{3,4},{5,6},{7,8},{9,10},{11,12},{13,14},{15,0},{2,1},{4,3},... | collective-permute-start | bytes 786440 | tf_op jit(solution)/shard_map/ppermute | solution.py:384
  7.7 0.0 collective-permute-start.1
  7.7 2.2 %residual_halo.1 = (f32[8,64,128]{2,1,0:T(8,128)S(1)}, f32[8,64,128]{2,1,0:T(8,128)S(1)}, s32[8,512]{1,0:T(8,128)S(1)}, f32[128,128]{1,0:T(8,128)S(1)}) custom-call(f32[2]{0:T(128)} %om_ref.3, f32[1,2,2,3,8,64,128]{6,5,4,3,2,1,0:T(8,128)} %e_ref.1, f32[1,2,2,3,8,64,128]{6,5,4,3,2,1,0:T(8,128)} %s_ref, f32[1,8,64,128]{3,2,1,0:T(8,128)} %c_ref.1, ...), custom_call_target="tpu_custom_call" | custom-call | flops 2000000 | bytes 3000000 | tf_op jit(solution)/shard_map/residual_halo/pallas_call | solution.py:386
  9.9 0.9 %collective-permute-start.2 = (f32[8,64,128]{2,1,0:T(8,128)S(1)}, f32[8,64,128]{2,1,0:T(8,128)S(1)}, u32[]{:S(2)}, u32[]{:S(2)}) collective-permute-start(f32[8,64,128]{2,1,0:T(8,128)S(1)} %get-tuple-element.27), channel_id=1, source_target_pairs={{1,2},{3,4},{5,6},{7,8},{9,10},{11,12},{13,14},{15,0},{2,1},{4,3},... | collective-permute-start | bytes 786440 | tf_op jit(solution)/shard_map/ppermute | solution.py:408
  10.8 0.0 copy-start.4
  10.8 1.3 %collective-permute-start.3 = (f32[8,64,128]{2,1,0:T(8,128)S(1)}, f32[8,64,128]{2,1,0:T(8,128)S(1)}, u32[]{:S(2)}, u32[]{:S(2)}) collective-permute-start(f32[8,64,128]{2,1,0:T(8,128)S(1)} %get-tuple-element.17), channel_id=1, source_target_pairs={{0,1},{2,3},{4,5},{6,7},{8,9},{10,11},{12,13},{14,15},{1,0},{3,2},... | collective-permute-start | bytes 786440 | tf_op jit(solution)/shard_map/ppermute | solution.py:409
  12.1 0.0 copy-done
  12.1 0.0 copy-done.1
  12.1 0.0 copy-done.2
  12.1 0.0 copy-done.3
  12.1 3.2 %residual.1.rin_ref = f32[12,9,72,128]{3,2,1,0:T(8,128)S(1)} custom-call(f32[2]{0:T(128)S(1)} %copy-done.3, f32[1,2,2,3,8,64,128]{6,5,4,3,2,1,0:T(8,128)S(1)} %copy-done, f32[1,2,2,3,8,64,128]{6,5,4,3,2,1,0:T(8,128)S(1)} %copy-done.1, f32[1,8,64,128]{3,2,1,0:T(8,128)S(1)} %copy-done.2), custom_call_target="tpu_custom_call" | custom-call | flops 30000000 | bytes 8000000 | tf_op jit(solution)/shard_map/residual/pallas_call | solution.py:415
  15.3 0.0 collective-permute-done.gone_ref
  15.3 1.6 %collective-permute-done.1.gtwo_ref = f32[8,64,128]{2,1,0:T(8,128)S(1)} collective-permute-done((f32[8,64,128]{2,1,0:T(8,128)S(1)}, f32[8,64,128]{2,1,0:T(8,128)S(1)}, u32[]{:S(2)}, u32[]{:S(2)}) %collective-permute-start.1) | collective-permute-done | bytes 262176 | tf_op jit(solution)/shard_map/ppermute | solution.py:385
  16.9 0.0 copy-done.4
  16.9 4.0 %adjoint.1 = (f32[1152,128]{1,0:T(8,128)S(1)}, f32[2,64,128]{2,1,0:T(8,128)S(1)}, f32[20,64,128]{2,1,0:T(8,128)S(1)}, f32[12,9,72,128]{3,2,1,0:T(8,128)S(1)}) custom-call(f32[2]{0:T(128)S(1)} %copy-done.3, s32[8]{0:T(128)S(1)} %copy-done.4, f32[1,2,2,3,8,64,128]{6,5,4,3,2,1,0:T(8,128)S(1)} %copy-done, ...), custom_call_target="tpu_custom_call", output_to_operand_aliasing={{3}: (8, {})} | custom-call | flops 40000000 | bytes 8000000 | tf_op jit(solution)/shard_map/adjoint/pallas_call | solution.py:418
  20.9 0.2 collective-permute-done.2.gone_ref
  21.1 0.0 collective-permute-done.3.gtwo_ref
  21.1 0.4 %residual_fix.1 = f32[1152,128]{1,0:T(8,128)S(1)} custom-call(f32[20,64,128]{2,1,0:T(8,128)S(1)} %get-tuple-element.25.fac_ref, f32[2,64,128]{2,1,0:T(8,128)S(1)} %get-tuple-element.26.rest_ref, f32[8,64,128]{2,1,0:T(8,128)S(1)} %collective-permute-done.2.gone_ref, f32[8,64,128]{2,1,0:T(8,128)S(1)} %collective-permute-done.3.gtwo_ref, ...), custom_call_target="tpu_custom_call" | custom-call | flops 20000000 | bytes 3000000 | tf_op jit(solution)/shard_map/residual_fix/pallas_call | solution.py:429
  21.5 21.3 %all_to_all.5 = f32[128,1,1152]{2,1,0:T(1,128)S(1)} all-to-all(f32[128,1,1152]{2,1,0:T(1,128)S(1)} %bitcast.5), channel_id=1, replica_groups=mesh['y'=4,'core'=2,'x'=4,'z'=4] {'core','y','x','z'}, dimensions={0} | all-to-all | bytes 1179648 | tf_op jit(solution)/shard_map/all_to_all | solution.py:432
  42.9 0.8 %owner_sum.1 = f32[32,128]{1,0:T(8,128)} custom-call(f32[1152,128]{1,0:T(8,128)S(1)} %bitcast.4), custom_call_target="tpu_custom_call" | custom-call | tf_op jit(solution)/shard_map/owner_sum/pallas_call | solution.py:433
Async XLA Ops:
  1.2 10.9 %copy-start = (f32[1,2,2,3,8,64,128]{6,5,4,3,2,1,0:T(8,128)S(1)}, f32[1,2,2,3,8,64,128]{6,5,4,3,2,1,0:T(8,128)}, u32[]{:S(2)}) copy-start(f32[1,2,2,3,8,64,128]{6,5,4,3,2,1,0:T(8,128)} %e_ref.1) | copy-start | bytes 9437188
  1.2 10.9 %copy-start.1 = (f32[1,2,2,3,8,64,128]{6,5,4,3,2,1,0:T(8,128)S(1)}, f32[1,2,2,3,8,64,128]{6,5,4,3,2,1,0:T(8,128)}, u32[]{:S(2)}) copy-start(f32[1,2,2,3,8,64,128]{6,5,4,3,2,1,0:T(8,128)} %s_ref) | copy-start | bytes 9437188
  1.2 10.9 %copy-start.2 = (f32[1,8,64,128]{3,2,1,0:T(8,128)S(1)}, f32[1,8,64,128]{3,2,1,0:T(8,128)}, u32[]{:S(2)}) copy-start(f32[1,8,64,128]{3,2,1,0:T(8,128)} %c_ref.1) | copy-start | bytes 786436
  1.3 10.9 %copy-start.3 = (f32[2]{0:T(128)S(1)}, f32[2]{0:T(128)}, u32[]{:S(2)}) copy-start(f32[2]{0:T(128)} %om_ref.3) | copy-start | bytes 28
  1.3 14.0 %collective-permute-start = (f32[8,64,128]{2,1,0:T(8,128)S(1)}, f32[8,64,128]{2,1,0:T(8,128)S(1)}, u32[]{:S(2)}, u32[]{:S(2)}) collective-permute-start(f32[8,64,128]{2,1,0:T(8,128)S(1)} %get-tuple-element.22), channel_id=1, source_target_pairs={{1,2},{3,4},{5,6},{7,8},{9,10},{11,12},{13,14},{15,0},{2,1},{4,3},... | collective-permute-start | bytes 786440 | tf_op jit(solution)/shard_map/ppermute | solution.py:384
  7.7 9.2 %collective-permute-start.1 = (f32[8,64,128]{2,1,0:T(8,128)S(1)}, f32[8,64,128]{2,1,0:T(8,128)S(1)}, u32[]{:S(2)}, u32[]{:S(2)}) collective-permute-start(f32[8,64,128]{2,1,0:T(8,128)S(1)} %get-tuple-element.23), channel_id=1, source_target_pairs={{0,1},{2,3},{4,5},{6,7},{8,9},{10,11},{12,13},{14,15},{1,0},{3,2},... | collective-permute-start | bytes 786440 | tf_op jit(solution)/shard_map/ppermute | solution.py:385
  9.9 11.2 %collective-permute-start.2 = (f32[8,64,128]{2,1,0:T(8,128)S(1)}, f32[8,64,128]{2,1,0:T(8,128)S(1)}, u32[]{:S(2)}, u32[]{:S(2)}) collective-permute-start(f32[8,64,128]{2,1,0:T(8,128)S(1)} %get-tuple-element.27), channel_id=1, source_target_pairs={{1,2},{3,4},{5,6},{7,8},{9,10},{11,12},{13,14},{15,0},{2,1},{4,3},... | collective-permute-start | bytes 786440 | tf_op jit(solution)/shard_map/ppermute | solution.py:408
  10.8 6.1 %copy-start.4 = (s32[8]{0:T(128)S(1)}, s32[8]{0:T(128)}, u32[]{:S(2)}) copy-start(s32[8]{0:T(128)} %tb_ref.1) | copy-start | bytes 100
  10.8 10.3 %collective-permute-start.3 = (f32[8,64,128]{2,1,0:T(8,128)S(1)}, f32[8,64,128]{2,1,0:T(8,128)S(1)}, u32[]{:S(2)}, u32[]{:S(2)}) collective-permute-start(f32[8,64,128]{2,1,0:T(8,128)S(1)} %get-tuple-element.17), channel_id=1, source_target_pairs={{0,1},{2,3},{4,5},{6,7},{8,9},{10,11},{12,13},{14,15},{1,0},{3,2},... | collective-permute-start | bytes 786440 | tf_op jit(solution)/shard_map/ppermute | solution.py:409

commit v7 on v6

--- a/solution.py
+++ b/solution.py
@@ -251,7 +251,7 @@
 
 def adjoint_kernel(
     om_ref, tb_ref, e_ref, c_ref, slot_ref, index_ref, gone_ref, gtwo_ref, rin_ref,
-    part_ref, rest_ref, fac_ref, r_ref, h_ref, g_ref, loc_ref,
+    part_ref, rest_ref, fac_ref, hot_ref, r_ref, h_ref, g_ref, loc_ref,
 ):
     live, low, nxt = place(tb_ref)
     odd = odd_brick()
@@ -309,6 +309,10 @@
 
     lax.fori_loop(0, PL, step, 0)
 
+    ends = lax.broadcasted_iota(I32, (DEV * SLOTS, NY), 0)
+    hot_ref[...] = jnp.concatenate(
+        [one_hot(ends == slot_ref[0:1, 0:NY]), one_hot(ends == slot_ref[0:1, ROWS - NY:ROWS])], axis=1
+    )
     rest_ref[0] = loc_ref[0:NY]
     rest_ref[1] = loc_ref[ROWS - NY:ROWS]
     lo, hi = NY, ROWS - NY
@@ -317,7 +321,7 @@
     part_ref[pl.ds(CAP, DEV, stride=SLOTS), :] = index_ref[...]
 
 
-def residual_fix_kernel(fac_ref, rest_ref, gone_ref, gtwo_ref, slot_ref, part_ref, out_ref, two_ref):
+def residual_fix_kernel(fac_ref, rest_ref, gone_ref, gtwo_ref, hot_ref, part_ref, out_ref, two_ref):
     odd = odd_brick()
     low, high = rest_ref[0], rest_ref[1]
     for ch in range(4):
@@ -330,9 +334,7 @@
         high = high + (o[0] * (by(ry) + bz(rz)) - o[1] * ry - o[2] * rz)
     two_ref[0:NY] = low
     two_ref[NY:2 * NY] = high
-    at = lax.broadcasted_iota(I32, (DEV * SLOTS, NY), 0)
-    hot = jnp.concatenate([one_hot(at == slot_ref[0:1, 0:NY]), one_hot(at == slot_ref[0:1, ROWS - NY:ROWS])], axis=1)
-    out_ref[...] = part_ref[...] + pick(hot, two_ref[...])
+    out_ref[...] = part_ref[...] + pick(hot_ref[...], two_ref[...])
 
 
 def owner_kernel(got_ref, out_ref):
@@ -415,12 +417,12 @@
     (r,) = call(
         residual_kernel, "residual", [SMEM] + [VMEM] * 3, [f32(12, PL + 1, NY + PAD, NZ)], halo, 30_000_000, 8_000_000,
     )(omegas_in, fields_v, sources_v, conductivity_v)
-    part, rest, fac, _ = pl.pallas_call(
+    part, rest, fac, hot, _ = pl.pallas_call(
         adjoint_kernel,
         in_specs=[SMEM, SMEM] + [VMEM] * 7,
-        out_specs=[VMEM] * 4,
-        out_shape=[packed, f32(2, NY, NZ), f32(20, NY, NZ), f32(12, PL + 1, NY + PAD, NZ)],
-        input_output_aliases={8: 3},
+        out_specs=[VMEM] * 5,
+        out_shape=[packed, f32(2, NY, NZ), f32(20, NY, NZ), jax.ShapeDtypeStruct((DEV * SLOTS, 2 * NY), BF16), f32(12, PL + 1, NY + PAD, NZ)],
+        input_output_aliases={8: 4},
         scratch_shapes=halo + [pltpu.VMEM((ROWS, NZ), F32)],
         compiler_params=pltpu.CompilerParams(vmem_limit_bytes=LIMIT),
         cost_estimate=pl.CostEstimate(flops=40_000_000, bytes_accessed=8_000_000, transcendentals=0),
@@ -428,7 +430,7 @@
     )(omegas_in, tx_bricks, fields_v, conductivity_v, slot, index, gone_e, gtwo_e, r)
     (send,) = call(
         residual_fix_kernel, "residual_fix", [VMEM] * 6, [packed], [pltpu.VMEM((2 * NY, NZ), F32)], 20_000_000, 3_000_000,
-    )(fac, rest, gone_r, gtwo_r, slot, part)
+    )(fac, rest, gone_r, gtwo_r, hot, part)
     got = lax.all_to_all(send.reshape(DEV, 1, SLOTS * NZ), SWAP_AXES, 0, 0, tiled=True).reshape(DEV * SLOTS, NZ)
     return pl.pallas_call(
         owner_kernel,

time: 44.4 us -> 44.4 us (level)
  transfers between devices with their start and end apart: 4 -> 4, of which waited for: 2 -> 2; matrix products, arithmetic and copies ran while one was open for 0% -> 0% of each run, Pallas kernels for 21% -> 22%
where the time goes in v7:
time: 44.4 us; the launch traced here: 43.7 us
  blocking collectives  21.3 us (48%)
  Pallas kernels  11.9 us (27%)
  starting transfers between devices  8.6 us (19%)
  waiting for transfers between devices  1.7 us (4%)
    all_to_all x1, blocking collectives, per_device(): lax.all_to_all(send.reshape(DEV, 1, SLOTS * NZ), SWAP_AXES, 0, 0, tiled=T...  21.3 us
    ppermute x1, starting transfers between devices, per_device(): gone_e = lax.ppermute(one_e, BRICK_AXES, with_next)  6.39 us
    pallas_call x1, Pallas kernels, per_device(): pl.pallas_call(adjoint_kernel, in_specs=[SMEM, SMEM] + [VMEM] * 7, out_sp...  4.03 us
    pallas_call x1, Pallas kernels, per_device(): call(residual_kernel, 'residual', [SMEM] + [VMEM] * 3, [f32(12, PL + 1, N...  3.19 us
    pallas_call x1, Pallas kernels, per_device(): call(residual_halo_kernel, 'residual_halo', [HBM] * 7, [pay, pay, jax.Sha...  2.21 us
    ppermute x1, waiting for transfers between devices, per_device(): gtwo_e = lax.ppermute(two_e, BRICK_AXES, with_last)  1.58 us
    ppermute x1, starting transfers between devices, per_device(): gtwo_r = lax.ppermute(two_r, BRICK_AXES, with_last)  1.31 us
    pallas_call x1, Pallas kernels, per_device(): call(field_halo_kernel, 'field_halo', [HBM], [pay, pay], [pltpu.VMEM((NF,...  1.21 us
  transfers between devices with their start and end apart: 4, of which 2 were waited for; matrix products, arithmetic and copies ran while one was open for 0% of the time, Pallas kernels for 22%

profile of v7, /device:TPU:0, one launch (start us, length us, event | category | flops | bytes accessed | tf_op | source)
XLA Modules:
  0.0 43.7 jit_solution(9968609975822796610)
XLA Ops:
  0.0 1.2 %field_halo.1 = (f32[8,64,128]{2,1,0:T(8,128)S(1)}, f32[8,64,128]{2,1,0:T(8,128)S(1)}) custom-call(f32[1,2,2,3,8,64,128]{6,5,4,3,2,1,0:T(8,128)} %e_ref.1), custom_call_target="tpu_custom_call" | custom-call | flops 400000 | bytes 1200000 | tf_op jit(solution)/shard_map/field_halo/pallas_call | solution.py:382
  1.2 0.0 copy-start
  1.2 0.0 copy-start.1
  1.2 0.0 copy-start.2
  1.3 0.0 copy-start.3
  1.3 6.4 %collective-permute-start = (f32[8,64,128]{2,1,0:T(8,128)S(1)}, f32[8,64,128]{2,1,0:T(8,128)S(1)}, u32[]{:S(2)}, u32[]{:S(2)}) collective-permute-start(f32[8,64,128]{2,1,0:T(8,128)S(1)} %get-tuple-element.23), channel_id=1, source_target_pairs={{1,2},{3,4},{5,6},{7,8},{9,10},{11,12},{13,14},{15,0},{2,1},{4,3},... | collective-permute-start | bytes 786440 | tf_op jit(solution)/shard_map/ppermute | solution.py:386
  7.7 0.0 collective-permute-start.1
  7.7 2.2 %residual_halo.1 = (f32[8,64,128]{2,1,0:T(8,128)S(1)}, f32[8,64,128]{2,1,0:T(8,128)S(1)}, s32[8,512]{1,0:T(8,128)S(1)}, f32[128,128]{1,0:T(8,128)S(1)}) custom-call(f32[2]{0:T(128)} %om_ref.3, f32[1,2,2,3,8,64,128]{6,5,4,3,2,1,0:T(8,128)} %e_ref.1, f32[1,2,2,3,8,64,128]{6,5,4,3,2,1,0:T(8,128)} %s_ref, f32[1,8,64,128]{3,2,1,0:T(8,128)} %c_ref.1, ...), custom_call_target="tpu_custom_call" | custom-call | flops 2000000 | bytes 3000000 | tf_op jit(solution)/shard_map/residual_halo/pallas_call | solution.py:388
  9.9 0.9 %collective-permute-start.2 = (f32[8,64,128]{2,1,0:T(8,128)S(1)}, f32[8,64,128]{2,1,0:T(8,128)S(1)}, u32[]{:S(2)}, u32[]{:S(2)}) collective-permute-start(f32[8,64,128]{2,1,0:T(8,128)S(1)} %get-tuple-element.28), channel_id=1, source_target_pairs={{1,2},{3,4},{5,6},{7,8},{9,10},{11,12},{13,14},{15,0},{2,1},{4,3},... | collective-permute-start | bytes 786440 | tf_op jit(solution)/shard_map/ppermute | solution.py:410
  10.8 0.0 copy-start.4
  10.8 1.3 %collective-permute-start.3 = (f32[8,64,128]{2,1,0:T(8,128)S(1)}, f32[8,64,128]{2,1,0:T(8,128)S(1)}, u32[]{:S(2)}, u32[]{:S(2)}) collective-permute-start(f32[8,64,128]{2,1,0:T(8,128)S(1)} %get-tuple-element.18), channel_id=1, source_target_pairs={{0,1},{2,3},{4,5},{6,7},{8,9},{10,11},{12,13},{14,15},{1,0},{3,2},... | collective-permute-start | bytes 786440 | tf_op jit(solution)/shard_map/ppermute | solution.py:411
  12.1 0.0 copy-done
  12.1 0.0 copy-done.1
  12.1 0.0 copy-done.2
  12.1 0.0 copy-done.3
  12.1 3.2 %residual.1.rin_ref = f32[12,9,72,128]{3,2,1,0:T(8,128)S(1)} custom-call(f32[2]{0:T(128)S(1)} %copy-done.3, f32[1,2,2,3,8,64,128]{6,5,4,3,2,1,0:T(8,128)S(1)} %copy-done, f32[1,2,2,3,8,64,128]{6,5,4,3,2,1,0:T(8,128)S(1)} %copy-done.1, f32[1,8,64,128]{3,2,1,0:T(8,128)S(1)} %copy-done.2), custom_call_target="tpu_custom_call" | custom-call | flops 30000000 | bytes 8000000 | tf_op jit(solution)/shard_map/residual/pallas_call | solution.py:417
  15.3 0.0 collective-permute-done.gone_ref
  15.3 1.6 %collective-permute-done.1.gtwo_ref = f32[8,64,128]{2,1,0:T(8,128)S(1)} collective-permute-done((f32[8,64,128]{2,1,0:T(8,128)S(1)}, f32[8,64,128]{2,1,0:T(8,128)S(1)}, u32[]{:S(2)}, u32[]{:S(2)}) %collective-permute-start.1) | collective-permute-done | bytes 262176 | tf_op jit(solution)/shard_map/ppermute | solution.py:387
  16.9 0.0 copy-done.4
  16.9 4.0 %adjoint.1 = (f32[1152,128]{1,0:T(8,128)S(1)}, f32[2,64,128]{2,1,0:T(8,128)S(1)}, f32[20,64,128]{2,1,0:T(8,128)S(1)}, bf16[1152,128]{1,0:T(8,128)(2,1)S(1)}, f32[12,9,72,128]{3,2,1,0:T(8,128)S(1)}) custom-call(f32[2]{0:T(128)S(1)} %copy-done.3, s32[8]{0:T(128)S(1)} %copy-done.4, ...), custom_call_target="tpu_custom_call", output_to_operand_aliasing={{4}: (8, {})} | custom-call | flops 40000000 | bytes 8000000 | tf_op jit(solution)/shard_map/adjoint/pallas_call | solution.py:420
  20.9 0.1 collective-permute-done.2.gone_ref
  21.1 0.0 collective-permute-done.3.gtwo_ref
  21.1 0.4 residual_fix.1
  21.5 21.3 %all_to_all.5 = f32[128,1,1152]{2,1,0:T(1,128)S(1)} all-to-all(f32[128,1,1152]{2,1,0:T(1,128)S(1)} %bitcast.5), channel_id=1, replica_groups=mesh['y'=4,'core'=2,'x'=4,'z'=4] {'core','y','x','z'}, dimensions={0} | all-to-all | bytes 1179648 | tf_op jit(solution)/shard_map/all_to_all | solution.py:434
  42.8 0.8 %owner_sum.1 = f32[32,128]{1,0:T(8,128)} custom-call(f32[1152,128]{1,0:T(8,128)S(1)} %bitcast.4), custom_call_target="tpu_custom_call" | custom-call | tf_op jit(solution)/shard_map/owner_sum/pallas_call | solution.py:435
Async XLA Ops:
  1.2 10.9 %copy-start = (f32[1,2,2,3,8,64,128]{6,5,4,3,2,1,0:T(8,128)S(1)}, f32[1,2,2,3,8,64,128]{6,5,4,3,2,1,0:T(8,128)}, u32[]{:S(2)}) copy-start(f32[1,2,2,3,8,64,128]{6,5,4,3,2,1,0:T(8,128)} %e_ref.1) | copy-start | bytes 9437188
  1.2 10.9 %copy-start.1 = (f32[1,2,2,3,8,64,128]{6,5,4,3,2,1,0:T(8,128)S(1)}, f32[1,2,2,3,8,64,128]{6,5,4,3,2,1,0:T(8,128)}, u32[]{:S(2)}) copy-start(f32[1,2,2,3,8,64,128]{6,5,4,3,2,1,0:T(8,128)} %s_ref) | copy-start | bytes 9437188
  1.2 10.9 %copy-start.2 = (f32[1,8,64,128]{3,2,1,0:T(8,128)S(1)}, f32[1,8,64,128]{3,2,1,0:T(8,128)}, u32[]{:S(2)}) copy-start(f32[1,8,64,128]{3,2,1,0:T(8,128)} %c_ref.1) | copy-start | bytes 786436
  1.3 10.9 %copy-start.3 = (f32[2]{0:T(128)S(1)}, f32[2]{0:T(128)}, u32[]{:S(2)}) copy-start(f32[2]{0:T(128)} %om_ref.3) | copy-start | bytes 28
  1.3 14.0 %collective-permute-start = (f32[8,64,128]{2,1,0:T(8,128)S(1)}, f32[8,64,128]{2,1,0:T(8,128)S(1)}, u32[]{:S(2)}, u32[]{:S(2)}) collective-permute-start(f32[8,64,128]{2,1,0:T(8,128)S(1)} %get-tuple-element.23), channel_id=1, source_target_pairs={{1,2},{3,4},{5,6},{7,8},{9,10},{11,12},{13,14},{15,0},{2,1},{4,3},... | collective-permute-start | bytes 786440 | tf_op jit(solution)/shard_map/ppermute | solution.py:386
  7.7 9.2 %collective-permute-start.1 = (f32[8,64,128]{2,1,0:T(8,128)S(1)}, f32[8,64,128]{2,1,0:T(8,128)S(1)}, u32[]{:S(2)}, u32[]{:S(2)}) collective-permute-start(f32[8,64,128]{2,1,0:T(8,128)S(1)} %get-tuple-element.24), channel_id=1, source_target_pairs={{0,1},{2,3},{4,5},{6,7},{8,9},{10,11},{12,13},{14,15},{1,0},{3,2},... | collective-permute-start | bytes 786440 | tf_op jit(solution)/shard_map/ppermute | solution.py:387
  9.9 11.2 %collective-permute-start.2 = (f32[8,64,128]{2,1,0:T(8,128)S(1)}, f32[8,64,128]{2,1,0:T(8,128)S(1)}, u32[]{:S(2)}, u32[]{:S(2)}) collective-permute-start(f32[8,64,128]{2,1,0:T(8,128)S(1)} %get-tuple-element.28), channel_id=1, source_target_pairs={{1,2},{3,4},{5,6},{7,8},{9,10},{11,12},{13,14},{15,0},{2,1},{4,3},... | collective-permute-start | bytes 786440 | tf_op jit(solution)/shard_map/ppermute | solution.py:410
  10.8 6.1 %copy-start.4 = (s32[8]{0:T(128)S(1)}, s32[8]{0:T(128)}, u32[]{:S(2)}) copy-start(s32[8]{0:T(128)} %tb_ref.1) | copy-start | bytes 100
  10.8 10.3 %collective-permute-start.3 = (f32[8,64,128]{2,1,0:T(8,128)S(1)}, f32[8,64,128]{2,1,0:T(8,128)S(1)}, u32[]{:S(2)}, u32[]{:S(2)}) collective-permute-start(f32[8,64,128]{2,1,0:T(8,128)S(1)} %get-tuple-element.18), channel_id=1, source_target_pairs={{0,1},{2,3},{4,5},{6,7},{8,9},{10,11},{12,13},{14,15},{1,0},{3,2},... | collective-permute-start | bytes 786440 | tf_op jit(solution)/shard_map/ppermute | solution.py:411

commit v8 on v7

--- a/solution.py
+++ b/solution.py
@@ -321,7 +321,7 @@
     part_ref[pl.ds(CAP, DEV, stride=SLOTS), :] = index_ref[...]
 
 
-def residual_fix_kernel(fac_ref, rest_ref, gone_ref, gtwo_ref, hot_ref, part_ref, out_ref, two_ref):
+def residual_fix_kernel(fac_ref, rest_ref, gone_ref, gtwo_ref, hot_ref, part_ref, out_ref):
     odd = odd_brick()
     low, high = rest_ref[0], rest_ref[1]
     for ch in range(4):
@@ -332,9 +332,7 @@
         low = low + (fac_ref[2 * ch] * qy + fac_ref[2 * ch + 1] * qz)
         o = [fac_ref[8 + 3 * ch + c] for c in range(3)]
         high = high + (o[0] * (by(ry) + bz(rz)) - o[1] * ry - o[2] * rz)
-    two_ref[0:NY] = low
-    two_ref[NY:2 * NY] = high
-    out_ref[...] = part_ref[...] + pick(hot_ref[...], two_ref[...])
+    out_ref[...] = part_ref[...] + pick(hot_ref[...], jnp.concatenate([low, high], axis=0))
 
 
 def owner_kernel(got_ref, out_ref):
@@ -429,7 +427,7 @@
         name="adjoint",
     )(omegas_in, tx_bricks, fields_v, conductivity_v, slot, index, gone_e, gtwo_e, r)
     (send,) = call(
-        residual_fix_kernel, "residual_fix", [VMEM] * 6, [packed], [pltpu.VMEM((2 * NY, NZ), F32)], 20_000_000, 3_000_000,
+        residual_fix_kernel, "residual_fix", [VMEM] * 6, [packed], [], 20_000_000, 3_000_000,
     )(fac, rest, gone_r, gtwo_r, hot, part)
     got = lax.all_to_all(send.reshape(DEV, 1, SLOTS * NZ), SWAP_AXES, 0, 0, tiled=True).reshape(DEV * SLOTS, NZ)
     return pl.pallas_call(

time: 44.4 us -> 44.4 us (level)
  no operation moved by 1% of the time
where the time goes in v8:
time: 44.4 us; the launch traced here: 43.7 us
  blocking collectives  21.3 us (48%)
  Pallas kernels  11.9 us (27%)
  starting transfers between devices  8.6 us (19%)
  waiting for transfers between devices  1.7 us (4%)
    all_to_all x1, blocking collectives, per_device(): lax.all_to_all(send.reshape(DEV, 1, SLOTS * NZ), SWAP_AXES, 0, 0, tiled=T...  21.3 us
    ppermute x1, starting transfers between devices, per_device(): gone_e = lax.ppermute(one_e, BRICK_AXES, with_next)  6.39 us
    pallas_call x1, Pallas kernels, per_device(): pl.pallas_call(adjoint_kernel, in_specs=[SMEM, SMEM] + [VMEM] * 7, out_sp...  4.03 us
    pallas_call x1, Pallas kernels, per_device(): call(residual_kernel, 'residual', [SMEM] + [VMEM] * 3, [f32(12, PL + 1, N...  3.19 us
    pallas_call x1, Pallas kernels, per_device(): call(residual_halo_kernel, 'residual_halo', [HBM] * 7, [pay, pay, jax.Sha...  2.21 us
    ppermute x1, waiting for transfers between devices, per_device(): gtwo_e = lax.ppermute(two_e, BRICK_AXES, with_last)  1.58 us
    ppermute x1, starting transfers between devices, per_device(): gtwo_r = lax.ppermute(two_r, BRICK_AXES, with_last)  1.31 us
    pallas_call x1, Pallas kernels, per_device(): call(field_halo_kernel, 'field_halo', [HBM], [pay, pay], [pltpu.VMEM((NF,...  1.21 us
  transfers between devices with their start and end apart: 4, of which 2 were waited for; matrix products, arithmetic and copies ran while one was open for 0% of the time, Pallas kernels for 22%

profile of v8, /device:TPU:0, one launch (start us, length us, event | category | flops | bytes accessed | tf_op | source)
XLA Modules:
  0.0 43.7 jit_solution(9968609975822796610)
XLA Ops:
  0.0 1.2 %field_halo.1 = (f32[8,64,128]{2,1,0:T(8,128)S(1)}, f32[8,64,128]{2,1,0:T(8,128)S(1)}) custom-call(f32[1,2,2,3,8,64,128]{6,5,4,3,2,1,0:T(8,128)} %e_ref.1), custom_call_target="tpu_custom_call" | custom-call | flops 400000 | bytes 1200000 | tf_op jit(solution)/shard_map/field_halo/pallas_call | solution.py:380
  1.2 0.0 copy-start
  1.2 0.0 copy-start.1
  1.2 0.0 copy-start.2
  1.3 0.0 copy-start.3
  1.3 6.4 %collective-permute-start = (f32[8,64,128]{2,1,0:T(8,128)S(1)}, f32[8,64,128]{2,1,0:T(8,128)S(1)}, u32[]{:S(2)}, u32[]{:S(2)}) collective-permute-start(f32[8,64,128]{2,1,0:T(8,128)S(1)} %get-tuple-element.23), channel_id=1, source_target_pairs={{1,2},{3,4},{5,6},{7,8},{9,10},{11,12},{13,14},{15,0},{2,1},{4,3},... | collective-permute-start | bytes 786440 | tf_op jit(solution)/shard_map/ppermute | solution.py:384
  7.7 0.0 collective-permute-start.1
  7.7 2.2 %residual_halo.1 = (f32[8,64,128]{2,1,0:T(8,128)S(1)}, f32[8,64,128]{2,1,0:T(8,128)S(1)}, s32[8,512]{1,0:T(8,128)S(1)}, f32[128,128]{1,0:T(8,128)S(1)}) custom-call(f32[2]{0:T(128)} %om_ref.3, f32[1,2,2,3,8,64,128]{6,5,4,3,2,1,0:T(8,128)} %e_ref.1, f32[1,2,2,3,8,64,128]{6,5,4,3,2,1,0:T(8,128)} %s_ref, f32[1,8,64,128]{3,2,1,0:T(8,128)} %c_ref.1, ...), custom_call_target="tpu_custom_call" | custom-call | flops 2000000 | bytes 3000000 | tf_op jit(solution)/shard_map/residual_halo/pallas_call | solution.py:386
  9.9 0.9 %collective-permute-start.2 = (f32[8,64,128]{2,1,0:T(8,128)S(1)}, f32[8,64,128]{2,1,0:T(8,128)S(1)}, u32[]{:S(2)}, u32[]{:S(2)}) collective-permute-start(f32[8,64,128]{2,1,0:T(8,128)S(1)} %get-tuple-element.28), channel_id=1, source_target_pairs={{1,2},{3,4},{5,6},{7,8},{9,10},{11,12},{13,14},{15,0},{2,1},{4,3},... | collective-permute-start | bytes 786440 | tf_op jit(solution)/shard_map/ppermute | solution.py:408
  10.8 0.0 copy-start.4
  10.8 1.3 %collective-permute-start.3 = (f32[8,64,128]{2,1,0:T(8,128)S(1)}, f32[8,64,128]{2,1,0:T(8,128)S(1)}, u32[]{:S(2)}, u32[]{:S(2)}) collective-permute-start(f32[8,64,128]{2,1,0:T(8,128)S(1)} %get-tuple-element.18), channel_id=1, source_target_pairs={{0,1},{2,3},{4,5},{6,7},{8,9},{10,11},{12,13},{14,15},{1,0},{3,2},... | collective-permute-start | bytes 786440 | tf_op jit(solution)/shard_map/ppermute | solution.py:409
  12.1 0.0 copy-done
  12.1 0.0 copy-done.1
  12.1 0.0 copy-done.2
  12.1 0.0 copy-done.3
  12.1 3.2 %residual.1.rin_ref = f32[12,9,72,128]{3,2,1,0:T(8,128)S(1)} custom-call(f32[2]{0:T(128)S(1)} %copy-done.3, f32[1,2,2,3,8,64,128]{6,5,4,3,2,1,0:T(8,128)S(1)} %copy-done, f32[1,2,2,3,8,64,128]{6,5,4,3,2,1,0:T(8,128)S(1)} %copy-done.1, f32[1,8,64,128]{3,2,1,0:T(8,128)S(1)} %copy-done.2), custom_call_target="tpu_custom_call" | custom-call | flops 30000000 | bytes 8000000 | tf_op jit(solution)/shard_map/residual/pallas_call | solution.py:415
  15.3 0.0 collective-permute-done.gone_ref
  15.3 1.6 %collective-permute-done.1.gtwo_ref = f32[8,64,128]{2,1,0:T(8,128)S(1)} collective-permute-done((f32[8,64,128]{2,1,0:T(8,128)S(1)}, f32[8,64,128]{2,1,0:T(8,128)S(1)}, u32[]{:S(2)}, u32[]{:S(2)}) %collective-permute-start.1) | collective-permute-done | bytes 262176 | tf_op jit(solution)/shard_map/ppermute | solution.py:385
  16.9 0.0 copy-done.4
  16.9 4.0 %adjoint.1 = (f32[1152,128]{1,0:T(8,128)S(1)}, f32[2,64,128]{2,1,0:T(8,128)S(1)}, f32[20,64,128]{2,1,0:T(8,128)S(1)}, bf16[1152,128]{1,0:T(8,128)(2,1)S(1)}, f32[12,9,72,128]{3,2,1,0:T(8,128)S(1)}) custom-call(f32[2]{0:T(128)S(1)} %copy-done.3, s32[8]{0:T(128)S(1)} %copy-done.4, ...), custom_call_target="tpu_custom_call", output_to_operand_aliasing={{4}: (8, {})} | custom-call | flops 40000000 | bytes 8000000 | tf_op jit(solution)/shard_map/adjoint/pallas_call | solution.py:418
  20.9 0.1 collective-permute-done.2.gone_ref
  21.1 0.0 collective-permute-done.3.gtwo_ref
  21.1 0.4 residual_fix.1
  21.5 21.3 %all_to_all.5 = f32[128,1,1152]{2,1,0:T(1,128)S(1)} all-to-all(f32[128,1,1152]{2,1,0:T(1,128)S(1)} %bitcast.5), channel_id=1, replica_groups=mesh['y'=4,'core'=2,'x'=4,'z'=4] {'core','y','x','z'}, dimensions={0} | all-to-all | bytes 1179648 | tf_op jit(solution)/shard_map/all_to_all | solution.py:432
  42.8 0.8 %owner_sum.1 = f32[32,128]{1,0:T(8,128)} custom-call(f32[1152,128]{1,0:T(8,128)S(1)} %bitcast.4), custom_call_target="tpu_custom_call" | custom-call | tf_op jit(solution)/shard_map/owner_sum/pallas_call | solution.py:433
Async XLA Ops:
  1.2 10.9 %copy-start = (f32[1,2,2,3,8,64,128]{6,5,4,3,2,1,0:T(8,128)S(1)}, f32[1,2,2,3,8,64,128]{6,5,4,3,2,1,0:T(8,128)}, u32[]{:S(2)}) copy-start(f32[1,2,2,3,8,64,128]{6,5,4,3,2,1,0:T(8,128)} %e_ref.1) | copy-start | bytes 9437188
  1.2 10.9 %copy-start.1 = (f32[1,2,2,3,8,64,128]{6,5,4,3,2,1,0:T(8,128)S(1)}, f32[1,2,2,3,8,64,128]{6,5,4,3,2,1,0:T(8,128)}, u32[]{:S(2)}) copy-start(f32[1,2,2,3,8,64,128]{6,5,4,3,2,1,0:T(8,128)} %s_ref) | copy-start | bytes 9437188
  1.2 10.9 %copy-start.2 = (f32[1,8,64,128]{3,2,1,0:T(8,128)S(1)}, f32[1,8,64,128]{3,2,1,0:T(8,128)}, u32[]{:S(2)}) copy-start(f32[1,8,64,128]{3,2,1,0:T(8,128)} %c_ref.1) | copy-start | bytes 786436
  1.3 10.9 %copy-start.3 = (f32[2]{0:T(128)S(1)}, f32[2]{0:T(128)}, u32[]{:S(2)}) copy-start(f32[2]{0:T(128)} %om_ref.3) | copy-start | bytes 28
  1.3 14.0 %collective-permute-start = (f32[8,64,128]{2,1,0:T(8,128)S(1)}, f32[8,64,128]{2,1,0:T(8,128)S(1)}, u32[]{:S(2)}, u32[]{:S(2)}) collective-permute-start(f32[8,64,128]{2,1,0:T(8,128)S(1)} %get-tuple-element.23), channel_id=1, source_target_pairs={{1,2},{3,4},{5,6},{7,8},{9,10},{11,12},{13,14},{15,0},{2,1},{4,3},... | collective-permute-start | bytes 786440 | tf_op jit(solution)/shard_map/ppermute | solution.py:384
  7.7 9.2 %collective-permute-start.1 = (f32[8,64,128]{2,1,0:T(8,128)S(1)}, f32[8,64,128]{2,1,0:T(8,128)S(1)}, u32[]{:S(2)}, u32[]{:S(2)}) collective-permute-start(f32[8,64,128]{2,1,0:T(8,128)S(1)} %get-tuple-element.24), channel_id=1, source_target_pairs={{0,1},{2,3},{4,5},{6,7},{8,9},{10,11},{12,13},{14,15},{1,0},{3,2},... | collective-permute-start | bytes 786440 | tf_op jit(solution)/shard_map/ppermute | solution.py:385
  9.9 11.2 %collective-permute-start.2 = (f32[8,64,128]{2,1,0:T(8,128)S(1)}, f32[8,64,128]{2,1,0:T(8,128)S(1)}, u32[]{:S(2)}, u32[]{:S(2)}) collective-permute-start(f32[8,64,128]{2,1,0:T(8,128)S(1)} %get-tuple-element.28), channel_id=1, source_target_pairs={{1,2},{3,4},{5,6},{7,8},{9,10},{11,12},{13,14},{15,0},{2,1},{4,3},... | collective-permute-start | bytes 786440 | tf_op jit(solution)/shard_map/ppermute | solution.py:408
  10.8 6.1 %copy-start.4 = (s32[8]{0:T(128)S(1)}, s32[8]{0:T(128)}, u32[]{:S(2)}) copy-start(s32[8]{0:T(128)} %tb_ref.1) | copy-start | bytes 100
  10.8 10.3 %collective-permute-start.3 = (f32[8,64,128]{2,1,0:T(8,128)S(1)}, f32[8,64,128]{2,1,0:T(8,128)S(1)}, u32[]{:S(2)}, u32[]{:S(2)}) collective-permute-start(f32[8,64,128]{2,1,0:T(8,128)S(1)} %get-tuple-element.18), channel_id=1, source_target_pairs={{0,1},{2,3},{4,5},{6,7},{8,9},{10,11},{12,13},{14,15},{1,0},{3,2},... | collective-permute-start | bytes 786440 | tf_op jit(solution)/shard_map/ppermute | solution.py:409
